TPU v7x, 32 devices: a whole 2x2x4 slice. The times are simulated.
32 devices in a mesh: group: 2 (over x), tm: 16 (over z, y, core).
Axes of the slice: x: 2, y: 2, z: 4, core: 2. Of those that a mesh axis runs over, the one named last changes fastest.
Arguments:
- hidden: bfloat16 [7680, 3072], P(('group', 'tm')), parts along dimension 0, may hold values from -6 to 6
- queries: bfloat16 [7680, 1536], P(('group', 'tm')), parts along dimension 0, may hold values from -6 to 6
- values: bfloat16 [7680, 1536], P(('group', 'tm')), parts along dimension 0, may hold values from -12 to 12
- key_weight: bfloat16 [3072, 1536], P('tm'), may hold values from -0.109375 to 0.109375
- query_gain: float32 [128], replicated, may hold values from 1 to 3
- key_gain: float32 [128], replicated, may hold values from 0.25 to 1.75
- rope_positions: int32 [3, 7680], P(None, ('group', 'tm')), parts along dimension 1, may hold values from 0 to 79, as said below
- block_mask: int32 [31, 2], replicated, may hold values from 0 to 1, as said below
Outputs:
- attended: bfloat16 [7680, 1536], P(('group', 'tm')), parts along dimension 0
There are 2 independent parts, one for each index of `group`. A program takes and returns all parts, laid end to end along the dimension named above; an argument that names none is the same for every part. Nothing has to cross between parts.
Inputs may be any that keep to these rules, and one draw needn't show every extreme that they name: `block_mask`: row 15 + d belongs to key frames at distance d (key frame minus query frame). The row with d = 0 is all ones. For d = 2^k or -2^k with 2^k < 16, the ones stand at blocks j0, j0 + m, j0 + 2 m and so on, with m = min(2^k, 2) and j0 < m, exactly ceil(2 / m) of them. Every other row is zero. `rope_positions`: row 0 is the latent frame index plus 63; rows 1 and 2 are a token's latent row and column: a frame's tokens are the row-major cells of a crop 20 columns wide whose corner, row 0 to 21 and column 0 to 60, moves from frame to frame.
All inputs are finite; a program needn't handle non-finite values.
Results may differ from a plain program's by a relative error of at most 0.0098.
Values may be sent and summed in bfloat16 or wider, within the bound.
No kernel may reach another device: no remote copies, remote signals or barrier semaphores. Data moves between devices by JAX's collectives and lax.ppermute only.
A program may use at most 128 MiB of HBM per device.

v0:
```python
import jax
import jax.numpy as jnp
from jax import lax
from jax.sharding import PartitionSpec as P

BLOCK = 128


ROPE_BASE = 256.0
NORM_EPS = 1e-06


def shifted(block, axis, distance):
    devices = range(lax.axis_size(axis))
    route = [(i - distance, i) for i in devices if i - distance in devices]
    return lax.ppermute(block, axis, route)


def head_norm(tensor, gain_vec):
    mean_sq = jnp.mean(tensor * tensor, axis=-1, keepdims=True)
    return tensor * lax.rsqrt(mean_sq + NORM_EPS) * gain_vec


def rotate(tensor, positions):
    head_dim = tensor.shape[-1]
    time_len = head_dim // 8
    space_len = (head_dim - time_len) // 2
    layout = ((0, time_len), (time_len, space_len), (time_len + space_len, space_len))
    pieces = []
    for axis_id in range(3):
        seg_start, length = layout[axis_id]
        half_len = length // 2
        exponent = jnp.arange(half_len, dtype=jnp.float32) * (-2.0 / length)
        frequency = jnp.power(jnp.float32(ROPE_BASE), exponent)
        angles = positions[axis_id].astype(jnp.float32)[:, None] * frequency[None, :]
        cosine = jnp.cos(angles)[:, None, :]
        sine_part = jnp.sin(angles)[:, None, :]
        first_half = tensor[..., seg_start : seg_start + half_len]
        second = tensor[..., seg_start + half_len : seg_start + length]
        pieces.append(first_half * cosine - second * sine_part)
        pieces.append(second * cosine + first_half * sine_part)
    return jnp.concatenate(pieces, axis=-1)


def body(hidden, queries, values, key_weight, query_gain, key_gain, rope_positions, block_mask):
    tok_rows = hidden.shape[0]
    proj_width = key_weight.shape[1]
    head_dim = query_gain.shape[0]
    head_count = proj_width // head_dim
    frames = lax.axis_size("tm")
    my_frame = lax.axis_index("tm")
    block_count = -(-tok_rows // BLOCK)
    padded = block_count * BLOCK
    levels = (frames - 1).bit_length()
    softmax_scale = head_dim ** (-0.5)
    key_raw = jnp.dot(
        hidden,
        lax.all_gather(key_weight, "tm", axis=0, tiled=True),
        preferred_element_type=jnp.float32,
    )
    key_rot = rotate(
        head_norm(key_raw.reshape(tok_rows, head_count, head_dim), key_gain), rope_positions
    ).astype(jnp.bfloat16)
    query_heads = queries.astype(jnp.float32).reshape(tok_rows, head_count, head_dim)
    query_rot = rotate(head_norm(query_heads, query_gain), rope_positions).astype(jnp.bfloat16)
    key_pad = jnp.pad(key_rot.reshape(tok_rows, proj_width), ((0, padded - tok_rows), (0, 0)))
    value_pad = jnp.pad(values, ((0, padded - tok_rows), (0, 0)))
    token_ok = jnp.arange(padded, dtype=jnp.int32) < tok_rows

    def frame_usable(offset):
        return jnp.repeat(block_mask[frames - 1 + offset] == 1, BLOCK)

    totals = (
        jnp.zeros((tok_rows, head_count, head_dim), jnp.float32),
        jnp.zeros((head_count, tok_rows), jnp.float32),
    )
    pending = [(key_pad, value_pad, (token_ok & frame_usable(0)).astype(jnp.float32))]
    pending_rows = padded
    for level_idx in range(levels):
        distance = 1 << level_idx
        lower_ok = my_frame - distance >= 0
        upper_ok = my_frame + distance < frames
        lower_keys, lower_vals = shifted((key_pad, value_pad), "tm", distance)
        upper_keys, upper_vals = shifted((key_pad, value_pad), "tm", -distance)
        lower_usable = token_ok & frame_usable(-distance) & lower_ok
        upper_usable = token_ok & frame_usable(distance) & upper_ok
        pending.append((lower_keys, lower_vals, lower_usable.astype(jnp.float32)))
        pending.append((upper_keys, upper_vals, upper_usable.astype(jnp.float32)))
        pending_rows = pending_rows + lower_keys.shape[0] + upper_keys.shape[0]
        keys_in = jnp.concatenate([entry[0] for entry in pending], axis=0)
        vals_in = jnp.concatenate([entry[1] for entry in pending], axis=0)
        attend_numerator, attend_denominator = totals
        key_heads = keys_in.reshape(keys_in.shape[0], head_count, head_dim)
        value_heads = vals_in.reshape(vals_in.shape[0], head_count, head_dim)
        scores = jnp.einsum(
            "qhd,khd->hqk", query_rot, key_heads, preferred_element_type=jnp.float32
        )
        weights = (
            jnp.exp(scores * softmax_scale)
            * jnp.concatenate([entry[2] for entry in pending], axis=0)[None, None, :]
        )
        attend_denominator = attend_denominator + jnp.sum(weights, axis=2)
        probabilities = weights.astype(jnp.bfloat16)
        attend_numerator = attend_numerator + jnp.einsum(
            "hqk,khd->qhd", probabilities, value_heads, preferred_element_type=jnp.float32
        )
        totals = (attend_numerator, attend_denominator)
        pending = []
        pending_rows = 0
    numerator, denominator = totals
    attended = numerator / jnp.transpose(denominator)[:, :, None]
    return attended.reshape(tok_rows, proj_width).astype(jnp.bfloat16)


def solution(mesh):
    in_specs = (
        P(("group", "tm"), None),
        P(("group", "tm"), None),
        P(("group", "tm"), None),
        P("tm", None),
        P(),
        P(),
        P(None, ("group", "tm")),
        P(),
    )
    out_specs = P(("group", "tm"), None)
    return jax.shard_map(body, mesh=mesh, in_specs=in_specs, out_specs=out_specs, check_vma=False)
```

profile of v0, /device:TPU:0, one launch (start us, length us, event | category | flops | bytes accessed | tf_op | source)
XLA Modules:
  0.0 262.7 jit_solution(18188222985566811068)
XLA Ops:
  11.0 6.5 %collective-permute-start.8 = (bf16[256,1536]{0,1:T(8,128)(2,1)}, bf16[256,1536]{0,1:T(8,128)(2,1)}, u32[]{:S(2)}, u32[]{:S(2)}) collective-permute-start(bf16[256,1536]{0,1:T(8,128)(2,1)} %pad.7), channel_id=1, source_target_pairs={{0,4},{1,5},{2,6},{3,7},{4,8},{5,9},{6,10},{7,11},{8,12},{9,13},{1... | collective-permute-start | bytes 2359304 | tf_op jit(solution)/shard_map/ppermute | solution.py:16
  20.0 6.0 %collective-permute-start.4 = (bf16[256,1536]{0,1:T(8,128)(2,1)}, bf16[256,1536]{0,1:T(8,128)(2,1)}, u32[]{:S(2)}, u32[]{:S(2)}) collective-permute-start(bf16[256,1536]{0,1:T(8,128)(2,1)} %pad.7), channel_id=1, source_target_pairs={{0,2},{1,3},{2,4},{3,5},{4,6},{5,7},{6,8},{7,9},{8,10},{9,11},{10,... | collective-permute-start | bytes 2359304 | tf_op jit(solution)/shard_map/ppermute | solution.py:16
  36.8 13.1 %collective-permute-done.9 = bf16[256,1536]{0,1:T(8,128)(2,1)} collective-permute-done((bf16[256,1536]{0,1:T(8,128)(2,1)}, bf16[256,1536]{0,1:T(8,128)(2,1)}, u32[]{:S(2)}, u32[]{:S(2)}) %collective-permute-start.9) | collective-permute-done | bytes 786464 | tf_op jit(solution)/shard_map/ppermute | solution.py:16
  49.9 2.2 collective-permute-start
  53.4 2.6 %pad_maximum_fusion.4 = bf16[512,1536]{0,1:T(8,128)(2,1)} fusion(bf16[256,1536]{0,1:T(8,128)(2,1)} %collective-permute-done.9, bf16[256,1536]{0,1:T(8,128)(2,1)} %collective-permute-done.8), kind=kLoop, calls=%fused_computation.28 | loop fusion | flops 3145728 | bytes 3145728 | tf_op jit(solution)/shard_map/concatenate | solution.py:91
  56.0 86.3 %collective-permute-start.12 = (bf16[256,1536]{0,1:T(8,128)(2,1)}, bf16[256,1536]{0,1:T(8,128)(2,1)}, u32[]{:S(2)}, u32[]{:S(2)}) collective-permute-start(bf16[256,1536]{0,1:T(8,128)(2,1)} %pad.7), channel_id=1, source_target_pairs={{0,8},{1,9},{2,10},{3,11},{4,12},{5,13},{6,14},{7,15},{16,24},{17,... | collective-permute-start | bytes 2359304 | tf_op jit(solution)/shard_map/ppermute | solution.py:16
  143.8 8.6 %fusion.39 = f32[240,1536]{0,1:T(8,128)} fusion(bf16[240,3072]{1,0:T(8,128)(2,1)S(1)} %copy-done, bf16[3072,1536]{1,0:T(8,128)(2,1)} %all-gather.2.cloned.1.call-done), kind=kOutput, calls=%fused_computation.99 | convolution fusion | flops 2264924160 | bytes 12386304 | tf_op jit(solution)/shard_map/dot_general | solution.py:56
  152.4 3.0 %copy.32 = f32[240,12,128]{2,0,1:T(8,128)} copy(f32[240,12,128]{0,2,1:T(8,128)} %bitcast.78) | data formatting | bytes 2949120 | tf_op jit(solution)/shard_map/reshape | solution.py:62
  157.3 2.1 multiply_multiply_fusion
  159.4 3.2 %add_convert_fusion = (bf16[240,12,28]{2,0,1:T(8,128)(2,1)}, bf16[240,12,28]{2,0,1:T(8,128)(2,1)}, bf16[240,12,28]{2,0,1:T(8,128)(2,1)}, bf16[240,12,28]{2,0,1:T(8,128)(2,1)}) fusion(f32[240,12,128]{2,0,1:T(8,128)S(1)} %get-tuple-element.59, f32[240,28]{1,0:T(8,128)S(1)} %get-tuple-element.36, f32[240,28]{1,0:T(8,128)S(1)} %get-tuple-element.35, ...), kind=kLoop, calls=%fused_computation.36 | loop fusion | flops 1290240 | bytes 2042880 | tf_op jit(solution)/shard_map/convert.10
  162.6 2.7 %add_convert_fusion.2 = (bf16[240,12,8]{2,0,1:T(8,128)(2,1)}, bf16[240,12,8]{2,0,1:T(8,128)(2,1)}, bf16[240,12,8]{2,0,1:T(8,128)(2,1)}, bf16[240,12,8]{2,0,1:T(8,128)(2,1)}) fusion(f32[240,12,128]{2,0,1:T(8,128)S(1)} %get-tuple-element.59, f32[240,8]{1,0:T(8,128)S(1)} %copy-done.6, f32[240,8]{1,0:T(8,128)S(1)} %copy-done.7, ...), kind=kLoop, calls=%fused_computation.40 | loop fusion | flops 368640 | bytes 568320 | tf_op jit(solution)/shard_map/convert.6
  165.2 5.4 %concatenate.58 = bf16[240,12,128]{2,0,1:T(8,128)(2,1)} concatenate(bf16[240,12,8]{2,0,1:T(8,128)(2,1)} %get-tuple-element.19, bf16[240,12,8]{2,0,1:T(8,128)(2,1)} %get-tuple-element.18, bf16[240,12,28]{2,0,1:T(8,128)(2,1)} %get-tuple-element.26, bf16[240,12,28]{2,0,1:T(8,128)(2,1)} %get-tuple-element.27, bf16[240,12,28]{2,0,1:T(8,128)(2,1)} %get-tuple-element.15, ...), dimensions={2} | concatenate | bytes 1474560 | tf_op jit(solution)/shard_map/concatenate | solution.py:42
  170.6 2.3 copy.33
  172.9 2.2 pad.8
  176.4 5.5 %collective-permute-start.10 = (bf16[256,1536]{0,1:T(8,128)(2,1)}, bf16[256,1536]{0,1:T(8,128)(2,1)}, u32[]{:S(2)}, u32[]{:S(2)}) collective-permute-start(bf16[256,1536]{0,1:T(8,128)(2,1)} %pad.8), channel_id=1, source_target_pairs={{0,4},{1,5},{2,6},{3,7},{4,8},{5,9},{6,10},{7,11},{8,12},{9,13},{1... | collective-permute-start | bytes 2359304 | tf_op jit(solution)/shard_map/ppermute | solution.py:16
  181.9 2.6 %pad_maximum_fusion.6 = bf16[512,1536]{0,1:T(8,128)(2,1)} fusion(bf16[256,1536]{0,1:T(8,128)(2,1)} %collective-permute-done.13, bf16[256,1536]{0,1:T(8,128)(2,1)} %collective-permute-done.12), kind=kLoop, calls=%fused_computation.30 | loop fusion | flops 3145728 | bytes 3145728 | tf_op jit(solution)/shard_map/concatenate | solution.py:91
  184.5 3.2 %pad_maximum_fusion = bf16[768,1536]{0,1:T(8,128)(2,1)} fusion(bf16[256,1536]{0,1:T(8,128)(2,1)} %collective-permute-done.1, bf16[256,1536]{0,1:T(8,128)(2,1)} %collective-permute-done, bf16[256,1536]{0,1:T(8,128)(2,1)} %pad.7), kind=kLoop, calls=%fused_computation.24 | loop fusion | flops 7077888 | bytes 4718592 | tf_op jit(solution)/shard_map/concatenate | solution.py:91
  189.1 4.0 %collective-permute-start.2 = (bf16[256,1536]{0,1:T(8,128)(2,1)}, bf16[256,1536]{0,1:T(8,128)(2,1)}, u32[]{:S(2)}, u32[]{:S(2)}) collective-permute-start(bf16[256,1536]{0,1:T(8,128)(2,1)} %pad.8), channel_id=1, source_target_pairs={{0,1},{1,2},{2,3},{3,4},{4,5},{5,6},{6,7},{7,8},{8,9},{9,10},{10,1... | collective-permute-start | bytes 2359304 | tf_op jit(solution)/shard_map/ppermute | solution.py:16
  194.4 3.2 %add_convert_fusion.3 = (bf16[240,12,28]{2,0,1:T(8,128)(2,1)}, bf16[240,12,28]{2,0,1:T(8,128)(2,1)}, bf16[240,12,28]{2,0,1:T(8,128)(2,1)}, bf16[240,12,28]{2,0,1:T(8,128)(2,1)}) fusion(f32[240,12,128]{2,0,1:T(8,128)S(1)} %get-tuple-element.60, f32[240,28]{1,0:T(8,128)S(1)} %get-tuple-element.36, f32[240,28]{1,0:T(8,128)S(1)} %get-tuple-element.35, ...), kind=kLoop, calls=%fused_computation.43 | loop fusion | flops 1290240 | bytes 2042880 | tf_op jit(solution)/shard_map/convert.16
  197.5 4.7 %concatenate.57 = bf16[240,12,128]{2,0,1:T(8,128)(2,1)S(1)} concatenate(bf16[240,12,8]{2,0,1:T(8,128)(2,1)} %get-tuple-element.30, bf16[240,12,8]{2,0,1:T(8,128)(2,1)} %get-tuple-element.31, bf16[240,12,28]{2,0,1:T(8,128)(2,1)} %get-tuple-element.28, bf16[240,12,28]{2,0,1:T(8,128)(2,1)} %get-tuple-element.29, bf16[240,12,28]{2,0,1:T(8,128)(2,1)} %get-tuple-element.21, ...), dimensions={2} | concatenate | bytes 1474560 | tf_op jit(solution)/shard_map/concatenate | solution.py:42
  202.3 4.6 %collective-permute-start.6 = (bf16[256,1536]{0,1:T(8,128)(2,1)}, bf16[256,1536]{0,1:T(8,128)(2,1)S(1)}, u32[]{:S(2)}, u32[]{:S(2)}) collective-permute-start(bf16[256,1536]{0,1:T(8,128)(2,1)} %pad.8), channel_id=1, source_target_pairs={{0,2},{1,3},{2,4},{3,5},{4,6},{5,7},{6,8},{7,9},{8,10},{9,11},{10,... | collective-permute-start | bytes 2359304 | tf_op jit(solution)/shard_map/ppermute | solution.py:16
  212.2 5.5 %collective-permute-start.14 = (bf16[256,1536]{0,1:T(8,128)(2,1)}, bf16[256,1536]{0,1:T(8,128)(2,1)S(1)}, u32[]{:S(2)}, u32[]{:S(2)}) collective-permute-start(bf16[256,1536]{0,1:T(8,128)(2,1)} %pad.8), channel_id=1, source_target_pairs={{0,8},{1,9},{2,10},{3,11},{4,12},{5,13},{6,14},{7,15},{16,24},{17,... | collective-permute-start | bytes 2359304 | tf_op jit(solution)/shard_map/ppermute | solution.py:16
  221.5 16.4 %collective-permute-done.6 = bf16[256,1536]{0,1:T(8,128)(2,1)S(1)} collective-permute-done((bf16[256,1536]{0,1:T(8,128)(2,1)}, bf16[256,1536]{0,1:T(8,128)(2,1)S(1)}, u32[]{:S(2)}, u32[]{:S(2)}) %collective-permute-start.6) | collective-permute-done | bytes 786464 | tf_op jit(solution)/shard_map/ppermute | solution.py:16
  243.6 7.7 %collective-permute-done.15 = bf16[256,1536]{0,1:T(8,128)(2,1)S(1)} collective-permute-done((bf16[256,1536]{0,1:T(8,128)(2,1)}, bf16[256,1536]{0,1:T(8,128)(2,1)S(1)}, u32[]{:S(2)}, u32[]{:S(2)}) %collective-permute-start.15) | collective-permute-done | bytes 786464 | tf_op jit(solution)/shard_map/ppermute | solution.py:16
  (97 shorter events, 45.4 us)
Async XLA Ops:
  6.5 137.3 %copy-start = (bf16[240,3072]{1,0:T(8,128)(2,1)S(1)}, bf16[240,3072]{1,0:T(8,128)(2,1)}, u32[]{:S(2)}) copy-start(bf16[240,3072]{1,0:T(8,128)(2,1)} %param.8) | copy-start | bytes 4423684
  6.5 137.3 %all-gather.2.cloned.1.call-start = ((), (), s32[]{:S(2)}) async-start(), calls=%async_computation | async-start | bytes 10027008 | tf_op jit(solution)/shard_map/all_gather | solution.py:58
  8.6 18.9 %copy-start.8 = (s32[31,2]{0,1:T(2,128)S(1)}, s32[31,2]{0,1:T(2,128)}, u32[]{:S(2)}) copy-start(s32[31,2]{0,1:T(2,128)} %param.15) | copy-start | bytes 748
  9.7 40.3 %collective-permute-start.9 = (bf16[256,1536]{0,1:T(8,128)(2,1)}, bf16[256,1536]{0,1:T(8,128)(2,1)}, u32[]{:S(2)}, u32[]{:S(2)}) collective-permute-start(bf16[256,1536]{0,1:T(8,128)(2,1)} %pad.7), channel_id=1, source_target_pairs={{4,0},{5,1},{6,2},{7,3},{8,4},{9,5},{10,6},{11,7},{12,8},{13,9},{1... | collective-permute-start | bytes 2359304 | tf_op jit(solution)/shard_map/ppermute | solution.py:16
  11.0 41.1 %collective-permute-start.8 = (bf16[256,1536]{0,1:T(8,128)(2,1)}, bf16[256,1536]{0,1:T(8,128)(2,1)}, u32[]{:S(2)}, u32[]{:S(2)}) collective-permute-start(bf16[256,1536]{0,1:T(8,128)(2,1)} %pad.7), channel_id=1, source_target_pairs={{0,4},{1,5},{2,6},{3,7},{4,8},{5,9},{6,10},{7,11},{8,12},{9,13},{1... | collective-permute-start | bytes 2359304 | tf_op jit(solution)/shard_map/ppermute | solution.py:16
  17.5 167.1 %collective-permute-start.1 = (bf16[256,1536]{0,1:T(8,128)(2,1)}, bf16[256,1536]{0,1:T(8,128)(2,1)}, u32[]{:S(2)}, u32[]{:S(2)}) collective-permute-start(bf16[256,1536]{0,1:T(8,128)(2,1)} %pad.7), channel_id=1, source_target_pairs={{1,0},{2,1},{3,2},{4,3},{5,4},{6,5},{7,6},{8,7},{9,8},{10,9},{11,1... | collective-permute-start | bytes 2359304 | tf_op jit(solution)/shard_map/ppermute | solution.py:16
  18.7 37.3 %collective-permute-start.5 = (bf16[256,1536]{0,1:T(8,128)(2,1)}, bf16[256,1536]{0,1:T(8,128)(2,1)}, u32[]{:S(2)}, u32[]{:S(2)}) collective-permute-start(bf16[256,1536]{0,1:T(8,128)(2,1)} %pad.7), channel_id=1, source_target_pairs={{2,0},{3,1},{4,2},{5,3},{6,4},{7,5},{8,6},{9,7},{10,8},{11,9},{12,... | collective-permute-start | bytes 2359304 | tf_op jit(solution)/shard_map/ppermute | solution.py:16
  20.0 122.3 %collective-permute-start.4 = (bf16[256,1536]{0,1:T(8,128)(2,1)}, bf16[256,1536]{0,1:T(8,128)(2,1)}, u32[]{:S(2)}, u32[]{:S(2)}) collective-permute-start(bf16[256,1536]{0,1:T(8,128)(2,1)} %pad.7), channel_id=1, source_target_pairs={{0,2},{1,3},{2,4},{3,5},{4,6},{5,7},{6,8},{7,9},{8,10},{9,11},{10,... | collective-permute-start | bytes 2359304 | tf_op jit(solution)/shard_map/ppermute | solution.py:16
  26.1 4.7 %copy-start.13 = (s32[3,240]{1,0:T(4,128)S(1)}, s32[3,240]{1,0:T(4,128)}, u32[]{:S(2)}) copy-start(s32[3,240]{1,0:T(4,128)} %param.14) | copy-start | bytes 8644
  49.9 134.6 %collective-permute-start = (bf16[256,1536]{0,1:T(8,128)(2,1)}, bf16[256,1536]{0,1:T(8,128)(2,1)}, u32[]{:S(2)}, u32[]{:S(2)}) collective-permute-start(bf16[256,1536]{0,1:T(8,128)(2,1)} %pad.7), channel_id=1, source_target_pairs={{0,1},{1,2},{2,3},{3,4},{4,5},{5,6},{6,7},{7,8},{8,9},{9,10},{10,1... | collective-permute-start | bytes 2359304 | tf_op jit(solution)/shard_map/ppermute | solution.py:16
  52.1 124.3 %collective-permute-start.13 = (bf16[256,1536]{0,1:T(8,128)(2,1)}, bf16[256,1536]{0,1:T(8,128)(2,1)}, u32[]{:S(2)}, u32[]{:S(2)}) collective-permute-start(bf16[256,1536]{0,1:T(8,128)(2,1)} %pad.7), channel_id=1, source_target_pairs={{8,0},{9,1},{10,2},{11,3},{12,4},{13,5},{14,6},{15,7},{24,16},{25,... | collective-permute-start | bytes 2359304 | tf_op jit(solution)/shard_map/ppermute | solution.py:16
  56.0 125.8 %collective-permute-start.12 = (bf16[256,1536]{0,1:T(8,128)(2,1)}, bf16[256,1536]{0,1:T(8,128)(2,1)}, u32[]{:S(2)}, u32[]{:S(2)}) collective-permute-start(bf16[256,1536]{0,1:T(8,128)(2,1)} %pad.7), channel_id=1, source_target_pairs={{0,8},{1,9},{2,10},{3,11},{4,12},{5,13},{6,14},{7,15},{16,24},{17,... | collective-permute-start | bytes 2359304 | tf_op jit(solution)/shard_map/ppermute | solution.py:16
  175.1 27.2 %collective-permute-start.11 = (bf16[256,1536]{0,1:T(8,128)(2,1)}, bf16[256,1536]{0,1:T(8,128)(2,1)}, u32[]{:S(2)}, u32[]{:S(2)}) collective-permute-start(bf16[256,1536]{0,1:T(8,128)(2,1)} %pad.8), channel_id=1, source_target_pairs={{4,0},{5,1},{6,2},{7,3},{8,4},{9,5},{10,6},{11,7},{12,8},{13,9},{1... | collective-permute-start | bytes 2359304 | tf_op jit(solution)/shard_map/ppermute | solution.py:16
  176.4 30.5 %collective-permute-start.10 = (bf16[256,1536]{0,1:T(8,128)(2,1)}, bf16[256,1536]{0,1:T(8,128)(2,1)}, u32[]{:S(2)}, u32[]{:S(2)}) collective-permute-start(bf16[256,1536]{0,1:T(8,128)(2,1)} %pad.8), channel_id=1, source_target_pairs={{0,4},{1,5},{2,6},{3,7},{4,8},{5,9},{6,10},{7,11},{8,12},{9,13},{1... | collective-permute-start | bytes 2359304 | tf_op jit(solution)/shard_map/ppermute | solution.py:16
  187.7 24.5 %collective-permute-start.3 = (bf16[256,1536]{0,1:T(8,128)(2,1)}, bf16[256,1536]{0,1:T(8,128)(2,1)}, u32[]{:S(2)}, u32[]{:S(2)}) collective-permute-start(bf16[256,1536]{0,1:T(8,128)(2,1)} %pad.8), channel_id=1, source_target_pairs={{1,0},{2,1},{3,2},{4,3},{5,4},{6,5},{7,6},{8,7},{9,8},{10,9},{11,1... | collective-permute-start | bytes 2359304 | tf_op jit(solution)/shard_map/ppermute | solution.py:16
  189.1 28.6 %collective-permute-start.2 = (bf16[256,1536]{0,1:T(8,128)(2,1)}, bf16[256,1536]{0,1:T(8,128)(2,1)}, u32[]{:S(2)}, u32[]{:S(2)}) collective-permute-start(bf16[256,1536]{0,1:T(8,128)(2,1)} %pad.8), channel_id=1, source_target_pairs={{0,1},{1,2},{2,3},{3,4},{4,5},{5,6},{6,7},{7,8},{8,9},{9,10},{10,1... | collective-permute-start | bytes 2359304 | tf_op jit(solution)/shard_map/ppermute | solution.py:16
  193.1 28.4 %collective-permute-start.7 = (bf16[256,1536]{0,1:T(8,128)(2,1)}, bf16[256,1536]{0,1:T(8,128)(2,1)}, u32[]{:S(2)}, u32[]{:S(2)}) collective-permute-start(bf16[256,1536]{0,1:T(8,128)(2,1)} %pad.8), channel_id=1, source_target_pairs={{2,0},{3,1},{4,2},{5,3},{6,4},{7,5},{8,6},{9,7},{10,8},{11,9},{12,... | collective-permute-start | bytes 2359304 | tf_op jit(solution)/shard_map/ppermute | solution.py:16
  202.3 7.4 %copy-start.11 = (f32[512]{0:T(512)S(1)}, f32[512]{0:T(512)}, u32[]{:S(2)}) copy-start(f32[512]{0:T(512)} %add_convert_fusion.8) | copy-start | bytes 6148
  202.3 35.6 %collective-permute-start.6 = (bf16[256,1536]{0,1:T(8,128)(2,1)}, bf16[256,1536]{0,1:T(8,128)(2,1)S(1)}, u32[]{:S(2)}, u32[]{:S(2)}) collective-permute-start(bf16[256,1536]{0,1:T(8,128)(2,1)} %pad.8), channel_id=1, source_target_pairs={{0,2},{1,3},{2,4},{3,5},{4,6},{5,7},{6,8},{7,9},{8,10},{9,11},{10,... | collective-permute-start | bytes 2359304 | tf_op jit(solution)/shard_map/ppermute | solution.py:16
  206.9 44.4 %collective-permute-start.15 = (bf16[256,1536]{0,1:T(8,128)(2,1)}, bf16[256,1536]{0,1:T(8,128)(2,1)S(1)}, u32[]{:S(2)}, u32[]{:S(2)}) collective-permute-start(bf16[256,1536]{0,1:T(8,128)(2,1)} %pad.8), channel_id=1, source_target_pairs={{8,0},{9,1},{10,2},{11,3},{12,4},{13,5},{14,6},{15,7},{24,16},{25,... | collective-permute-start | bytes 2359304 | tf_op jit(solution)/shard_map/ppermute | solution.py:16
  212.1 7.3 %copy-start.9 = (f32[768]{0:T(1024)S(1)}, f32[768]{0:T(1024)}, u32[]{:S(2)}) copy-start(f32[768]{0:T(1024)} %add_convert_fusion.6) | copy-start | bytes 9220
  212.2 39.2 %collective-permute-start.14 = (bf16[256,1536]{0,1:T(8,128)(2,1)}, bf16[256,1536]{0,1:T(8,128)(2,1)S(1)}, u32[]{:S(2)}, u32[]{:S(2)}) collective-permute-start(bf16[256,1536]{0,1:T(8,128)(2,1)} %pad.8), channel_id=1, source_target_pairs={{0,8},{1,9},{2,10},{3,11},{4,12},{5,13},{6,14},{7,15},{16,24},{17,... | collective-permute-start | bytes 2359304 | tf_op jit(solution)/shard_map/ppermute | solution.py:16
  221.5 17.6 %copy-start.10 = (f32[512]{0:T(512)S(1)}, f32[512]{0:T(512)}, u32[]{:S(2)}) copy-start(f32[512]{0:T(512)} %add_convert_fusion.7) | copy-start | bytes 6148
  243.6 7.9 %copy-start.12 = (f32[512]{0:T(512)S(1)}, f32[512]{0:T(512)}, u32[]{:S(2)}) copy-start(f32[512]{0:T(512)} %add_convert_fusion.9) | copy-start | bytes 6148
  (9 other events, 19.4 us)
Sparse Core Ops, SparseCore 0:
  9.6 133.7 all-gather.1
where the time goes:
time: 267 us; the launch traced here: 263 us
  starting transfers between devices  131 us (49%)
  waiting for transfers between devices  38 us (14%)
  other arithmetic  33.4 us (13%)
  local copies, waits for them, and re-layouts  26.9 us (10%)
  matrix products  19.6 us (7%)
  between operations  13.9 us (5%)
    ppermute x16, starting transfers between devices, shifted(): return lax.ppermute(block, axis, route)  131 us
    ppermute x16, waiting for transfers between devices, shifted(): return lax.ppermute(block, axis, route)  37.2 us
    concatenate x3, local copies, waits for them, and re-layouts, rotate(): return jnp.concatenate(pieces, axis=-1)  12.4 us
    concatenate x4, other arithmetic, body(): vals_in = jnp.concatenate([entry[1] for entry in pending], axis=0)  9.92 us
    another operation x3, other arithmetic  8.99 us
    dot_general x1, matrix products, body(): jnp.dot(hidden, lax.all_gather(key_weight, 'tm', axis=0, tiled=True), pre...  8.6 us
    dot_general x4, matrix products, body(): jnp.einsum('qhd,khd->hqk', query_rot, key_heads, preferred_element_type=j...  5.89 us
  transfers between devices with their start and end apart: 17, of which 3 were waited for; matrix products, arithmetic and copies ran while one was open for 28% of the time, Pallas kernels for 0%

commit v1 on v0

v1 whole, which is shorter than its diff:
```python
import functools

import jax
import jax.numpy as jnp
import numpy as np
from jax import lax
from jax.experimental import pallas as pl
from jax.experimental.pallas import tpu as pltpu
from jax.sharding import PartitionSpec as P

BLOCK = 128
ROPE_BASE = 256.0
NORM_EPS = 1e-06
BOTH = ("group", "tm")
MIB = 1 << 20
VMEM = pl.BlockSpec(memory_space=pltpu.VMEM)
SMEM = pl.BlockSpec(memory_space=pltpu.SMEM)


def routes(groups, n, where):
    pairs = []
    for g in range(groups):
        for t in range(n):
            to = where(g, t // 4, t // 2 % 2, t % 2)
            if to is not None and 0 <= to[1] < n // 4:
                pairs.append((g * n + t, to[0] * n + (to[1] * 2 + to[2]) * 2 + to[3]))
    return pairs


def rope_layout(head_dim):
    time_len = head_dim // 8
    space_len = (head_dim - time_len) // 2
    return ((0, time_len), (time_len, space_len), (time_len + space_len, space_len))


def rope_tables(positions, head_dim):
    angles = []
    sign = np.ones((head_dim,), np.float32)
    for axis_id, (start, length) in enumerate(rope_layout(head_dim)):
        half = length // 2
        exponent = jnp.arange(half, dtype=jnp.float32) * (-2.0 / length)
        frequency = jnp.power(jnp.float32(ROPE_BASE), exponent)
        angle = positions[axis_id].astype(jnp.float32)[:, None] * frequency[None, :]
        angles += [angle, angle]
        sign[start : start + half] = -1.0
    angles = jnp.concatenate(angles, axis=-1)
    return jnp.cos(angles), jnp.sin(angles) * sign[None, :]


def norm_rotate(u, gain, cosine, sine):
    head_dim = u.shape[-1]
    mean_sq = jnp.mean(u * u, axis=-1, keepdims=True)
    u = u * lax.rsqrt(mean_sq + NORM_EPS) * gain
    lane = lax.broadcasted_iota(jnp.int32, u.shape, 1)
    other = None
    for start, length in reversed(rope_layout(head_dim)):
        half = length // 2
        ahead = pltpu.roll(u, head_dim - half, 1)
        behind = pltpu.roll(u, half, 1)
        mixed = jnp.where(lane < start + half, ahead, behind)
        other = mixed if other is None else jnp.where(lane < start + length, mixed, other)
    return u * cosine + other * sine


def query_kernel(place, own, mate, gain, cosine, sine, out):
    rows, width = own.shape
    head_dim = gain.shape[1]
    c = place[0]
    for src, slot in ((own, c), (mate, 1 - c)):
        at = pl.ds(pl.multiple_of(slot * rows, 16), rows)
        cos_t, sin_t = cosine[at, :], sine[at, :]
        for h in range(width // head_dim):
            cols = slice(h * head_dim, (h + 1) * head_dim)
            u = src[:, cols].astype(jnp.float32)
            out[at, cols] = norm_rotate(u, gain[...], cos_t, sin_t).astype(out.dtype)


def key_kernel(spans, place, own, mate, gain, cosine, sine, *refs):
    pieces, (out, hid, weight) = refs[: len(spans)], refs[len(spans) :]
    rows = own.shape[0]
    head_dim = gain.shape[1]
    half_width = weight.shape[2]
    c = place[0]
    hid[pl.ds(pl.multiple_of(c * rows, 16), rows), :] = own[...]
    hid[pl.ds(pl.multiple_of((1 - c) * rows, 16), rows), :] = mate[...]
    for i, span in enumerate(spans):
        half, first = place[1 + 2 * i], place[2 + 2 * i]
        weight[half, pl.ds(pl.multiple_of(first, 16), span), :] = pieces[i][...]
    for half in range(2):
        raw = jnp.dot(hid[...], weight[half], preferred_element_type=jnp.float32)
        for h in range(half_width // head_dim):
            u = raw[:, h * head_dim : (h + 1) * head_dim]
            at = half * half_width + h * head_dim
            out[:, at : at + head_dim] = norm_rotate(
                u, gain[...], cosine[...], sine[...]
            ).astype(out.dtype)


def attend_kernel(far, place, *refs):
    per = 5 + 2 * (far - 1)
    query, keys, vals = refs[0], refs[1 : 1 + per], refs[1 + per : 1 + 2 * per]
    keep, send, key_all, val_all, mask_all = refs[1 + 2 * per :]
    rows = query.shape[0] // 2
    head_dim = BLOCK
    heads = query.shape[1] // head_dim
    overlap = 2 * BLOCK - rows
    c, y = place[0], place[1]
    total = key_all.shape[1]
    scale = jnp.float32(head_dim ** (-0.5))

    def start_of(j):
        return pl.multiple_of(j * (rows - BLOCK), 16)

    lane = lax.broadcasted_iota(jnp.int32, (1, BLOCK), 1)

    def block_mask(j, valid):
        live = jnp.logical_and(valid == 1, jnp.logical_or(j == 0, lane >= overlap))
        return jnp.where(live, 1.0, 0.0).astype(jnp.float32)

    lower_j, lower_ok, upper_j, upper_ok = (place[2 + i] for i in range(4))
    whole = 2 * rows
    at_near, at_extra, at_side, at_far = whole, whole + 256, whole + 256 + BLOCK, whole + 256 + 2 * BLOCK
    ones = jnp.ones((1, total), jnp.float32)
    del ones

    for source, dest in ((keys, key_all), (vals, val_all)):
        own, from_below, from_above, inner, crossing = source[:5]
        for f in range(2):
            dest[f, 0:whole, :] = own[...]
            dest[f, whole:512, :] = jnp.zeros((512 - whole, dest.shape[2]), dest.dtype)
            dest[f, 512 + rows : 768, :] = jnp.zeros((256 - rows, dest.shape[2]), dest.dtype)

        def put_pair(piece, near, j):
            dest[near, 512 : 512 + rows, :] = piece[0:rows, :]
            dest[near, 768:896, :] = piece[rows : rows + BLOCK, :]
            dest[1 - near, 896:1024, :] = piece[pl.ds(start_of(j), BLOCK), :]

        @pl.when(y == 0)
        def _():
            put_pair(inner, 1, upper_j)
            put_pair(crossing, 0, lower_j)

        @pl.when(y == 1)
        def _():
            put_pair(inner, 0, lower_j)
            put_pair(crossing, 1, upper_j)

        for f in range(2):
            for side, ref in ((0, from_below), (1, from_above)):
                j = place[6 + 2 * side]
                at = 1024 + side * BLOCK
                dest[f, at : at + BLOCK, :] = ref[pl.ds(f * rows + start_of(j), BLOCK), :]
        for level in range(1, far):
            below, above = source[5 + 2 * (level - 1) : 7 + 2 * (level - 1)]
            at = 1024 + 2 * BLOCK * level
            if level < far - 1:
                for f in range(2):
                    dest[f, at : at + BLOCK, :] = below[f * BLOCK : (f + 1) * BLOCK, :]
                    dest[f, at + BLOCK : at + 2 * BLOCK, :] = above[f * BLOCK : (f + 1) * BLOCK, :]
            else:
                use_below = place[6 + 4 * level + 1] == 1

                @pl.when(use_below)
                def _():
                    for f in range(2):
                        dest[f, at : at + BLOCK, :] = below[f * BLOCK : (f + 1) * BLOCK, :]

                @pl.when(jnp.logical_not(use_below))
                def _():
                    for f in range(2):
                        dest[f, at : at + BLOCK, :] = above[f * BLOCK : (f + 1) * BLOCK, :]

    lane_512 = lax.broadcasted_iota(jnp.int32, (1, 512), 1)
    lane_256 = lax.broadcasted_iota(jnp.int32, (1, 256), 1)
    own_mask = jnp.where(lane_512 < whole, 1.0, 0.0).astype(jnp.float32)
    for f in range(2):
        near_ok, near_j = (lower_ok, lower_j) if f == 0 else (upper_ok, upper_j)
        side_ok, side_j = (upper_ok, upper_j) if f == 0 else (lower_ok, lower_j)
        mask_all[f, :, 0:512] = own_mask
        mask_all[f, :, 512:768] = jnp.where(
            jnp.logical_and(lane_256 < rows, near_ok == 1), 1.0, 0.0
        ).astype(jnp.float32)
        mask_all[f, :, 768:896] = block_mask(near_j, near_ok)
        mask_all[f, :, 896:1024] = block_mask(side_j, side_ok)
        for level in range(far):
            at = 1024 + 2 * BLOCK * level
            base = 6 + 4 * level
            low = block_mask(place[base], place[base + 1])
            high = block_mask(place[base + 2], place[base + 3])
            if level < far - 1:
                mask_all[f, :, at : at + BLOCK] = low
                mask_all[f, :, at + BLOCK : at + 2 * BLOCK] = high
            else:
                mask_all[f, :, at : at + BLOCK] = low + high

    for f in range(2):
        mask = mask_all[f]
        for h in range(heads):
            cols = slice(h * head_dim, (h + 1) * head_dim)
            q = query[f * rows : (f + 1) * rows, cols]
            scores = lax.dot_general(
                q, key_all[f, :, cols], (((1,), (1,)), ((), ())), preferred_element_type=jnp.float32
            )
            weights = jnp.exp(scores * scale) * mask
            denominator = jnp.sum(weights, axis=1, keepdims=True)
            numerator = jnp.dot(
                weights.astype(jnp.bfloat16), val_all[f, :, cols], preferred_element_type=jnp.float32
            )
            result = (numerator / denominator).astype(keep.dtype)

            @pl.when(c == f)
            def _():
                keep[:, cols] = result

            @pl.when(c != f)
            def _():
                send[:, cols] = result


def body(hidden, queries, values, key_weight, query_gain, key_gain, rope_positions, block_mask):
    groups, n = lax.axis_size("group"), lax.axis_size("tm")
    depth = n // 4
    rows, model = hidden.shape
    span, width = key_weight.shape
    head_dim = query_gain.shape[0]
    half, quarter = width // 2, width // 4
    me, tm = lax.axis_index("group"), lax.axis_index("tm")
    x, z, y, c = me % 2, tm // 4, tm // 2 % 2, tm % 2
    levels = (n - 1).bit_length()
    far = levels - 2

    def send(array, where):
        return lax.ppermute(array, BOTH, routes(groups, n, where))

    def to_mate(array):
        return send(array, lambda g, z, y, c: (g, z, y, 1 - c))

    def to_y(array):
        return send(array, lambda g, z, y, c: (g, z, 1 - y, c))

    def to_x(array):
        return send(array, lambda g, z, y, c: (g ^ 1, z, y, c))

    def to_z(array, k):
        return send(array, lambda g, z, y, c: (g, z + k, y, c))

    def around_z(array, k):
        return send(array, lambda g, z, y, c: (g, (z + k) % depth, y, c))

    def after(array, *others):
        return lax.optimization_barrier((array, *others))[0]

    def kept(distance):
        return block_mask[n - 1 + distance, 1]

    def block_start(j):
        return j * (rows - BLOCK)

    weight_own = lax.dynamic_slice_in_dim(key_weight, c * half + x * quarter, quarter, 1)
    weight_mate = to_mate(lax.dynamic_slice_in_dim(key_weight, (1 - c) * half + x * quarter, quarter, 1))
    unit = jnp.where(
        c == 0,
        jnp.concatenate([weight_own, weight_mate], 0),
        jnp.concatenate([weight_mate, weight_own], 0),
    )
    value_own = lax.dynamic_slice_in_dim(values, c * half, half, 1)
    value_mate = to_mate(lax.dynamic_slice_in_dim(values, (1 - c) * half, half, 1))
    query_own = lax.dynamic_slice_in_dim(queries, c * half, half, 1)
    query_mate = to_mate(lax.dynamic_slice_in_dim(queries, (1 - c) * half, half, 1))
    hidden_mate = to_mate(hidden)
    positions_mate = to_mate(rope_positions)

    units = [unit] + [around_z(unit, k) for k in range(1, depth)]
    pieces, spans, pieces_at = [], [], []
    for k in range(depth):
        source = (z + depth - k) % depth
        first, first_other = (source * 2 + y) * 2 * span, (source * 2 + 1 - y) * 2 * span
        by_x, by_y = to_x(units[k]), to_y(units[k])
        diag_low, diag_high = to_y(by_x[:span]), to_x(by_y[span:])
        pieces += [units[k], by_y, by_x, diag_low, diag_high]
        spans += [2 * span, 2 * span, 2 * span, span, span]
        pieces_at += [x, first, x, first_other, 1 - x, first]
        pieces_at += [1 - x, first_other, 1 - x, first_other + span]

    def both_frames(own, mate):
        return jnp.where(c == 0, jnp.concatenate([own, mate], 0), jnp.concatenate([mate, own], 0))

    def exchange(both):
        below, above = to_z(both, 1), to_z(both, -1)

        def pair_piece(whole, rest, j):
            return jnp.concatenate([whole, lax.dynamic_slice_in_dim(rest, block_start(j), BLOCK, 0)], 0)

        def up_piece(a):
            return pair_piece(a[rows:], a[:rows], kept(-2))

        def down_piece(a):
            return pair_piece(a[:rows], a[rows:], kept(2))

        def far_piece(a, j):
            return jnp.concatenate(
                [lax.dynamic_slice_in_dim(a[f * rows : (f + 1) * rows], block_start(j), BLOCK, 0) for f in (0, 1)],
                0,
            )

        inner = to_y(jnp.where(y == 0, up_piece(both), down_piece(both)))
        crossing = to_y(jnp.where(y == 1, up_piece(below), down_piece(above)))
        result = [both, below, above, inner, crossing]
        for level in range(1, far):
            step = 1 << level
            if level == 1:
                result.append(to_z(far_piece(below, kept(-4 * step)), 1))
                result.append(to_z(far_piece(above, kept(4 * step)), -1))
            else:
                result.append(to_z(far_piece(both, kept(-4 * step)), step))
                result.append(to_z(far_piece(both, kept(4 * step)), -step))
        return result

    value_parts = exchange(after(both_frames(value_own, value_mate), units[-1]))

    positions = jnp.where(
        c == 0,
        jnp.concatenate([rope_positions, positions_mate], 1),
        jnp.concatenate([positions_mate, rope_positions], 1),
    )
    cosine, sine = rope_tables(positions, head_dim)
    place = jnp.stack([c]).astype(jnp.int32)
    query_rot = pl.pallas_call(
        query_kernel,
        out_shape=jax.ShapeDtypeStruct((2 * rows, half), jnp.bfloat16),
        in_specs=[SMEM] + [VMEM] * 5,
        out_specs=VMEM,
        compiler_params=pltpu.CompilerParams(vmem_limit_bytes=24 * MIB),
        name="query_rot",
    )(place, query_own, query_mate, query_gain[None], cosine, sine)
    place = jnp.stack([c] + pieces_at).astype(jnp.int32)
    key_rot = pl.pallas_call(
        functools.partial(key_kernel, tuple(spans)),
        out_shape=jax.ShapeDtypeStruct((2 * rows, half), jnp.bfloat16),
        in_specs=[SMEM] + [VMEM] * (5 + len(pieces)),
        out_specs=VMEM,
        scratch_shapes=[
            pltpu.VMEM((2 * rows, model), jnp.bfloat16),
            pltpu.VMEM((2, model, quarter), jnp.bfloat16),
        ],
        compiler_params=pltpu.CompilerParams(vmem_limit_bytes=40 * MIB),
        name="key_rot",
    )(place, hidden, hidden_mate, key_gain[None], cosine, sine, *pieces)
    key_parts = exchange(key_rot)

    pair = tm // 2
    place = [c, y, kept(-2), pair >= 1, kept(2), pair < n // 2 - 1]
    for level in range(far):
        step = 1 << level
        place += [kept(-4 * step), z - step >= 0, kept(4 * step), z + step < depth]
    place = jnp.stack([p.astype(jnp.int32) for p in place])
    total = 1024 + 2 * BLOCK * far - BLOCK
    keep, out = pl.pallas_call(
        functools.partial(attend_kernel, far),
        out_shape=[jax.ShapeDtypeStruct((rows, half), jnp.bfloat16)] * 2,
        in_specs=[SMEM] + [VMEM] * (1 + len(key_parts) + len(value_parts)),
        out_specs=[VMEM, VMEM],
        scratch_shapes=[
            pltpu.VMEM((2, total, half), jnp.bfloat16),
            pltpu.VMEM((2, total, half), jnp.bfloat16),
            pltpu.VMEM((2, 1, total), jnp.float32),
        ],
        compiler_params=pltpu.CompilerParams(vmem_limit_bytes=40 * MIB),
        name="attend",
    )(place, query_rot, *key_parts, *value_parts)
    other = to_mate(out)
    return jnp.where(
        c == 0, jnp.concatenate([keep, other], 1), jnp.concatenate([other, keep], 1)
    )


def solution(mesh):
    in_specs = (
        P(BOTH, None),
        P(BOTH, None),
        P(BOTH, None),
        P("tm", None),
        P(),
        P(),
        P(None, BOTH),
        P(),
    )
    return jax.shard_map(body, mesh=mesh, in_specs=in_specs, out_specs=P(BOTH, None), check_vma=False)
```

time: 267 us -> 152 us (0.57); the launches traced: 263 us -> 151 us
  starting transfers between devices: 131 us -> 54 us
  other arithmetic: 33.4 us -> 7.42 us
  matrix products: 19.6 us -> 0 us
  Pallas kernels: 0 us -> 18.8 us
  waiting for transfers between devices: 38 us -> 49 us
  between operations: 13.9 us -> 3.51 us
  local copies, waits for them, and re-layouts: 26.9 us -> 18 us
    ppermute x16 -> x37, starting transfers between devices: 131 us -> 54 us  [send(): return lax.ppermute(array, BOTH, routes(groups, n, where))]
    dot_general x9 -> x0, matrix products: 19.6 us -> none  [the longest x1 8.6 us: body(): jnp.dot(hidden, lax.all_gather(key_weight, 'tm', axis=0, tiled=True), pre...]
    pallas_call x0 -> x3, Pallas kernels: none -> 18.8 us  [the longest x1 9.7 us: body(): pl.pallas_call(functools.partial(attend_kernel, far), out_shape=[jax.Shap...]
    concatenate x12 -> x4, other arithmetic: 16.9 us -> 1.66 us  [far_piece(): jnp.concatenate([lax.dynamic_slice_in_dim(a[f * rows:(f + 1) * rows], blo...]
    concatenate x3 -> x1, local copies, waits for them, and re-layouts: 12.4 us -> 0.41 us  [rope_tables(): angles = jnp.concatenate(angles, axis=-1)]
    ppermute x16 -> x37, waiting for transfers between devices: 37.2 us -> 49 us  [send(): return lax.ppermute(array, BOTH, routes(groups, n, where))]
    another operation x3 -> x0, other arithmetic: 8.99 us -> none
    reshape x3 -> x0, local copies, waits for them, and re-layouts: 5.96 us -> none  [the longest x1 2.99 us: body(): key_raw.reshape(tok_rows, head_count, head_dim)]
  transfers between devices with their start and end apart: 17 -> 37, of which waited for: 3 -> 10; matrix products, arithmetic and copies ran while one was open for 28% -> 11% of each run, Pallas kernels for 0% -> 6%
where the time goes in v1:
time: 152 us; the launch traced here: 151 us
  starting transfers between devices  54 us (36%)
  waiting for transfers between devices  49 us (32%)
  Pallas kernels  18.8 us (12%)
  local copies, waits for them, and re-layouts  18 us (12%)
  other arithmetic  7.42 us (5%)
  between operations  3.51 us (2%)
    ppermute x37, starting transfers between devices, send(): return lax.ppermute(array, BOTH, routes(groups, n, where))  54 us
    ppermute x37, waiting for transfers between devices, send(): return lax.ppermute(array, BOTH, routes(groups, n, where))  49 us
    pallas_call x1, Pallas kernels, body(): pl.pallas_call(functools.partial(attend_kernel, far), out_shape=[jax.Shap...  9.7 us
    unnamed x58, local copies, waits for them, and re-layouts  7.3 us
    pallas_call x1, Pallas kernels, body(): pl.pallas_call(functools.partial(key_kernel, tuple(spans)), out_shape=jax...  6.23 us
    another operation x1, local copies, waits for them, and re-layouts, body(): place = jnp.stack([p.astype(jnp.int32) for p in place])  3.94 us
  transfers between devices with their start and end apart: 37, of which 10 were waited for; matrix products, arithmetic and copies ran while one was open for 11% of the time, Pallas kernels for 6%

profile of v1, /device:TPU:0, one launch (start us, length us, event | category | flops | bytes accessed | tf_op | source)
XLA Modules:
  0.0 150.8 jit_solution(13214248244950494817)
XLA Ops:
  1.7 1.9 %constant_dynamic-slice_fusion.9 = (bf16[240,768]{1,0:T(8,128)(2,1)S(1)}, bf16[240,768]{1,0:T(8,128)(2,1)}) fusion(bf16[240,1536]{1,0:T(8,128)(2,1)} %param.11, s32[]{:T(128)S(6)} %select_n.136, s32[]{:T(128)S(6)} %select_n.137), kind=kLoop, calls=%fused_computation.25 | loop fusion | bytes 1474568 | tf_op jit(solution)/shard_map/dynamic_slice | solution.py:266
  8.8 2.6 %collective-permute-start.4 = (bf16[384,384]{1,0:T(8,128)(2,1)S(1)}, bf16[384,384]{1,0:T(8,128)(2,1)S(1)}, u32[]{:S(2)}, u32[]{:S(2)}) collective-permute-start(bf16[384,384]{1,0:T(8,128)(2,1)S(1)} %maximum_select_fusion.6.refs_0_), channel_id=1, source_target_pairs={{0,2},{1,3},{2,0},{3,1},{4,6},{5,7},{6,4},{7,5},{8,10},{9,11},{10,... | collective-permute-start | bytes 884744 | tf_op jit(solution)/shard_map/ppermute | solution.py:233
  11.5 1.6 %collective-permute-start.8 = (bf16[384,384]{1,0:T(8,128)(2,1)S(1)}, bf16[384,384]{1,0:T(8,128)(2,1)S(1)}, u32[]{:S(2)}, u32[]{:S(2)}) collective-permute-start(bf16[384,384]{1,0:T(8,128)(2,1)S(1)} %maximum_select_fusion.6.refs_0_), channel_id=1, source_target_pairs={{0,4},{1,5},{2,6},{3,7},{4,8},{5,9},{6,10},{7,11},{8,12},{9,13},{1... | collective-permute-start | bytes 884744 | tf_op jit(solution)/shard_map/ppermute | solution.py:233
  13.0 2.6 %collective-permute-start.13 = (bf16[384,384]{1,0:T(8,128)(2,1)S(1)}, bf16[384,384]{1,0:T(8,128)(2,1)}, u32[]{:S(2)}, u32[]{:S(2)}) collective-permute-start(bf16[384,384]{1,0:T(8,128)(2,1)S(1)} %maximum_select_fusion.6.refs_0_), channel_id=1, source_target_pairs={{0,8},{1,9},{2,10},{3,11},{4,12},{5,13},{6,14},{7,15},{8,0},{9,1},... | collective-permute-start | bytes 884744 | tf_op jit(solution)/shard_map/ppermute | solution.py:233
  17.2 1.6 %collective-permute-start.5 = (bf16[384,384]{1,0:T(8,128)(2,1)S(1)}, bf16[384,384]{1,0:T(8,128)(2,1)}, u32[]{:S(2)}, u32[]{:S(2)}) collective-permute-start(bf16[384,384]{1,0:T(8,128)(2,1)S(1)} %maximum_select_fusion.6.refs_0_), channel_id=1, source_target_pairs={{0,16},{1,17},{2,18},{3,19},{4,20},{5,21},{6,22},{7,23},{8,24},{9,... | collective-permute-start | bytes 884744 | tf_op jit(solution)/shard_map/ppermute | solution.py:233
  19.3 3.9 %collective-permute-done.8.refs_5_ = bf16[384,384]{1,0:T(8,128)(2,1)S(1)} collective-permute-done((bf16[384,384]{1,0:T(8,128)(2,1)S(1)}, bf16[384,384]{1,0:T(8,128)(2,1)S(1)}, u32[]{:S(2)}, u32[]{:S(2)}) %collective-permute-start.8) | collective-permute-done | bytes 294944 | tf_op jit(solution)/shard_map/ppermute | solution.py:233
  23.5 1.7 %collective-permute-start.10 = (bf16[384,384]{1,0:T(8,128)(2,1)S(1)}, bf16[384,384]{1,0:T(8,128)(2,1)S(1)}, u32[]{:S(2)}, u32[]{:S(2)}) collective-permute-start(bf16[384,384]{1,0:T(8,128)(2,1)S(1)} %collective-permute-done.8.refs_5_), channel_id=1, source_target_pairs={{0,16},{1,17},{2,18},{3,19},{4,20},{5,21},{6,22},{7,23},{8,24},{9,... | collective-permute-start | bytes 884744 | tf_op jit(solution)/shard_map/ppermute | solution.py:233
  25.2 10.1 %collective-permute-done.13.refs_10_ = bf16[384,384]{1,0:T(8,128)(2,1)} collective-permute-done((bf16[384,384]{1,0:T(8,128)(2,1)S(1)}, bf16[384,384]{1,0:T(8,128)(2,1)}, u32[]{:S(2)}, u32[]{:S(2)}) %collective-permute-start.13) | collective-permute-done | bytes 294944 | tf_op jit(solution)/shard_map/ppermute | solution.py:233
  37.6 8.1 %collective-permute-start.30 = (bf16[480,768]{1,0:T(8,128)(2,1)S(1)}, bf16[480,768]{1,0:T(8,128)(2,1)S(1)}, u32[]{:S(2)}, u32[]{:S(2)}) collective-permute-start(bf16[480,768]{1,0:T(8,128)(2,1)S(1)} %maximum_select_fusion.refs_8_), channel_id=1, source_target_pairs={{0,4},{1,5},{2,6},{3,7},{4,8},{5,9},{6,10},{7,11},{8,12},{9,13},{1... | collective-permute-start | bytes 2211848 | tf_op jit(solution)/shard_map/ppermute | solution.py:233
  50.7 7.0 %collective-permute-done.20.refs_17_ = bf16[384,384]{1,0:T(8,128)(2,1)S(1)} collective-permute-done((bf16[384,384]{1,0:T(8,128)(2,1)S(1)}, bf16[384,384]{1,0:T(8,128)(2,1)S(1)}, u32[]{:S(2)}, u32[]{:S(2)}) %collective-permute-start.20) | collective-permute-done | bytes 294944 | tf_op jit(solution)/shard_map/ppermute | solution.py:233
  61.9 5.6 %collective-permute-done.31.refs_10_ = bf16[480,768]{1,0:T(8,128)(2,1)S(1)} collective-permute-done((bf16[480,768]{1,0:T(8,128)(2,1)S(1)}, bf16[480,768]{1,0:T(8,128)(2,1)S(1)}, u32[]{:S(2)}, u32[]{:S(2)}) %collective-permute-start.31) | collective-permute-done | bytes 737312 | tf_op jit(solution)/shard_map/ppermute | solution.py:233
  70.2 1.5 %collective-permute-start.21 = (bf16[192,384]{1,0:T(8,128)(2,1)S(1)}, bf16[192,384]{1,0:T(8,128)(2,1)S(1)}, u32[]{:S(2)}, u32[]{:S(2)}) collective-permute-start(bf16[192,384]{1,0:T(8,128)(2,1)S(1)} %slice.149), channel_id=1, source_target_pairs={{0,2},{1,3},{2,0},{3,1},{4,6},{5,7},{6,4},{7,5},{8,10},{9,11},{10,... | collective-permute-start | bytes 442376 | tf_op jit(solution)/shard_map/ppermute | solution.py:233
  71.8 2.5 %collective-permute-done.12.refs_9_ = bf16[192,384]{1,0:T(8,128)(2,1)S(1)} collective-permute-done((bf16[192,384]{1,0:T(8,128)(2,1)S(1)}, bf16[192,384]{1,0:T(8,128)(2,1)S(1)}, u32[]{:S(2)}, u32[]{:S(2)}) %collective-permute-start.12) | collective-permute-done | bytes 147488 | tf_op jit(solution)/shard_map/ppermute | solution.py:233
  77.8 1.6 %collective-permute-start.33 = (bf16[368,768]{1,0:T(8,128)(2,1)}, bf16[368,768]{1,0:T(8,128)(2,1)}, u32[]{:S(2)}, u32[]{:S(2)}) collective-permute-start(bf16[368,768]{1,0:T(8,128)(2,1)} %maximum_select_fusion.5), channel_id=1, source_target_pairs={{0,2},{1,3},{2,0},{3,1},{4,6},{5,7},{6,4},{7,5},{8,10},{9,11},{10,... | collective-permute-start | bytes 1695752 | tf_op jit(solution)/shard_map/ppermute | solution.py:233
  79.5 6.2 %key_rot.1.refs_1_ = bf16[480,768]{1,0:T(8,128)(2,1)S(1)} custom-call(s32[41]{0:T(128)S(1)} %stack.147.place, bf16[240,3072]{1,0:T(8,128)(2,1)S(1)} %copy-done.4, bf16[240,3072]{1,0:T(8,128)(2,1)S(1)} %collective-permute-done.2.mate, f32[1,128]{1,0:T(1,128)S(1)} %bitcast.37, f32[480,128]{1,0:T(8,128)S(1)} %get-tuple-element.38.cosine, ...), custom_call_target="tpu_custom_call" | custom-call | tf_op jit(solution)/shard_map/key_rot/pallas_call | solution.py:337
  85.7 3.0 %collective-permute-start.23 = (bf16[480,768]{1,0:T(8,128)(2,1)S(1)}, bf16[480,768]{1,0:T(8,128)(2,1)S(1)}, u32[]{:S(2)}, u32[]{:S(2)}) collective-permute-start(bf16[480,768]{1,0:T(8,128)(2,1)S(1)} %key_rot.1.refs_1_), channel_id=1, source_target_pairs={{0,4},{1,5},{2,6},{3,7},{4,8},{5,9},{6,10},{7,11},{8,12},{9,13},{1... | collective-permute-start | bytes 2211848 | tf_op jit(solution)/shard_map/ppermute | solution.py:233
  91.1 12.0 %collective-permute-done.23.refs_2_ = bf16[480,768]{1,0:T(8,128)(2,1)S(1)} collective-permute-done((bf16[480,768]{1,0:T(8,128)(2,1)S(1)}, bf16[480,768]{1,0:T(8,128)(2,1)S(1)}, u32[]{:S(2)}, u32[]{:S(2)}) %collective-permute-start.23) | collective-permute-done | bytes 737312 | tf_op jit(solution)/shard_map/ppermute | solution.py:233
  103.1 4.4 %collective-permute-start.34 = (bf16[256,768]{1,0:T(8,128)(2,1)S(1)}, bf16[256,768]{1,0:T(8,128)(2,1)S(1)}, u32[]{:S(2)}, u32[]{:S(2)}) collective-permute-start(bf16[256,768]{1,0:T(8,128)(2,1)S(1)} %pad_maximum_fusion.2), channel_id=1, source_target_pairs={{0,4},{1,5},{2,6},{3,7},{4,8},{5,9},{6,10},{7,11},{8,12},{9,13},{1... | collective-permute-start | bytes 1179656 | tf_op jit(solution)/shard_map/ppermute | solution.py:233
  116.1 5.3 %collective-permute-start.27 = (bf16[256,768]{1,0:T(8,128)(2,1)}, bf16[256,768]{1,0:T(8,128)(2,1)}, u32[]{:S(2)}, u32[]{:S(2)}) collective-permute-start(bf16[256,768]{1,0:T(8,128)(2,1)} %pad_maximum_fusion), channel_id=1, source_target_pairs={{0,4},{1,5},{2,6},{3,7},{4,8},{5,9},{6,10},{7,11},{8,12},{9,13},{1... | collective-permute-start | bytes 1179656 | tf_op jit(solution)/shard_map/ppermute | solution.py:233
  123.6 3.9 %stack.132.place = s32[14]{0:T(128)S(1)} concatenate(s32[1]{0:T(128)} %bitcast.place, s32[1]{0:T(128)} %bitcast.1, s32[1]{0:T(128)} %bitcast.2, s32[1]{0:T(128)} %bitcast.3, s32[1]{0:T(128)} %bitcast.4, s32[1]{0:T(128)} %bitcast.5, s32[1]{0:T(128)} %bitcast.6, s32[1]{0:T(128)} %bitcast.7, s32[1]{0:T(128)} %bitcast.8, s32[1]{0:T(128)} %bitcast.9, s32[1]{0:T(128)} %bitcast.10, ...), dimensions={0} | concatenate | bytes 112 | tf_op jit(solution)/shard_map/stack | solution.py:356
  129.6 2.9 %query_rot.1.refs_0_ = bf16[480,768]{1,0:T(8,128)(2,1)S(1)} custom-call(s32[1]{0:T(128)} %bitcast.place, bf16[240,768]{1,0:T(8,128)(2,1)S(1)} %copy-done.5, bf16[240,768]{1,0:T(8,128)(2,1)S(1)} %copy-done.17, f32[1,128]{1,0:T(1,128)S(1)} %bitcast.38, f32[480,128]{1,0:T(8,128)S(1)} %get-tuple-element.38.cosine, f32[480,128]{1,0:T(8,128)S(1)} %get-tuple-element.37.sine), custom_call_target="tpu_custom_call" | custom-call | tf_op jit(solution)/shard_map/query_rot/pallas_call | solution.py:328
  132.5 3.7 %collective-permute-done.26.refs_5_ = bf16[368,768]{1,0:T(8,128)(2,1)} collective-permute-done((bf16[368,768]{1,0:T(8,128)(2,1)}, bf16[368,768]{1,0:T(8,128)(2,1)}, u32[]{:S(2)}, u32[]{:S(2)}) %collective-permute-start.26) | collective-permute-done | bytes 565280 | tf_op jit(solution)/shard_map/ppermute | solution.py:233
  138.3 9.7 %attend.1 = (bf16[240,768]{1,0:T(8,128)(2,1)S(1)}, bf16[240,768]{1,0:T(8,128)(2,1)S(1)}) custom-call(s32[14]{0:T(128)S(1)} %stack.132.place, bf16[480,768]{1,0:T(8,128)(2,1)S(1)} %query_rot.1.refs_0_, bf16[480,768]{1,0:T(8,128)(2,1)S(1)} %key_rot.1.refs_1_, bf16[480,768]{1,0:T(8,128)(2,1)S(1)} %copy-done.1, bf16[480,768]{1,0:T(8,128)(2,1)S(1)} %copy-done.3, ...), custom_call_target="tpu_custom_call" | custom-call | tf_op jit(solution)/shard_map/attend/pallas_call | solution.py:358
  148.1 1.7 %collective-permute-done.36 = bf16[240,768]{1,0:T(8,128)(2,1)S(1)} collective-permute-done((bf16[240,768]{1,0:T(8,128)(2,1)S(1)}, bf16[240,768]{1,0:T(8,128)(2,1)S(1)}, u32[]{:S(2)}, u32[]{:S(2)}) %collective-permute-start.36) | collective-permute-done | bytes 368672 | tf_op jit(solution)/shard_map/ppermute | solution.py:233
  (160 shorter events, 42.3 us)
Async XLA Ops:
  3.6 13.6 %collective-permute-start.29 = (bf16[240,768]{1,0:T(8,128)(2,1)}, bf16[240,768]{1,0:T(8,128)(2,1)S(1)}, u32[]{:S(2)}, u32[]{:S(2)}) collective-permute-start(bf16[240,768]{1,0:T(8,128)(2,1)} %get-tuple-element.18), channel_id=1, source_target_pairs={{0,1},{1,0},{2,3},{3,2},{4,5},{5,4},{6,7},{7,6},{8,9},{9,8},{10,11... | collective-permute-start | bytes 1105928 | tf_op jit(solution)/shard_map/ppermute | solution.py:233
  8.8 14.7 %collective-permute-start.4 = (bf16[384,384]{1,0:T(8,128)(2,1)S(1)}, bf16[384,384]{1,0:T(8,128)(2,1)S(1)}, u32[]{:S(2)}, u32[]{:S(2)}) collective-permute-start(bf16[384,384]{1,0:T(8,128)(2,1)S(1)} %maximum_select_fusion.6.refs_0_), channel_id=1, source_target_pairs={{0,2},{1,3},{2,0},{3,1},{4,6},{5,7},{6,4},{7,5},{8,10},{9,11},{10,... | collective-permute-start | bytes 884744 | tf_op jit(solution)/shard_map/ppermute | solution.py:233
  11.5 11.8 %collective-permute-start.8 = (bf16[384,384]{1,0:T(8,128)(2,1)S(1)}, bf16[384,384]{1,0:T(8,128)(2,1)S(1)}, u32[]{:S(2)}, u32[]{:S(2)}) collective-permute-start(bf16[384,384]{1,0:T(8,128)(2,1)S(1)} %maximum_select_fusion.6.refs_0_), channel_id=1, source_target_pairs={{0,4},{1,5},{2,6},{3,7},{4,8},{5,9},{6,10},{7,11},{8,12},{9,13},{1... | collective-permute-start | bytes 884744 | tf_op jit(solution)/shard_map/ppermute | solution.py:233
  13.0 22.3 %collective-permute-start.13 = (bf16[384,384]{1,0:T(8,128)(2,1)S(1)}, bf16[384,384]{1,0:T(8,128)(2,1)}, u32[]{:S(2)}, u32[]{:S(2)}) collective-permute-start(bf16[384,384]{1,0:T(8,128)(2,1)S(1)} %maximum_select_fusion.6.refs_0_), channel_id=1, source_target_pairs={{0,8},{1,9},{2,10},{3,11},{4,12},{5,13},{6,14},{7,15},{8,0},{9,1},... | collective-permute-start | bytes 884744 | tf_op jit(solution)/shard_map/ppermute | solution.py:233
  15.6 20.2 %collective-permute-start.18 = (bf16[384,384]{1,0:T(8,128)(2,1)S(1)}, bf16[384,384]{1,0:T(8,128)(2,1)S(1)}, u32[]{:S(2)}, u32[]{:S(2)}) collective-permute-start(bf16[384,384]{1,0:T(8,128)(2,1)S(1)} %maximum_select_fusion.6.refs_0_), channel_id=1, source_target_pairs={{0,12},{1,13},{2,14},{3,15},{4,0},{5,1},{6,2},{7,3},{8,4},{9,5},{1... | collective-permute-start | bytes 884744 | tf_op jit(solution)/shard_map/ppermute | solution.py:233
  17.2 20.4 %collective-permute-start.5 = (bf16[384,384]{1,0:T(8,128)(2,1)S(1)}, bf16[384,384]{1,0:T(8,128)(2,1)}, u32[]{:S(2)}, u32[]{:S(2)}) collective-permute-start(bf16[384,384]{1,0:T(8,128)(2,1)S(1)} %maximum_select_fusion.6.refs_0_), channel_id=1, source_target_pairs={{0,16},{1,17},{2,18},{3,19},{4,20},{5,21},{6,22},{7,23},{8,24},{9,... | collective-permute-start | bytes 884744 | tf_op jit(solution)/shard_map/ppermute | solution.py:233
  23.2 23.4 %collective-permute-start.9 = (bf16[384,384]{1,0:T(8,128)(2,1)S(1)}, bf16[384,384]{1,0:T(8,128)(2,1)S(1)}, u32[]{:S(2)}, u32[]{:S(2)}) collective-permute-start(bf16[384,384]{1,0:T(8,128)(2,1)S(1)} %collective-permute-done.8.refs_5_), channel_id=1, source_target_pairs={{0,2},{1,3},{2,0},{3,1},{4,6},{5,7},{6,4},{7,5},{8,10},{9,11},{10,... | collective-permute-start | bytes 884744 | tf_op jit(solution)/shard_map/ppermute | solution.py:233
  23.5 23.2 %collective-permute-start.10 = (bf16[384,384]{1,0:T(8,128)(2,1)S(1)}, bf16[384,384]{1,0:T(8,128)(2,1)S(1)}, u32[]{:S(2)}, u32[]{:S(2)}) collective-permute-start(bf16[384,384]{1,0:T(8,128)(2,1)S(1)} %collective-permute-done.8.refs_5_), channel_id=1, source_target_pairs={{0,16},{1,17},{2,18},{3,19},{4,20},{5,21},{6,22},{7,23},{8,24},{9,... | collective-permute-start | bytes 884744 | tf_op jit(solution)/shard_map/ppermute | solution.py:233
  35.3 12.7 %collective-permute-start.14 = (bf16[384,384]{1,0:T(8,128)(2,1)}, bf16[384,384]{1,0:T(8,128)(2,1)S(1)}, u32[]{:S(2)}, u32[]{:S(2)}) collective-permute-start(bf16[384,384]{1,0:T(8,128)(2,1)} %collective-permute-done.13.refs_10_), channel_id=1, source_target_pairs={{0,2},{1,3},{2,0},{3,1},{4,6},{5,7},{6,4},{7,5},{8,10},{9,11},{10,... | collective-permute-start | bytes 884744 | tf_op jit(solution)/shard_map/ppermute | solution.py:233
  35.8 12.8 %collective-permute-start.15 = (bf16[384,384]{1,0:T(8,128)(2,1)}, bf16[384,384]{1,0:T(8,128)(2,1)S(1)}, u32[]{:S(2)}, u32[]{:S(2)}) collective-permute-start(bf16[384,384]{1,0:T(8,128)(2,1)} %collective-permute-done.13.refs_10_), channel_id=1, source_target_pairs={{0,16},{1,17},{2,18},{3,19},{4,20},{5,21},{6,22},{7,23},{8,24},{9,... | collective-permute-start | bytes 884744 | tf_op jit(solution)/shard_map/ppermute | solution.py:233
  37.6 23.7 %collective-permute-start.30 = (bf16[480,768]{1,0:T(8,128)(2,1)S(1)}, bf16[480,768]{1,0:T(8,128)(2,1)S(1)}, u32[]{:S(2)}, u32[]{:S(2)}) collective-permute-start(bf16[480,768]{1,0:T(8,128)(2,1)S(1)} %maximum_select_fusion.refs_8_), channel_id=1, source_target_pairs={{0,4},{1,5},{2,6},{3,7},{4,8},{5,9},{6,10},{7,11},{8,12},{9,13},{1... | collective-permute-start | bytes 2211848 | tf_op jit(solution)/shard_map/ppermute | solution.py:233
  46.6 32.8 %collective-permute-start.2 = (bf16[240,3072]{1,0:T(8,128)(2,1)S(1)}, bf16[240,3072]{1,0:T(8,128)(2,1)S(1)}, u32[]{:S(2)}, u32[]{:S(2)}) collective-permute-start(bf16[240,3072]{1,0:T(8,128)(2,1)S(1)} %copy-done.4), channel_id=1, source_target_pairs={{0,1},{1,0},{2,3},{3,2},{4,5},{5,4},{6,7},{7,6},{8,9},{9,8},{10,11... | collective-permute-start | bytes 4423688 | tf_op jit(solution)/shard_map/ppermute | solution.py:233
  46.7 20.8 %collective-permute-start.31 = (bf16[480,768]{1,0:T(8,128)(2,1)S(1)}, bf16[480,768]{1,0:T(8,128)(2,1)S(1)}, u32[]{:S(2)}, u32[]{:S(2)}) collective-permute-start(bf16[480,768]{1,0:T(8,128)(2,1)S(1)} %maximum_select_fusion.refs_8_), channel_id=1, source_target_pairs={{4,0},{5,1},{6,2},{7,3},{8,4},{9,5},{10,6},{11,7},{12,8},{13,9},{1... | collective-permute-start | bytes 2211848 | tf_op jit(solution)/shard_map/ppermute | solution.py:233
  48.0 11.2 %collective-permute-start.19 = (bf16[384,384]{1,0:T(8,128)(2,1)S(1)}, bf16[384,384]{1,0:T(8,128)(2,1)S(1)}, u32[]{:S(2)}, u32[]{:S(2)}) collective-permute-start(bf16[384,384]{1,0:T(8,128)(2,1)S(1)} %copy-done.21), channel_id=1, source_target_pairs={{0,2},{1,3},{2,0},{3,1},{4,6},{5,7},{6,4},{7,5},{8,10},{9,11},{10,... | collective-permute-start | bytes 884744 | tf_op jit(solution)/shard_map/ppermute | solution.py:233
  76.0 34.8 %collective-permute-start = (bf16[240,768]{1,0:T(8,128)(2,1)S(1)}, bf16[240,768]{1,0:T(8,128)(2,1)S(1)}, u32[]{:S(2)}, u32[]{:S(2)}) collective-permute-start(bf16[240,768]{1,0:T(8,128)(2,1)S(1)} %copy-done.25), channel_id=1, source_target_pairs={{0,1},{1,0},{2,3},{3,2},{4,5},{5,4},{6,7},{7,6},{8,9},{9,8},{10,11... | collective-permute-start | bytes 1105928 | tf_op jit(solution)/shard_map/ppermute | solution.py:233
  77.4 35.7 %collective-permute-start.32 = (bf16[368,768]{1,0:T(8,128)(2,1)S(1)}, bf16[368,768]{1,0:T(8,128)(2,1)S(1)}, u32[]{:S(2)}, u32[]{:S(2)}) collective-permute-start(bf16[368,768]{1,0:T(8,128)(2,1)S(1)} %maximum_select_fusion.4), channel_id=1, source_target_pairs={{0,2},{1,3},{2,0},{3,1},{4,6},{5,7},{6,4},{7,5},{8,10},{9,11},{10,... | collective-permute-start | bytes 1695752 | tf_op jit(solution)/shard_map/ppermute | solution.py:233
  77.8 54.7 %collective-permute-start.33 = (bf16[368,768]{1,0:T(8,128)(2,1)}, bf16[368,768]{1,0:T(8,128)(2,1)}, u32[]{:S(2)}, u32[]{:S(2)}) collective-permute-start(bf16[368,768]{1,0:T(8,128)(2,1)} %maximum_select_fusion.5), channel_id=1, source_target_pairs={{0,2},{1,3},{2,0},{3,1},{4,6},{5,7},{6,4},{7,5},{8,10},{9,11},{10,... | collective-permute-start | bytes 1695752 | tf_op jit(solution)/shard_map/ppermute | solution.py:233
  85.7 17.4 %collective-permute-start.23 = (bf16[480,768]{1,0:T(8,128)(2,1)S(1)}, bf16[480,768]{1,0:T(8,128)(2,1)S(1)}, u32[]{:S(2)}, u32[]{:S(2)}) collective-permute-start(bf16[480,768]{1,0:T(8,128)(2,1)S(1)} %key_rot.1.refs_1_), channel_id=1, source_target_pairs={{0,4},{1,5},{2,6},{3,7},{4,8},{5,9},{6,10},{7,11},{8,12},{9,13},{1... | collective-permute-start | bytes 2211848 | tf_op jit(solution)/shard_map/ppermute | solution.py:233
  88.7 18.9 %collective-permute-start.24 = (bf16[480,768]{1,0:T(8,128)(2,1)S(1)}, bf16[480,768]{1,0:T(8,128)(2,1)S(1)}, u32[]{:S(2)}, u32[]{:S(2)}) collective-permute-start(bf16[480,768]{1,0:T(8,128)(2,1)S(1)} %key_rot.1.refs_1_), channel_id=1, source_target_pairs={{4,0},{5,1},{6,2},{7,3},{8,4},{9,5},{10,6},{11,7},{12,8},{13,9},{1... | collective-permute-start | bytes 2211848 | tf_op jit(solution)/shard_map/ppermute | solution.py:233
  103.1 12.2 %collective-permute-start.34 = (bf16[256,768]{1,0:T(8,128)(2,1)S(1)}, bf16[256,768]{1,0:T(8,128)(2,1)S(1)}, u32[]{:S(2)}, u32[]{:S(2)}) collective-permute-start(bf16[256,768]{1,0:T(8,128)(2,1)S(1)} %pad_maximum_fusion.2), channel_id=1, source_target_pairs={{0,4},{1,5},{2,6},{3,7},{4,8},{5,9},{6,10},{7,11},{8,12},{9,13},{1... | collective-permute-start | bytes 1179656 | tf_op jit(solution)/shard_map/ppermute | solution.py:233
  107.7 13.7 %collective-permute-start.35 = (bf16[256,768]{1,0:T(8,128)(2,1)S(1)}, bf16[256,768]{1,0:T(8,128)(2,1)S(1)}, u32[]{:S(2)}, u32[]{:S(2)}) collective-permute-start(bf16[256,768]{1,0:T(8,128)(2,1)S(1)} %pad_maximum_fusion.3), channel_id=1, source_target_pairs={{4,0},{5,1},{6,2},{7,3},{8,4},{9,5},{10,6},{11,7},{12,8},{13,9},{1... | collective-permute-start | bytes 1179656 | tf_op jit(solution)/shard_map/ppermute | solution.py:233
  111.6 20.9 %collective-permute-start.25 = (bf16[368,768]{1,0:T(8,128)(2,1)}, bf16[368,768]{1,0:T(8,128)(2,1)}, u32[]{:S(2)}, u32[]{:S(2)}) collective-permute-start(bf16[368,768]{1,0:T(8,128)(2,1)} %maximum_select_fusion.2), channel_id=1, source_target_pairs={{0,2},{1,3},{2,0},{3,1},{4,6},{5,7},{6,4},{7,5},{8,10},{9,11},{10,... | collective-permute-start | bytes 1695752 | tf_op jit(solution)/shard_map/ppermute | solution.py:233
  114.0 22.3 %collective-permute-start.26 = (bf16[368,768]{1,0:T(8,128)(2,1)}, bf16[368,768]{1,0:T(8,128)(2,1)}, u32[]{:S(2)}, u32[]{:S(2)}) collective-permute-start(bf16[368,768]{1,0:T(8,128)(2,1)} %maximum_select_fusion.3), channel_id=1, source_target_pairs={{0,2},{1,3},{2,0},{3,1},{4,6},{5,7},{6,4},{7,5},{8,10},{9,11},{10,... | collective-permute-start | bytes 1695752 | tf_op jit(solution)/shard_map/ppermute | solution.py:233
  116.1 16.5 %collective-permute-start.27 = (bf16[256,768]{1,0:T(8,128)(2,1)}, bf16[256,768]{1,0:T(8,128)(2,1)}, u32[]{:S(2)}, u32[]{:S(2)}) collective-permute-start(bf16[256,768]{1,0:T(8,128)(2,1)} %pad_maximum_fusion), channel_id=1, source_target_pairs={{0,4},{1,5},{2,6},{3,7},{4,8},{5,9},{6,10},{7,11},{8,12},{9,13},{1... | collective-permute-start | bytes 1179656 | tf_op jit(solution)/shard_map/ppermute | solution.py:233
  (42 other events, 315.6 us)

commit v2 on v0

v2 whole, which is shorter than its diff:
```python
import functools

import jax
import jax.numpy as jnp
import numpy as np
from jax import lax
from jax.experimental import pallas as pl
from jax.experimental.pallas import tpu as pltpu
from jax.sharding import PartitionSpec as P

BLOCK = 128
ROPE_BASE = 256.0
NORM_EPS = 1e-06
BOTH = ("group", "tm")
MIB = 1 << 20
VMEM = pl.BlockSpec(memory_space=pltpu.VMEM)
SMEM = pl.BlockSpec(memory_space=pltpu.SMEM)
ANY = pl.BlockSpec(memory_space=pl.ANY)
HBM = pl.BlockSpec(memory_space=pltpu.HBM)
SMALL = pl.CostEstimate(flops=1, bytes_accessed=1, transcendentals=0)


def routes(groups, n, where):
    pairs = []
    for g in range(groups):
        for t in range(n):
            to = where(g, t // 4, t // 2 % 2, t % 2)
            if to is not None and 0 <= to[1] < n // 4:
                pairs.append((g * n + t, to[0] * n + (to[1] * 2 + to[2]) * 2 + to[3]))
    return pairs


def rope_layout(head_dim):
    time_len = head_dim // 8
    space_len = (head_dim - time_len) // 2
    return ((0, time_len), (time_len, space_len), (time_len + space_len, space_len))


def rope_tables(positions, head_dim):
    angles = []
    sign = np.ones((head_dim,), np.float32)
    for axis_id, (start, length) in enumerate(rope_layout(head_dim)):
        half = length // 2
        exponent = jnp.arange(half, dtype=jnp.float32) * (-2.0 / length)
        frequency = jnp.power(jnp.float32(ROPE_BASE), exponent)
        angle = positions[:, axis_id, None] * frequency[None, :]
        angles += [angle, angle]
        sign[start : start + half] = -1.0
    angles = jnp.concatenate(angles, axis=-1)
    return jnp.cos(angles), jnp.sin(angles) * sign[None, :]


def norm_rotate(u, gain, cosine, sine):
    head_dim = u.shape[-1]
    mean_sq = jnp.mean(u * u, axis=-1, keepdims=True)
    u = u * lax.rsqrt(mean_sq + NORM_EPS) * gain
    lane = lax.broadcasted_iota(jnp.int32, u.shape, 1)
    other = None
    rolled = {}
    for start, length in reversed(rope_layout(head_dim)):
        half = length // 2
        if half not in rolled:
            rolled[half] = pltpu.roll(u, head_dim - half, 1), pltpu.roll(u, half, 1)
        ahead, behind = rolled[half]
        mixed = jnp.where(lane < start + half, ahead, behind)
        other = mixed if other is None else jnp.where(lane < start + length, mixed, other)
    return u * cosine + other * sine


def place_of():
    tm = lax.axis_index("tm")
    return lax.axis_index("group") % 2, tm // 4, tm // 2 % 2, tm % 2


def run_all(copies):
    for copy in copies:
        copy.start()
    for copy in copies:
        copy.wait()


def copy_rows(moves, sems):
    run_all([
        pltpu.make_async_copy(
            source.at[pl.ds(at, count)], target.at[pl.ds(to, count)], sems.at[i]
        )
        for i, (source, at, count, target, to) in enumerate(moves)
    ])


def pack_kernel(hidden, values, queries, positions, out, sems):
    model, width = hidden.shape[1], values.shape[1] // 2
    _, _, _, c = place_of()
    theirs = pl.ds(pl.multiple_of((1 - c) * width, BLOCK), width)
    run_all([
        pltpu.make_async_copy(hidden, out.at[:, pl.ds(0, model)], sems.at[0]),
        pltpu.make_async_copy(values.at[:, theirs], out.at[:, pl.ds(model, width)], sems.at[1]),
        pltpu.make_async_copy(queries.at[:, theirs], out.at[:, pl.ds(model + width, width)], sems.at[2]),
        pltpu.make_async_copy(positions, out.at[:, pl.ds(model + 2 * width, BLOCK)], sems.at[3]),
    ])


def pair_of(own, packed, width):
    _, _, _, c = place_of()
    model = packed.shape[1] - BLOCK - 2 * width
    return own.at[:, pl.ds(pl.multiple_of(c * width, BLOCK), width)], packed.at[:, pl.ds(model, width)]


def join_kernel(values, positions, packed, *refs):
    units, (joined, both, places, sems) = refs[:-4], refs[-4:]
    rows, width = values.shape[0], both.shape[1]
    size = units[0].shape[0]
    _, _, _, c = place_of()
    own, mate = pair_of(values, packed, width)
    last = packed.at[:, pl.ds(packed.shape[1] - BLOCK, BLOCK)]
    first_at, second_at = pl.multiple_of(c * rows, 16), pl.multiple_of((1 - c) * rows, 16)
    moves = [(unit, 0, size, joined, k * size) for k, unit in enumerate(units)]
    moves += [(own, 0, rows, both, first_at), (mate, 0, rows, both, second_at)]
    moves += [(positions, 0, rows, places, first_at), (last, 0, rows, places, second_at)]
    copy_rows(moves, sems)


def take_inner(kept, y, both, inner):
    rows = both.shape[0] // 2
    shift = rows - BLOCK
    middle = kept.shape[0] // 2
    whole = jnp.where(y == 0, rows, 0)
    block = jnp.where(y == 0, kept[middle - 2] * shift, rows + kept[middle + 2] * shift)
    inner[0:rows, :] = both[pl.ds(pl.multiple_of(whole, 16), rows), :]
    inner[rows:, :] = both[pl.ds(pl.multiple_of(block, 16), BLOCK), :]


def onward_kernel(forward, with_inner, kept, both, below, above, *refs):
    outs, sems = refs[:-1], refs[-1]
    rows = below.shape[0] // 2
    shift = rows - BLOCK
    middle = kept.shape[0] // 2
    _, _, y, _ = place_of()

    def start(j, frame):
        return pl.multiple_of(frame * rows + j * shift, 16)

    moves = []
    if forward:
        for out, source, j in ((outs[0], below, kept[middle - 8]), (outs[1], above, kept[middle + 8])):
            moves += [(source, start(j, f), BLOCK, out, f * BLOCK) for f in range(2)]
    to = outs[-1]
    low_j, high_j = kept[middle - 2], kept[middle + 2]

    def lower(source, at):
        return [(source, rows, rows, to, at), (source, start(low_j, 0), BLOCK, to, at + rows)]

    def upper(source, at):
        return [(source, 0, rows, to, at), (source, start(high_j, 1), BLOCK, to, at + rows)]

    at = rows + BLOCK if with_inner else 0

    @pl.when(y == 1)
    def _():
        copy_rows(moves + (upper(both, 0) if with_inner else []) + lower(below, at), sems)

    @pl.when(y == 0)
    def _():
        copy_rows(moves + (lower(both, 0) if with_inner else []) + upper(above, at), sems)


def rows_kernel(plan, *refs):
    sems = refs[-1]
    copy_rows([(refs[a], at, n, refs[b], to) for a, at, n, b, to in plan], sems)


def query_kernel(queries, packed, gain, cosine, sine, out, held, sems):
    rows, width = queries.shape[0], held.shape[1]
    head_dim = gain.shape[1]
    model = packed.shape[1] - BLOCK - 2 * width
    _, _, _, c = place_of()
    own = queries.at[:, pl.ds(pl.multiple_of(c * width, BLOCK), width)]
    mate = packed.at[:, pl.ds(model + width, width)]
    first_at, second_at = pl.multiple_of(c * rows, 16), pl.multiple_of((1 - c) * rows, 16)
    copy_rows([(own, 0, rows, held, first_at), (mate, 0, rows, held, second_at)], sems)
    for h in range(width // head_dim):
        cols = slice(h * head_dim, (h + 1) * head_dim)
        u = held[:, cols].astype(jnp.float32)
        out[:, cols] = norm_rotate(u, gain[...], cosine[...], sine[...]).astype(out.dtype)


def key_kernel(sources, n_pieces, kept, own, packed, gain, cosine, sine, *refs):
    pieces, (out, hidden, weight, sems) = refs[:n_pieces], refs[-4:]
    x, z, y, c = place_of()
    rows, model = own.shape
    head_dim = gain.shape[1]
    span = sum(source[5] for source in sources if source[2] == 0 and source[3] == 0)
    depth = model // (2 * span)
    mate = packed.at[:, pl.ds(0, model)]
    copies = []
    for i, (source, slot) in enumerate(((own, c), (mate, 1 - c))):
        at = pl.ds(pl.multiple_of(slot * rows, 16), rows)
        copies.append(pltpu.make_async_copy(source, hidden.at[at], sems.at[i]))
    for i, (piece, first, below, other_y, to, count) in enumerate(sources):
        pair = lax.rem(z + depth - below, depth) * 2 + (1 - y if other_y else y)
        at = pl.ds(pl.multiple_of(pair * span + to, 16), count)
        copies.append(
            pltpu.make_async_copy(pieces[piece].at[pl.ds(first, count)], weight.at[at], sems.at[2 + i])
        )
    run_all(copies)
    raw = jnp.dot(hidden[...], weight[...], preferred_element_type=jnp.float32)
    for h in range(weight.shape[1] // head_dim):
        cols = slice(h * head_dim, (h + 1) * head_dim)
        out[:, cols] = norm_rotate(raw[:, cols], gain[...], cosine[...], sine[...]).astype(out.dtype)
    if len(refs) > n_pieces + 4:
        first, both, inner = refs[n_pieces : n_pieces + 3]
        width = out.shape[1]
        run_all([
            pltpu.make_async_copy(
                half, both.at[:, pl.ds(pl.multiple_of(at * width, BLOCK), width)], sems.at[i]
            )
            for i, (half, at) in enumerate(((first, x), (out, 1 - x)))
        ])
        take_inner(kept, y, both, inner)


def gather(copies, dest, used, sems, kind):
    made = []
    for i, (piece, row, count, at) in enumerate(copies):
        copy = pltpu.make_async_copy(
            piece.at[pl.ds(row, count)], dest.at[pl.ds(at, count)], sems.at[kind, i]
        )
        copy.start()
        made.append(copy)
    if used < dest.shape[0]:
        dest[used:, :] = jnp.zeros((dest.shape[0] - used, dest.shape[1]), dest.dtype)
    return made


def key_mask(runs, total, overlap):
    lane = lax.broadcasted_iota(jnp.int32, (1, total), 1)
    mask, at = jnp.zeros((1, total), jnp.int32), 0
    for count, j, ok in runs:
        live = ok if j is None else jnp.where(lane < at + overlap, jnp.where(j == 0, ok, 0), ok)
        mask = jnp.where(jnp.logical_and(lane >= at, lane < at + count), live, mask)
        at += count
    return mask.astype(jnp.float32)


def attend(query, keys, vals, mask, cols):
    head_dim = query.shape[1]
    scale = jnp.float32(head_dim ** (-0.5) * np.log2(np.e))
    scores = lax.dot_general(
        query, keys[:, cols], (((1,), (1,)), ((), ())), preferred_element_type=jnp.float32
    )
    weights = jnp.exp2(scores * scale) * mask
    total = jnp.sum(weights, axis=1, keepdims=True)
    return jnp.dot(weights.astype(jnp.bfloat16), vals[:, cols], preferred_element_type=jnp.float32), total


def attend_early_kernel(depth, kept, query, *refs):
    keys, vals = refs[:4], refs[4:8]
    sums, weights, key_0, val_0, key_1, val_1, sems = refs[8:]
    rows = query.shape[0] // 2
    head_dim = BLOCK
    _, z, y, _ = place_of()
    middle = kept.shape[0] // 2
    inner_j = jnp.where(y == 0, kept[middle + 2], kept[middle - 2])
    low_j, high_j = kept[middle - 4], kept[middle + 4]
    low_ok, high_ok = jnp.where(z >= 1, 1, 0), jnp.where(z + 1 < depth, 1, 0)
    shift = rows - BLOCK
    near, other = 1 - y, y

    def plan(pieces, frame, is_near):
        own, below, above, inner = pieces
        if is_near:
            parts = [(own, 0, 2 * rows), (inner, 0, rows + BLOCK)]
        else:
            parts = [(own, 0, 2 * rows), (inner, pl.multiple_of(inner_j * shift, 16), BLOCK)]
        for piece, j in ((below, low_j), (above, high_j)):
            parts.append((piece, pl.multiple_of(frame * rows + j * shift, 16), BLOCK))
        copies, at = [], 0
        for piece, row, count in parts:
            copies.append((piece, row, count, at))
            at += count
        return copies, at

    work = []
    for i, (frame, key_all, val_all) in enumerate(((near, key_0, val_0), (other, key_1, val_1))):
        made = []
        for kind, (pieces, dest) in enumerate(((keys, key_all), (vals, val_all))):
            copies, used = plan(pieces, frame, i == 0)
            made += gather(copies, dest, used, sems.at[i], kind)
        runs = [(2 * rows, None, 1)] + ([(rows, None, 1)] if i == 0 else [])
        runs += [(BLOCK, inner_j, 1), (BLOCK, low_j, low_ok), (BLOCK, high_j, high_ok)]
        work.append((frame, key_all, val_all, made, key_mask(runs, key_all.shape[0], 2 * BLOCK - rows)))
    lane = lax.broadcasted_iota(jnp.int32, (1, weights.shape[2]), 1)
    for frame, key_all, val_all, made, mask in work:
        for copy in made:
            copy.wait()
        at = pl.ds(pl.multiple_of(frame * rows, 16), rows)
        found = jnp.zeros((rows, weights.shape[2]), jnp.float32)
        for h in range(query.shape[1] // head_dim):
            cols = slice(h * head_dim, (h + 1) * head_dim)
            sums[frame, :, cols], total = attend(query[at, cols], key_all, val_all, mask, cols)
            found = jnp.where(lane == h, total, found)
        weights[frame] = found


def attend_late_kernel(far, kept, query, sums, weights, *refs):
    per = 1 + 2 * (far - 1)
    keys, vals = refs[:per], refs[per : 2 * per]
    keep, send, key_0, val_0, key_1, val_1, sems = refs[2 * per :]
    rows = query.shape[0] // 2
    head_dim = BLOCK
    depth = 1 << far
    _, z, y, c = place_of()
    middle = kept.shape[0] // 2
    crossing_j = jnp.where(y == 0, kept[middle - 2], kept[middle + 2])
    crossing_ok = jnp.where(y == 0, jnp.where(z >= 1, 1, 0), jnp.where(z + 1 < depth, 1, 0))
    near, other = y, 1 - y
    use_below = z >= depth // 2
    runs_far = []
    for level in range(1, far - 1):
        step = 1 << level
        runs_far.append((BLOCK, kept[middle - 4 * step], jnp.where(z >= step, 1, 0)))
        runs_far.append((BLOCK, kept[middle + 4 * step], jnp.where(z + step < depth, 1, 0)))
    top = 2 * depth
    runs_far.append((BLOCK, jnp.where(use_below, kept[middle - top], kept[middle + top]), 1))

    work = []
    for i, (frame, key_all, val_all) in enumerate(((near, key_0, val_0), (other, key_1, val_1))):
        made, lasts = [], []
        first = rows + BLOCK if i == 0 else BLOCK
        used = first + BLOCK * len(runs_far)
        for kind, (pieces, dest) in enumerate(((keys, key_all), (vals, val_all))):
            at_row = pieces[0].shape[0] - (rows + BLOCK)
            if i == 0:
                copies = [(pieces[0], at_row, first, 0)]
            else:
                copies = [(pieces[0], pl.multiple_of(at_row + crossing_j * (rows - BLOCK), 16), first, 0)]
            for k in range(2 * (far - 2)):
                copies.append((pieces[1 + k], pl.multiple_of(frame * BLOCK, BLOCK), BLOCK, first + k * BLOCK))
            made += gather(copies, dest, used, sems.at[i], kind)
            for piece, taken in ((pieces[-2], use_below), (pieces[-1], jnp.logical_not(use_below))):
                copy = pltpu.make_async_copy(
                    piece.at[pl.ds(pl.multiple_of(frame * BLOCK, BLOCK), BLOCK)],
                    dest.at[pl.ds(used - BLOCK, BLOCK)],
                    sems.at[i, kind, len(copies)],
                )
                lasts.append((copy, taken))
        for copy, taken in lasts:

            @pl.when(taken)
            def _():
                copy.start()

        runs = [(rows, None, crossing_ok)] if i == 0 else []
        runs += [(BLOCK, crossing_j, crossing_ok)] + runs_far
        mask = key_mask(runs, key_all.shape[0], 2 * BLOCK - rows)
        work.append((frame, key_all, val_all, made, lasts, mask))
    for frame, key_all, val_all, made, lasts, mask in work:
        for copy in made:
            copy.wait()
        for copy, taken in lasts:

            @pl.when(taken)
            def _():
                copy.wait()

        at = pl.ds(pl.multiple_of(frame * rows, 16), rows)
        before = weights[frame]
        for h in range(query.shape[1] // head_dim):
            cols = slice(h * head_dim, (h + 1) * head_dim)
            more, total = attend(query[at, cols], key_all, val_all, mask, cols)
            result = (sums[frame, :, cols] + more) / (before[:, h : h + 1] + total)

            @pl.when(frame == c)
            def _():
                keep[:, cols] = result.astype(keep.dtype)

            @pl.when(frame != c)
            def _():
                send[:, cols] = result.astype(send.dtype)


def body(hidden, queries, values, key_weight, query_gain, key_gain, rope_positions, block_mask):
    groups, n = lax.axis_size("group"), lax.axis_size("tm")
    depth = n // 4
    rows, model = hidden.shape
    span, width = key_weight.shape
    head_dim = query_gain.shape[0]
    half, quarter = width // 2, width // 4
    me, tm = lax.axis_index("group"), lax.axis_index("tm")
    x, z, y, c = me % 2, tm // 4, tm // 2 % 2, tm % 2
    levels = (n - 1).bit_length()
    far = levels - 2

    def send(array, where):
        return lax.ppermute(array, BOTH, routes(groups, n, where))

    def to_mate(array):
        return send(array, lambda g, z, y, c: (g, z, y, 1 - c))

    def to_y(array):
        return send(array, lambda g, z, y, c: (g, z, 1 - y, c))

    def to_x(array):
        return send(array, lambda g, z, y, c: (g ^ 1, z, y, c))

    def to_z(array, k):
        return send(array, lambda g, z, y, c: (g, z + k, y, c))

    def around_z(array, k):
        return send(array, lambda g, z, y, c: (g, (z + k) % depth, y, c))

    def call(name, kernel, outs, operands, scratch, ties=(), vmem=8, dtype=jnp.bfloat16):
        n_in, n_ties = len(operands), len(ties)

        def run(*refs):
            kernel(*refs[:n_in], *refs[n_in + n_ties :])

        return pl.pallas_call(
            run,
            out_shape=[jax.ShapeDtypeStruct(shape, dtype) for shape in outs],
            in_specs=[spec for spec, _ in operands] + [ANY] * n_ties,
            out_specs=[VMEM] * len(outs),
            scratch_shapes=scratch,
            compiler_params=pltpu.CompilerParams(vmem_limit_bytes=vmem * MIB),
            cost_estimate=SMALL,
            name=name,
        )(*[array for _, array in operands], *ties)

    def dma(count):
        return pltpu.SemaphoreType.DMA((count,))

    def in_place(*arrays):
        return [(ANY, array) for array in arrays]

    def by_core(own, mate):
        return jnp.where(c == 0, jnp.concatenate([own, mate], 0), jnp.concatenate([mate, own], 0))

    kept_blocks = block_mask[:, 1]
    kept = (SMEM, kept_blocks)

    weight_mate = to_mate(lax.dynamic_slice_in_dim(key_weight, (1 - c) * half + x * quarter, quarter, 1))
    weight_own = lax.dynamic_slice_in_dim(key_weight, c * half + x * quarter, quarter, 1)
    unit = by_core(weight_own, weight_mate)
    size = 2 * span

    units = [unit]
    for _ in range(1, depth):
        units.append(around_z(units[-1], 1))
    x_0, y_0, x_1, y_1 = to_x(unit), to_y(unit), to_x(units[1]), to_y(units[1])
    low, high = call(
        "turn_early",
        functools.partial(
            rows_kernel,
            [(0, 0, span, 4, 0), (1, 0, span, 4, span), (2, span, span, 5, 0), (3, span, span, 5, span)],
        ),
        [(size, quarter)] * 2,
        in_place(x_0, x_1, y_0, y_1),
        [dma(4)],
    )
    low, high = to_y(low), to_x(high)

    positions = jnp.pad(rope_positions.T.astype(jnp.bfloat16), ((0, 0), (0, BLOCK - 3)))
    (packed,) = call(
        "pack",
        pack_kernel,
        [(rows, model + width + BLOCK)],
        [(HBM, hidden), (HBM, values), (HBM, queries), (HBM, positions)],
        [dma(4)],
        ties=[unit],
    )
    packed = to_mate(packed)
    rest = depth - 2
    joined, value_both, positions = call(
        "join",
        join_kernel,
        [(rest * size, quarter), (2 * rows, half), (2 * rows, BLOCK)],
        [(HBM, values), (HBM, positions)] + in_place(packed, *units[2:]),
        [dma(rest + 4)],
        ties=[low, high],
    )
    cosine, sine = rope_tables(positions[:, :3].astype(jnp.float32), head_dim)
    (query_rot,) = call(
        "query_rot",
        query_kernel,
        [(2 * rows, half)],
        [(HBM, queries), (ANY, packed), (VMEM, query_gain[None]), (VMEM, cosine), (VMEM, sine)],
        [pltpu.VMEM((2 * rows, half), jnp.bfloat16), dma(2)],
        vmem=24,
    )
    x_rest, y_rest = to_x(joined), to_y(joined)

    def exchange(name, both, with_inner, ties=()):
        columns = both.shape[1]
        below, above = to_z(both, 1), to_z(both, -1)
        outs = [(2 * BLOCK, columns)] * 2 if far > 1 else []
        onward = call(
            name,
            functools.partial(onward_kernel, far > 1, with_inner),
            outs + [((rows + BLOCK) * (2 if with_inner else 1), columns)],
            [kept] + in_place(both, below, above),
            [dma(8)],
            ties=ties,
        )
        later = [to_y(onward[-1])]
        for level in range(1, far):
            step = 1 << level
            if level == 1:
                later += [to_z(onward[0], 1), to_z(onward[1], -1)]
            else:
                for sign in (-1, 1):
                    j = kept_blocks[n - 1 + sign * 4 * step] * (rows - BLOCK)
                    blocks = [lax.dynamic_slice_in_dim(both, f * rows + j, BLOCK, 0) for f in (0, 1)]
                    later.append(to_z(jnp.concatenate(blocks, 0), -sign * step))
        return [both, below, above], later, onward[-1]

    value_parts, value_later, _ = exchange("value_onward", value_both, True)
    cut = rest * size // 2
    late_low, late_high = call(
        "turn_late",
        functools.partial(rows_kernel, [(0, 0, cut, 2, 0), (1, cut, cut, 3, 0)]),
        [(cut, quarter)] * 2,
        in_place(x_rest, y_rest),
        [dma(2)],
        ties=[query_rot],
    )
    turned = late_low
    late_low, late_high = to_y(late_low), to_x(late_high)

    sources_0 = [(0, 0, 0, 0, 0, size), (1, 0, 0, 1, 0, size), (2, 0, 1, 0, 0, size), (3, 0, 1, 1, 0, size)]
    sources_1 = [(0, 0, 0, 0, 0, size), (1, 0, 1, 0, 0, size)]
    for k in range(2):
        sources_1 += [(3, k * span, k, 1, 0, span), (4, k * span, k, 1, span, span)]
    for k in range(rest):
        sources_0 += [(4, k * size, k + 2, 0, 0, size), (5, k * size, k + 2, 1, 0, size)]
        sources_1.append((2, k * size, k + 2, 0, 0, size))
        for first in (k * size, k * size + span):
            late = 5 if first < cut else 6
            sources_1.append((late, first % cut, k + 2, 1, first - k * size, span))

    def keys_of(name, sources, pieces, outs, extra, ties):
        return call(
            name,
            functools.partial(key_kernel, sources, len(pieces)),
            outs,
            [kept, (HBM, hidden), (ANY, packed), (VMEM, key_gain[None]), (VMEM, cosine), (VMEM, sine)]
            + in_place(*pieces) + [(VMEM, array) for array in extra],
            ([pltpu.VMEM((2 * rows, quarter), jnp.bfloat16)] if extra else [])
            + [
                pltpu.VMEM((2 * rows, model), jnp.bfloat16),
                pltpu.VMEM((model, quarter), jnp.bfloat16),
                dma(2 + len(sources)),
            ],
            ties=ties,
            vmem=24,
        )

    pieces = (unit, y_0, units[1], y_1, joined, y_rest)
    (first_half,) = keys_of("key_rot_0", sources_0, pieces, [(2 * rows, quarter)], [], [turned])
    pieces = (x_0, x_1, x_rest, low, high, late_low, late_high)
    key_both, key_inner = keys_of(
        "key_rot_1",
        sources_1,
        pieces,
        [(2 * rows, half), (rows + BLOCK, half)],
        [first_half],
        value_later[1:3],
    )
    key_inner = to_y(key_inner)
    key_parts, key_later, key_onward = exchange("key_onward", key_both, False)

    def padded(count):
        return -(-count // BLOCK) * BLOCK

    def gathered(*counts):
        return [pltpu.VMEM((padded(count), half), jnp.bfloat16) for count in counts for _ in range(2)]

    sums, weights = call(
        "attend_early",
        functools.partial(attend_early_kernel, depth),
        [(2, rows, half), (2, rows, BLOCK)],
        [kept, (VMEM, query_rot)] + in_place(*key_parts, key_inner, *value_parts, value_later[0]),
        gathered(3 * rows + 3 * BLOCK, 2 * rows + 3 * BLOCK) + [pltpu.SemaphoreType.DMA((2, 2, 4))],
        ties=[key_onward],
        vmem=32,
        dtype=jnp.float32,
    )
    n_far = 2 * (far - 2) + 1
    keep, other = call(
        "attend_late",
        functools.partial(attend_late_kernel, far),
        [(rows, half)] * 2,
        [kept, (VMEM, query_rot), (VMEM, sums), (VMEM, weights)] + in_place(*key_later, *value_later),
        gathered(rows + (1 + n_far) * BLOCK, (1 + n_far) * BLOCK)
        + [pltpu.SemaphoreType.DMA((2, 2, 1 + n_far))],
        vmem=32,
    )
    other = to_mate(other)
    return jnp.where(
        c == 0, jnp.concatenate([keep, other], 1), jnp.concatenate([other, keep], 1)
    )


def solution(mesh):
    in_specs = (
        P(BOTH, None),
        P(BOTH, None),
        P(BOTH, None),
        P("tm", None),
        P(),
        P(),
        P(None, BOTH),
        P(),
    )
    return jax.shard_map(body, mesh=mesh, in_specs=in_specs, out_specs=P(BOTH, None), check_vma=False)
```

time: 267 us -> 152 us (0.57); the launches traced: 263 us -> 151 us
  starting transfers between devices: 131 us -> 43.8 us
  Pallas kernels: 0 us -> 36.6 us
  other arithmetic: 33.4 us -> 3.86 us
  waiting for transfers between devices: 38 us -> 59.2 us
  matrix products: 19.6 us -> 0 us
  local copies, waits for them, and re-layouts: 26.9 us -> 7.42 us
  between operations: 13.9 us -> 0.55 us
    ppermute x16 -> x27, starting transfers between devices: 131 us -> 43.8 us  [send(): return lax.ppermute(array, BOTH, routes(groups, n, where))]
    pallas_call x0 -> x11, Pallas kernels: none -> 36.6 us  [call(): pl.pallas_call(run, out_shape=[jax.ShapeDtypeStruct(shape, dtype) for sha...]
    ppermute x16 -> x27, waiting for transfers between devices: 37.2 us -> 59.2 us  [send(): return lax.ppermute(array, BOTH, routes(groups, n, where))]
    dot_general x9 -> x0, matrix products: 19.6 us -> none  [the longest x1 8.6 us: body(): jnp.dot(hidden, lax.all_gather(key_weight, 'tm', axis=0, tiled=True), pre...]
    concatenate x12 -> x0, other arithmetic: 16.9 us -> none  [the longest x4 9.92 us: body(): vals_in = jnp.concatenate([entry[1] for entry in pending], axis=0)]
    concatenate x3 -> x1, local copies, waits for them, and re-layouts: 12.4 us -> 2.4 us  [rope_tables(): angles = jnp.concatenate(angles, axis=-1)]
    another operation x3 -> x0, other arithmetic: 8.99 us -> none
    reshape x3 -> x0, local copies, waits for them, and re-layouts: 5.96 us -> none  [the longest x1 2.99 us: body(): key_raw.reshape(tok_rows, head_count, head_dim)]
  transfers between devices with their start and end apart: 17 -> 27, of which waited for: 3 -> 12; matrix products, arithmetic and copies ran while one was open for 28% -> 4% of each run, Pallas kernels for 0% -> 14%
where the time goes in v2:
time: 152 us; the launch traced here: 151 us
  waiting for transfers between devices  59.2 us (39%)
  starting transfers between devices  43.8 us (29%)
  Pallas kernels  36.6 us (24%)
  local copies, waits for them, and re-layouts  7.42 us (5%)
  other arithmetic  3.86 us (3%)
    ppermute x27, waiting for transfers between devices, send(): return lax.ppermute(array, BOTH, routes(groups, n, where))  59.2 us
    ppermute x27, starting transfers between devices, send(): return lax.ppermute(array, BOTH, routes(groups, n, where))  43.8 us
    pallas_call x11, Pallas kernels, call(): pl.pallas_call(run, out_shape=[jax.ShapeDtypeStruct(shape, dtype) for sha...  36.6 us
    unnamed x48, local copies, waits for them, and re-layouts  3.31 us
  transfers between devices with their start and end apart: 27, of which 12 were waited for; matrix products, arithmetic and copies ran while one was open for 4% of the time, Pallas kernels for 14%

profile of v2, /device:TPU:0, one launch (start us, length us, event | category | flops | bytes accessed | tf_op | source)
XLA Modules:
  0.0 151.4 jit_solution(9590406713222727756)
XLA Ops:
  5.9 2.7 %collective-permute-start.2 = (bf16[384,384]{1,0:T(8,128)(2,1)S(1)}, bf16[384,384]{1,0:T(8,128)(2,1)S(1)}, u32[]{:S(2)}, u32[]{:S(2)}) collective-permute-start(bf16[384,384]{1,0:T(8,128)(2,1)S(1)} %maximum_select_fusion.1.refs_4_.refs_6_), channel_id=1, source_target_pairs={{0,4},{1,5},{2,6},{3,7},{4,8},{5,9},{6,10},{7,11},{8,12},{9,13},{1... | collective-permute-start | bytes 884744 | tf_op jit(solution)/shard_map/ppermute | solution.py:395
  8.6 1.5 %collective-permute-start.7 = (bf16[384,384]{1,0:T(8,128)(2,1)S(1)}, bf16[384,384]{1,0:T(8,128)(2,1)S(1)}, u32[]{:S(2)}, u32[]{:S(2)}) collective-permute-start(bf16[384,384]{1,0:T(8,128)(2,1)S(1)} %maximum_select_fusion.1.refs_4_.refs_6_), channel_id=1, source_target_pairs={{0,2},{1,3},{2,0},{3,1},{4,6},{5,7},{6,4},{7,5},{8,10},{9,11},{10,... | collective-permute-start | bytes 884744 | tf_op jit(solution)/shard_map/ppermute | solution.py:395
  10.1 1.5 collective-permute-start.5
  11.6 6.5 %collective-permute-done.2.refs_8_ = bf16[384,384]{1,0:T(8,128)(2,1)S(1)} collective-permute-done((bf16[384,384]{1,0:T(8,128)(2,1)S(1)}, bf16[384,384]{1,0:T(8,128)(2,1)S(1)}, u32[]{:S(2)}, u32[]{:S(2)}) %collective-permute-start.2) | collective-permute-done | bytes 294944 | tf_op jit(solution)/shard_map/ppermute | solution.py:395
  18.1 1.5 %collective-permute-start.8 = (bf16[384,384]{1,0:T(8,128)(2,1)S(1)}, bf16[384,384]{1,0:T(8,128)(2,1)S(1)}, u32[]{:S(2)}, u32[]{:S(2)}) collective-permute-start(bf16[384,384]{1,0:T(8,128)(2,1)S(1)} %collective-permute-done.2.refs_8_), channel_id=1, source_target_pairs={{0,2},{1,3},{2,0},{3,1},{4,6},{5,7},{6,4},{7,5},{8,10},{9,11},{10,... | collective-permute-start | bytes 884744 | tf_op jit(solution)/shard_map/ppermute | solution.py:395
  21.9 4.9 %collective-permute-done.8.refs_3_.refs_9_ = bf16[384,384]{1,0:T(8,128)(2,1)S(1)} collective-permute-done((bf16[384,384]{1,0:T(8,128)(2,1)S(1)}, bf16[384,384]{1,0:T(8,128)(2,1)S(1)}, u32[]{:S(2)}, u32[]{:S(2)}) %collective-permute-start.8) | collective-permute-done | bytes 294944 | tf_op jit(solution)/shard_map/ppermute | solution.py:395
  31.0 8.8 %collective-permute-done.4.refs_4_ = bf16[384,384]{1,0:T(8,128)(2,1)S(1)} collective-permute-done((bf16[384,384]{1,0:T(8,128)(2,1)S(1)}, bf16[384,384]{1,0:T(8,128)(2,1)S(1)}, u32[]{:S(2)}, u32[]{:S(2)}) %collective-permute-start.4) | collective-permute-done | bytes 294944 | tf_op jit(solution)/shard_map/ppermute | solution.py:395
  44.3 5.4 %collective-permute-start.15 = (bf16[480,768]{1,0:T(8,128)(2,1)}, bf16[480,768]{1,0:T(8,128)(2,1)}, u32[]{:S(2)}, u32[]{:S(2)}) collective-permute-start(bf16[480,768]{1,0:T(8,128)(2,1)} %get-tuple-element.30.refs_1_.refs_6_), channel_id=1, source_target_pairs={{0,4},{1,5},{2,6},{3,7},{4,8},{5,9},{6,10},{7,11},{8,12},{9,13},{1... | collective-permute-start | bytes 2211848 | tf_op jit(solution)/shard_map/ppermute | solution.py:395
  51.3 2.4 %concatenate.17 = f32[480,128]{1,0:T(8,128)} concatenate(f32[480,8]{1,0:T(8,128)S(1)} %broadcast_multiply_fusion.2, f32[480,8]{1,0:T(8,128)S(1)} %broadcast_multiply_fusion.2, f32[480,28]{1,0:T(8,128)} %get-tuple-element.51, f32[480,28]{1,0:T(8,128)} %get-tuple-element.51, f32[480,28]{1,0:T(8,128)} %get-tuple-element.50, f32[480,28]{1,0:T(8,128)} %get-tuple-element.50), dimensions={1} | concatenate | bytes 491520 | tf_op jit(solution)/shard_map/concatenate | solution.py:49
  53.7 6.0 %collective-permute-done.16.refs_3_.refs_8_ = bf16[480,768]{1,0:T(8,128)(2,1)} collective-permute-done((bf16[480,768]{1,0:T(8,128)(2,1)}, bf16[480,768]{1,0:T(8,128)(2,1)}, u32[]{:S(2)}, u32[]{:S(2)}) %collective-permute-start.16) | collective-permute-done | bytes 737312 | tf_op jit(solution)/shard_map/ppermute | solution.py:395
  60.9 2.2 %value_onward.1 = (bf16[256,768]{1,0:T(8,128)(2,1)S(1)}, bf16[256,768]{1,0:T(8,128)(2,1)S(1)}, bf16[736,768]{1,0:T(8,128)(2,1)S(1)}) custom-call(s32[31]{0:T(128)S(1)} %slice_bitcast_fusion.refs_0_, bf16[480,768]{1,0:T(8,128)(2,1)} %get-tuple-element.30.refs_1_.refs_6_, bf16[480,768]{1,0:T(8,128)(2,1)} %collective-permute-done.15.refs_2_.refs_7_, ...), custom_call_target="tpu_custom_call" | custom-call | flops 1 | bytes 1 | tf_op jit(solution)/shard_map/value_onward/pallas_call | solution.py:418
  63.1 4.4 %collective-permute-start.17 = (bf16[256,768]{1,0:T(8,128)(2,1)S(1)}, bf16[256,768]{1,0:T(8,128)(2,1)S(1)}, u32[]{:S(2)}, u32[]{:S(2)}) collective-permute-start(bf16[256,768]{1,0:T(8,128)(2,1)S(1)} %get-tuple-element.31), channel_id=1, source_target_pairs={{0,4},{1,5},{2,6},{3,7},{4,8},{5,9},{6,10},{7,11},{8,12},{9,13},{1... | collective-permute-start | bytes 1179656 | tf_op jit(solution)/shard_map/ppermute | solution.py:395
  69.7 2.3 %query_rot.1.refs_2_.refs_1_ = bf16[480,768]{1,0:T(8,128)(2,1)S(1)} custom-call(bf16[240,1536]{1,0:T(8,128)(2,1)S(1)} %copy-done.2, bf16[240,4736]{1,0:T(8,128)(2,1)S(1)} %collective-permute-done.1.refs_2_.refs_1_, f32[1,128]{1,0:T(1,128)S(1)} %bitcast.7, f32[480,128]{1,0:T(8,128)S(1)} %get-tuple-element.49.refs_3_.refs_4_, ...), custom_call_target="tpu_custom_call" | custom-call | flops 1 | bytes 1 | tf_op jit(solution)/shard_map/query_rot/pallas_call | solution.py:418
  73.3 1.6 %collective-permute-start.14 = (bf16[384,384]{1,0:T(8,128)(2,1)S(1)}, bf16[384,384]{1,0:T(8,128)(2,1)S(1)}, u32[]{:S(2)}, u32[]{:S(2)}) collective-permute-start(bf16[384,384]{1,0:T(8,128)(2,1)S(1)} %get-tuple-element.29), channel_id=1, source_target_pairs={{0,16},{1,17},{2,18},{3,19},{4,20},{5,21},{6,22},{7,23},{8,24},{9,... | collective-permute-start | bytes 884744 | tf_op jit(solution)/shard_map/ppermute | solution.py:395
  76.4 5.6 %key_rot_0.1.refs_13_ = bf16[480,384]{1,0:T(8,128)(2,1)S(1)} custom-call(s32[31]{0:T(128)S(1)} %slice_bitcast_fusion.refs_0_, bf16[240,3072]{1,0:T(8,128)(2,1)S(1)} %copy-done.1, bf16[240,4736]{1,0:T(8,128)(2,1)S(1)} %collective-permute-done.1.refs_2_.refs_1_, f32[1,128]{1,0:T(1,128)S(1)} %bitcast.5, f32[480,128]{1,0:T(8,128)S(1)} %get-tuple-element.49.refs_3_.refs_4_, ...), custom_call_target="tpu_custom_call" | custom-call | flops 1 | bytes 1 | tf_op jit(solution)/shard_map/key_rot_0/pallas_call | solution.py:418
  82.1 6.7 %key_rot_1.1 = (bf16[480,768]{1,0:T(8,128)(2,1)S(1)}, bf16[368,768]{1,0:T(8,128)(2,1)S(1)}) custom-call(s32[31]{0:T(128)S(1)} %slice_bitcast_fusion.refs_0_, bf16[240,3072]{1,0:T(8,128)(2,1)S(1)} %copy-done.1, bf16[240,4736]{1,0:T(8,128)(2,1)S(1)} %collective-permute-done.1.refs_2_.refs_1_, f32[1,128]{1,0:T(1,128)S(1)} %bitcast.6, ...), custom_call_target="tpu_custom_call" | custom-call | flops 1 | bytes 1 | tf_op jit(solution)/shard_map/key_rot_1/pallas_call | solution.py:418
  90.0 5.2 %collective-permute-start.19 = (bf16[480,768]{1,0:T(8,128)(2,1)S(1)}, bf16[480,768]{1,0:T(8,128)(2,1)S(1)}, u32[]{:S(2)}, u32[]{:S(2)}) collective-permute-start(bf16[480,768]{1,0:T(8,128)(2,1)S(1)} %get-tuple-element.33.refs_1_.refs_2_), channel_id=1, source_target_pairs={{0,4},{1,5},{2,6},{3,7},{4,8},{5,9},{6,10},{7,11},{8,12},{9,13},{1... | collective-permute-start | bytes 2211848 | tf_op jit(solution)/shard_map/ppermute | solution.py:395
  97.4 6.9 %collective-permute-done.20.refs_3_.refs_4_ = bf16[480,768]{1,0:T(8,128)(2,1)S(1)} collective-permute-done((bf16[480,768]{1,0:T(8,128)(2,1)S(1)}, bf16[480,768]{1,0:T(8,128)(2,1)S(1)}, u32[]{:S(2)}, u32[]{:S(2)}) %collective-permute-start.20) | collective-permute-done | bytes 737312 | tf_op jit(solution)/shard_map/ppermute | solution.py:395
  105.5 2.1 %key_onward.1 = (bf16[256,768]{1,0:T(8,128)(2,1)S(1)}, bf16[256,768]{1,0:T(8,128)(2,1)S(1)}, bf16[368,768]{1,0:T(8,128)(2,1)S(1)}) custom-call(s32[31]{0:T(128)S(1)} %slice_bitcast_fusion.refs_0_, bf16[480,768]{1,0:T(8,128)(2,1)S(1)} %get-tuple-element.33.refs_1_.refs_2_, bf16[480,768]{1,0:T(8,128)(2,1)S(1)} %collective-permute-done.19.refs_2_.refs_3_, ...), custom_call_target="tpu_custom_call" | custom-call | flops 1 | bytes 1 | tf_op jit(solution)/shard_map/key_onward/pallas_call | solution.py:418
  107.9 4.4 %collective-permute-start.24 = (bf16[256,768]{1,0:T(8,128)(2,1)S(1)}, bf16[256,768]{1,0:T(8,128)(2,1)S(1)}, u32[]{:S(2)}, u32[]{:S(2)}) collective-permute-start(bf16[256,768]{1,0:T(8,128)(2,1)S(1)} %get-tuple-element.39), channel_id=1, source_target_pairs={{0,4},{1,5},{2,6},{3,7},{4,8},{5,9},{6,10},{7,11},{8,12},{9,13},{1... | collective-permute-start | bytes 1179656 | tf_op jit(solution)/shard_map/ppermute | solution.py:395
  113.8 20.6 %collective-permute-done.21.refs_5_ = bf16[368,768]{1,0:T(8,128)(2,1)S(1)} collective-permute-done((bf16[368,768]{1,0:T(8,128)(2,1)S(1)}, bf16[368,768]{1,0:T(8,128)(2,1)S(1)}, u32[]{:S(2)}, u32[]{:S(2)}) %collective-permute-start.21) | collective-permute-done | bytes 565280 | tf_op jit(solution)/shard_map/ppermute | solution.py:395
  134.4 6.9 %attend_early.1 = (f32[2,240,768]{2,1,0:T(8,128)S(1)}, f32[2,240,128]{2,1,0:T(8,128)S(1)}) custom-call(s32[31]{0:T(128)S(1)} %slice_bitcast_fusion.refs_0_, bf16[480,768]{1,0:T(8,128)(2,1)S(1)} %query_rot.1.refs_2_.refs_1_, bf16[480,768]{1,0:T(8,128)(2,1)S(1)} %get-tuple-element.33.refs_1_.refs_2_, ...), custom_call_target="tpu_custom_call" | custom-call | flops 1 | bytes 1 | tf_op jit(solution)/shard_map/attend_early/pallas_call | solution.py:418
  141.3 7.3 %attend_late.1 = (bf16[240,768]{1,0:T(8,128)(2,1)S(1)}, bf16[240,768]{1,0:T(8,128)(2,1)S(1)}) custom-call(s32[31]{0:T(128)S(1)} %slice_bitcast_fusion.refs_0_, bf16[480,768]{1,0:T(8,128)(2,1)S(1)} %query_rot.1.refs_2_.refs_1_, f32[2,240,768]{2,1,0:T(8,128)S(1)} %get-tuple-element.37.refs_2_, f32[2,240,128]{2,1,0:T(8,128)S(1)} %get-tuple-element.38.refs_3_, ...), custom_call_target="tpu_custom_call" | custom-call | flops 1 | bytes 1 | tf_op jit(solution)/shard_map/attend_late/pallas_call | solution.py:418
  148.7 1.7 %collective-permute-done.26 = bf16[240,768]{1,0:T(8,128)(2,1)S(1)} collective-permute-done((bf16[240,768]{1,0:T(8,128)(2,1)S(1)}, bf16[240,768]{1,0:T(8,128)(2,1)S(1)}, u32[]{:S(2)}, u32[]{:S(2)}) %collective-permute-start.26) | collective-permute-done | bytes 368672 | tf_op jit(solution)/shard_map/ppermute | solution.py:395
  (104 shorter events, 31.8 us)
Async XLA Ops:
  5.4 34.4 %collective-permute-start.1 = (bf16[240,4736]{1,0:T(8,128)(2,1)S(1)}, bf16[240,4736]{1,0:T(8,128)(2,1)S(1)}, u32[]{:S(2)}, u32[]{:S(2)}) collective-permute-start(bf16[240,4736]{1,0:T(8,128)(2,1)S(1)} %pack.1), channel_id=1, source_target_pairs={{0,1},{1,0},{2,3},{3,2},{4,5},{5,4},{6,7},{7,6},{8,9},{9,8},{10,11... | collective-permute-start | bytes 6819848 | tf_op jit(solution)/shard_map/ppermute | solution.py:395
  5.9 12.3 %collective-permute-start.2 = (bf16[384,384]{1,0:T(8,128)(2,1)S(1)}, bf16[384,384]{1,0:T(8,128)(2,1)S(1)}, u32[]{:S(2)}, u32[]{:S(2)}) collective-permute-start(bf16[384,384]{1,0:T(8,128)(2,1)S(1)} %maximum_select_fusion.1.refs_4_.refs_6_), channel_id=1, source_target_pairs={{0,4},{1,5},{2,6},{3,7},{4,8},{5,9},{6,10},{7,11},{8,12},{9,13},{1... | collective-permute-start | bytes 884744 | tf_op jit(solution)/shard_map/ppermute | solution.py:395
  8.6 12.6 %collective-permute-start.7 = (bf16[384,384]{1,0:T(8,128)(2,1)S(1)}, bf16[384,384]{1,0:T(8,128)(2,1)S(1)}, u32[]{:S(2)}, u32[]{:S(2)}) collective-permute-start(bf16[384,384]{1,0:T(8,128)(2,1)S(1)} %maximum_select_fusion.1.refs_4_.refs_6_), channel_id=1, source_target_pairs={{0,2},{1,3},{2,0},{3,1},{4,6},{5,7},{6,4},{7,5},{8,10},{9,11},{10,... | collective-permute-start | bytes 884744 | tf_op jit(solution)/shard_map/ppermute | solution.py:395
  10.1 11.8 %collective-permute-start.5 = (bf16[384,384]{1,0:T(8,128)(2,1)S(1)}, bf16[384,384]{1,0:T(8,128)(2,1)S(1)}, u32[]{:S(2)}, u32[]{:S(2)}) collective-permute-start(bf16[384,384]{1,0:T(8,128)(2,1)S(1)} %maximum_select_fusion.1.refs_4_.refs_6_), channel_id=1, source_target_pairs={{0,16},{1,17},{2,18},{3,19},{4,20},{5,21},{6,22},{7,23},{8,24},{9,... | collective-permute-start | bytes 884744 | tf_op jit(solution)/shard_map/ppermute | solution.py:395
  18.1 8.7 %collective-permute-start.8 = (bf16[384,384]{1,0:T(8,128)(2,1)S(1)}, bf16[384,384]{1,0:T(8,128)(2,1)S(1)}, u32[]{:S(2)}, u32[]{:S(2)}) collective-permute-start(bf16[384,384]{1,0:T(8,128)(2,1)S(1)} %collective-permute-done.2.refs_8_), channel_id=1, source_target_pairs={{0,2},{1,3},{2,0},{3,1},{4,6},{5,7},{6,4},{7,5},{8,10},{9,11},{10,... | collective-permute-start | bytes 884744 | tf_op jit(solution)/shard_map/ppermute | solution.py:395
  19.7 8.3 %collective-permute-start.6 = (bf16[384,384]{1,0:T(8,128)(2,1)S(1)}, bf16[384,384]{1,0:T(8,128)(2,1)S(1)}, u32[]{:S(2)}, u32[]{:S(2)}) collective-permute-start(bf16[384,384]{1,0:T(8,128)(2,1)S(1)} %collective-permute-done.2.refs_8_), channel_id=1, source_target_pairs={{0,16},{1,17},{2,18},{3,19},{4,20},{5,21},{6,22},{7,23},{8,24},{9,... | collective-permute-start | bytes 884744 | tf_op jit(solution)/shard_map/ppermute | solution.py:395
  21.2 9.8 %collective-permute-start.3 = (bf16[384,384]{1,0:T(8,128)(2,1)S(1)}, bf16[384,384]{1,0:T(8,128)(2,1)S(1)}, u32[]{:S(2)}, u32[]{:S(2)}) collective-permute-start(bf16[384,384]{1,0:T(8,128)(2,1)S(1)} %collective-permute-done.2.refs_8_), channel_id=1, source_target_pairs={{0,4},{1,5},{2,6},{3,7},{4,8},{5,9},{6,10},{7,11},{8,12},{9,13},{1... | collective-permute-start | bytes 884744 | tf_op jit(solution)/shard_map/ppermute | solution.py:395
  28.7 11.1 %collective-permute-start.9 = (bf16[384,384]{1,0:T(8,128)(2,1)S(1)}, bf16[384,384]{1,0:T(8,128)(2,1)S(1)}, u32[]{:S(2)}, u32[]{:S(2)}) collective-permute-start(bf16[384,384]{1,0:T(8,128)(2,1)S(1)} %get-tuple-element.24), channel_id=1, source_target_pairs={{0,2},{1,3},{2,0},{3,1},{4,6},{5,7},{6,4},{7,5},{8,10},{9,11},{10,... | collective-permute-start | bytes 884744 | tf_op jit(solution)/shard_map/ppermute | solution.py:395
  29.4 10.3 %collective-permute-start.10 = (bf16[384,384]{1,0:T(8,128)(2,1)S(1)}, bf16[384,384]{1,0:T(8,128)(2,1)S(1)}, u32[]{:S(2)}, u32[]{:S(2)}) collective-permute-start(bf16[384,384]{1,0:T(8,128)(2,1)S(1)} %get-tuple-element.25), channel_id=1, source_target_pairs={{0,16},{1,17},{2,18},{3,19},{4,20},{5,21},{6,22},{7,23},{8,24},{9,... | collective-permute-start | bytes 884744 | tf_op jit(solution)/shard_map/ppermute | solution.py:395
  30.9 8.9 %collective-permute-start.4 = (bf16[384,384]{1,0:T(8,128)(2,1)S(1)}, bf16[384,384]{1,0:T(8,128)(2,1)S(1)}, u32[]{:S(2)}, u32[]{:S(2)}) collective-permute-start(bf16[384,384]{1,0:T(8,128)(2,1)S(1)} %collective-permute-done.3.refs_3_), channel_id=1, source_target_pairs={{0,4},{1,5},{2,6},{3,7},{4,8},{5,9},{6,10},{7,11},{8,12},{9,13},{1... | collective-permute-start | bytes 884744 | tf_op jit(solution)/shard_map/ppermute | solution.py:395
  41.3 30.8 %collective-permute-start.12 = (bf16[768,384]{1,0:T(8,128)(2,1)}, bf16[768,384]{1,0:T(8,128)(2,1)}, u32[]{:S(2)}, u32[]{:S(2)}) collective-permute-start(bf16[768,384]{1,0:T(8,128)(2,1)} %get-tuple-element.27.refs_10_), channel_id=1, source_target_pairs={{0,2},{1,3},{2,0},{3,1},{4,6},{5,7},{6,4},{7,5},{8,10},{9,11},{10,... | collective-permute-start | bytes 1769480 | tf_op jit(solution)/shard_map/ppermute | solution.py:395
  42.5 29.6 %collective-permute-start.11 = (bf16[768,384]{1,0:T(8,128)(2,1)}, bf16[768,384]{1,0:T(8,128)(2,1)}, u32[]{:S(2)}, u32[]{:S(2)}) collective-permute-start(bf16[768,384]{1,0:T(8,128)(2,1)} %get-tuple-element.27.refs_10_), channel_id=1, source_target_pairs={{0,16},{1,17},{2,18},{3,19},{4,20},{5,21},{6,22},{7,23},{8,24},{9,... | collective-permute-start | bytes 1769480 | tf_op jit(solution)/shard_map/ppermute | solution.py:395
  43.0 16.7 %collective-permute-start.16 = (bf16[480,768]{1,0:T(8,128)(2,1)}, bf16[480,768]{1,0:T(8,128)(2,1)}, u32[]{:S(2)}, u32[]{:S(2)}) collective-permute-start(bf16[480,768]{1,0:T(8,128)(2,1)} %get-tuple-element.30.refs_1_.refs_6_), channel_id=1, source_target_pairs={{4,0},{5,1},{6,2},{7,3},{8,4},{9,5},{10,6},{11,7},{12,8},{13,9},{1... | collective-permute-start | bytes 2211848 | tf_op jit(solution)/shard_map/ppermute | solution.py:395
  44.3 16.6 %collective-permute-start.15 = (bf16[480,768]{1,0:T(8,128)(2,1)}, bf16[480,768]{1,0:T(8,128)(2,1)}, u32[]{:S(2)}, u32[]{:S(2)}) collective-permute-start(bf16[480,768]{1,0:T(8,128)(2,1)} %get-tuple-element.30.refs_1_.refs_6_), channel_id=1, source_target_pairs={{0,4},{1,5},{2,6},{3,7},{4,8},{5,9},{6,10},{7,11},{8,12},{9,13},{1... | collective-permute-start | bytes 2211848 | tf_op jit(solution)/shard_map/ppermute | solution.py:395
  63.1 18.9 %collective-permute-start.17 = (bf16[256,768]{1,0:T(8,128)(2,1)S(1)}, bf16[256,768]{1,0:T(8,128)(2,1)S(1)}, u32[]{:S(2)}, u32[]{:S(2)}) collective-permute-start(bf16[256,768]{1,0:T(8,128)(2,1)S(1)} %get-tuple-element.31), channel_id=1, source_target_pairs={{0,4},{1,5},{2,6},{3,7},{4,8},{5,9},{6,10},{7,11},{8,12},{9,13},{1... | collective-permute-start | bytes 1179656 | tf_op jit(solution)/shard_map/ppermute | solution.py:395
  67.5 14.5 %collective-permute-start.18 = (bf16[256,768]{1,0:T(8,128)(2,1)S(1)}, bf16[256,768]{1,0:T(8,128)(2,1)S(1)}, u32[]{:S(2)}, u32[]{:S(2)}) collective-permute-start(bf16[256,768]{1,0:T(8,128)(2,1)S(1)} %get-tuple-element.32), channel_id=1, source_target_pairs={{4,0},{5,1},{6,2},{7,3},{8,4},{9,5},{10,6},{11,7},{12,8},{13,9},{1... | collective-permute-start | bytes 1179656 | tf_op jit(solution)/shard_map/ppermute | solution.py:395
  73.3 8.7 %collective-permute-start.14 = (bf16[384,384]{1,0:T(8,128)(2,1)S(1)}, bf16[384,384]{1,0:T(8,128)(2,1)S(1)}, u32[]{:S(2)}, u32[]{:S(2)}) collective-permute-start(bf16[384,384]{1,0:T(8,128)(2,1)S(1)} %get-tuple-element.29), channel_id=1, source_target_pairs={{0,16},{1,17},{2,18},{3,19},{4,20},{5,21},{6,22},{7,23},{8,24},{9,... | collective-permute-start | bytes 884744 | tf_op jit(solution)/shard_map/ppermute | solution.py:395
  88.7 15.5 %collective-permute-start.20 = (bf16[480,768]{1,0:T(8,128)(2,1)S(1)}, bf16[480,768]{1,0:T(8,128)(2,1)S(1)}, u32[]{:S(2)}, u32[]{:S(2)}) collective-permute-start(bf16[480,768]{1,0:T(8,128)(2,1)S(1)} %get-tuple-element.33.refs_1_.refs_2_), channel_id=1, source_target_pairs={{4,0},{5,1},{6,2},{7,3},{8,4},{9,5},{10,6},{11,7},{12,8},{13,9},{1... | collective-permute-start | bytes 2211848 | tf_op jit(solution)/shard_map/ppermute | solution.py:395
  90.0 15.4 %collective-permute-start.19 = (bf16[480,768]{1,0:T(8,128)(2,1)S(1)}, bf16[480,768]{1,0:T(8,128)(2,1)S(1)}, u32[]{:S(2)}, u32[]{:S(2)}) collective-permute-start(bf16[480,768]{1,0:T(8,128)(2,1)S(1)} %get-tuple-element.33.refs_1_.refs_2_), channel_id=1, source_target_pairs={{0,4},{1,5},{2,6},{3,7},{4,8},{5,9},{6,10},{7,11},{8,12},{9,13},{1... | collective-permute-start | bytes 2211848 | tf_op jit(solution)/shard_map/ppermute | solution.py:395
  95.3 39.1 %collective-permute-start.22 = (bf16[736,768]{1,0:T(8,128)(2,1)S(1)}, bf16[736,768]{1,0:T(8,128)(2,1)S(1)}, u32[]{:S(2)}, u32[]{:S(2)}) collective-permute-start(bf16[736,768]{1,0:T(8,128)(2,1)S(1)} %get-tuple-element.35), channel_id=1, source_target_pairs={{0,2},{1,3},{2,0},{3,1},{4,6},{5,7},{6,4},{7,5},{8,10},{9,11},{10,... | collective-permute-start | bytes 3391496 | tf_op jit(solution)/shard_map/ppermute | solution.py:395
  96.4 38.0 %collective-permute-start.21 = (bf16[368,768]{1,0:T(8,128)(2,1)S(1)}, bf16[368,768]{1,0:T(8,128)(2,1)S(1)}, u32[]{:S(2)}, u32[]{:S(2)}) collective-permute-start(bf16[368,768]{1,0:T(8,128)(2,1)S(1)} %get-tuple-element.34), channel_id=1, source_target_pairs={{0,2},{1,3},{2,0},{3,1},{4,6},{5,7},{6,4},{7,5},{8,10},{9,11},{10,... | collective-permute-start | bytes 1695752 | tf_op jit(solution)/shard_map/ppermute | solution.py:395
  107.5 33.8 %collective-permute-start.23 = (bf16[368,768]{1,0:T(8,128)(2,1)S(1)}, bf16[368,768]{1,0:T(8,128)(2,1)S(1)}, u32[]{:S(2)}, u32[]{:S(2)}) collective-permute-start(bf16[368,768]{1,0:T(8,128)(2,1)S(1)} %get-tuple-element.36.refs_10_), channel_id=1, source_target_pairs={{0,2},{1,3},{2,0},{3,1},{4,6},{5,7},{6,4},{7,5},{8,10},{9,11},{10,... | collective-permute-start | bytes 1695752 | tf_op jit(solution)/shard_map/ppermute | solution.py:395
  107.9 33.4 %collective-permute-start.24 = (bf16[256,768]{1,0:T(8,128)(2,1)S(1)}, bf16[256,768]{1,0:T(8,128)(2,1)S(1)}, u32[]{:S(2)}, u32[]{:S(2)}) collective-permute-start(bf16[256,768]{1,0:T(8,128)(2,1)S(1)} %get-tuple-element.39), channel_id=1, source_target_pairs={{0,4},{1,5},{2,6},{3,7},{4,8},{5,9},{6,10},{7,11},{8,12},{9,13},{1... | collective-permute-start | bytes 1179656 | tf_op jit(solution)/shard_map/ppermute | solution.py:395
  112.3 29.0 %collective-permute-start.25 = (bf16[256,768]{1,0:T(8,128)(2,1)S(1)}, bf16[256,768]{1,0:T(8,128)(2,1)S(1)}, u32[]{:S(2)}, u32[]{:S(2)}) collective-permute-start(bf16[256,768]{1,0:T(8,128)(2,1)S(1)} %get-tuple-element.40), channel_id=1, source_target_pairs={{4,0},{5,1},{6,2},{7,3},{8,4},{9,5},{10,6},{11,7},{12,8},{13,9},{1... | collective-permute-start | bytes 1179656 | tf_op jit(solution)/shard_map/ppermute | solution.py:395
  (27 other events, 215.9 us)

commit v3 on v2

--- a/solution.py
+++ b/solution.py
@@ -36,18 +36,15 @@
     return ((0, time_len), (time_len, space_len), (time_len + space_len, space_len))
 
 
-def rope_tables(positions, head_dim):
-    angles = []
-    sign = np.ones((head_dim,), np.float32)
+def rope_rows(head_dim):
+    frequency, axis, sign = (np.ones((1, head_dim), np.float32) for _ in range(3))
     for axis_id, (start, length) in enumerate(rope_layout(head_dim)):
         half = length // 2
-        exponent = jnp.arange(half, dtype=jnp.float32) * (-2.0 / length)
-        frequency = jnp.power(jnp.float32(ROPE_BASE), exponent)
-        angle = positions[:, axis_id, None] * frequency[None, :]
-        angles += [angle, angle]
-        sign[start : start + half] = -1.0
-    angles = jnp.concatenate(angles, axis=-1)
-    return jnp.cos(angles), jnp.sin(angles) * sign[None, :]
+        steps = np.float32(ROPE_BASE) ** (np.arange(half, dtype=np.float32) * np.float32(-2.0 / length))
+        frequency[0, start : start + length] = np.concatenate([steps, steps])
+        axis[0, start : start + length] = axis_id
+        sign[0, start : start + half] = -1.0
+    return np.concatenate([frequency, axis, sign], 0)
 
 
 def norm_rotate(u, gain, cosine, sine):
@@ -130,7 +127,24 @@
     inner[rows:, :] = both[pl.ds(pl.multiple_of(block, 16), BLOCK), :]
 
 
-def onward_kernel(forward, with_inner, kept, both, below, above, *refs):
+def inner_kernel(kept, values, packed, inner, sems):
+    rows, width = values.shape[0], inner.shape[1]
+    _, _, y, c = place_of()
+    own, mate = pair_of(values, packed, width)
+    middle = kept.shape[0] // 2
+    j = jnp.where(y == 0, kept[middle - 2], kept[middle + 2])
+    block = pl.multiple_of(j * (rows - BLOCK), 16)
+
+    @pl.when(c == 1 - y)
+    def _():
+        copy_rows([(own, 0, rows, inner, 0), (mate, block, BLOCK, inner, rows)], sems)
+
+    @pl.when(c == y)
+    def _():
+        copy_rows([(mate, 0, rows, inner, 0), (own, block, BLOCK, inner, rows)], sems)
+
+
+def onward_kernel(forward, kept, below, above, *refs):
     outs, sems = refs[:-1], refs[-1]
     rows = below.shape[0] // 2
     shift = rows - BLOCK
@@ -145,23 +159,16 @@
         for out, source, j in ((outs[0], below, kept[middle - 8]), (outs[1], above, kept[middle + 8])):
             moves += [(source, start(j, f), BLOCK, out, f * BLOCK) for f in range(2)]
     to = outs[-1]
-    low_j, high_j = kept[middle - 2], kept[middle + 2]
-
-    def lower(source, at):
-        return [(source, rows, rows, to, at), (source, start(low_j, 0), BLOCK, to, at + rows)]
-
-    def upper(source, at):
-        return [(source, 0, rows, to, at), (source, start(high_j, 1), BLOCK, to, at + rows)]
-
-    at = rows + BLOCK if with_inner else 0
+    up = [(below, rows, rows, to, 0), (below, start(kept[middle - 2], 0), BLOCK, to, rows)]
+    down = [(above, 0, rows, to, 0), (above, start(kept[middle + 2], 1), BLOCK, to, rows)]
 
     @pl.when(y == 1)
     def _():
-        copy_rows(moves + (upper(both, 0) if with_inner else []) + lower(below, at), sems)
+        copy_rows(moves + up, sems)
 
     @pl.when(y == 0)
     def _():
-        copy_rows(moves + (lower(both, 0) if with_inner else []) + upper(above, at), sems)
+        copy_rows(moves + down, sems)
 
 
 def rows_kernel(plan, *refs):
@@ -169,7 +176,7 @@
     copy_rows([(refs[a], at, n, refs[b], to) for a, at, n, b, to in plan], sems)
 
 
-def query_kernel(queries, packed, gain, cosine, sine, out, held, sems):
+def query_kernel(queries, packed, gain, positions, lanes, out, cosine, sine, held, sems):
     rows, width = queries.shape[0], held.shape[1]
     head_dim = gain.shape[1]
     model = packed.shape[1] - BLOCK - 2 * width
@@ -178,6 +185,11 @@
     mate = packed.at[:, pl.ds(model + width, width)]
     first_at, second_at = pl.multiple_of(c * rows, 16), pl.multiple_of((1 - c) * rows, 16)
     copy_rows([(own, 0, rows, held, first_at), (mate, 0, rows, held, second_at)], sems)
+    time, row, col = (positions[:, i : i + 1].astype(jnp.float32) for i in range(3))
+    axis = lanes[1:2, :]
+    angle = jnp.where(axis == 0.0, time, jnp.where(axis == 1.0, row, col)) * lanes[0:1, :]
+    cosine[...] = jnp.cos(angle)
+    sine[...] = jnp.sin(angle) * lanes[2:3, :]
     for h in range(width // head_dim):
         cols = slice(h * head_dim, (h + 1) * head_dim)
         u = held[:, cols].astype(jnp.float32)
@@ -242,22 +254,34 @@
     return mask.astype(jnp.float32)
 
 
-def attend(query, keys, vals, mask, cols):
-    head_dim = query.shape[1]
+def attend(query, at, keys, vals, mask):
+    head_dim = BLOCK
+    heads = range(query.shape[1] // head_dim)
     scale = jnp.float32(head_dim ** (-0.5) * np.log2(np.e))
-    scores = lax.dot_general(
-        query, keys[:, cols], (((1,), (1,)), ((), ())), preferred_element_type=jnp.float32
-    )
-    weights = jnp.exp2(scores * scale) * mask
-    total = jnp.sum(weights, axis=1, keepdims=True)
-    return jnp.dot(weights.astype(jnp.bfloat16), vals[:, cols], preferred_element_type=jnp.float32), total
+    cols = [slice(h * head_dim, (h + 1) * head_dim) for h in heads]
+
+    def scores(h):
+        return lax.dot_general(
+            query[at, cols[h]],
+            keys[:, cols[h]],
+            (((1,), (1,)), ((), ())),
+            preferred_element_type=jnp.float32,
+        )
+
+    ahead = scores(0)
+    for h in heads:
+        now, ahead = ahead, scores(h + 1) if h + 1 in heads else None
+        weights = jnp.exp2(now * scale) * mask
+        total = jnp.sum(weights, axis=1, keepdims=True)
+        yield cols[h], jnp.dot(
+            weights.astype(jnp.bfloat16), vals[:, cols[h]], preferred_element_type=jnp.float32
+        ), total
 
 
 def attend_early_kernel(depth, kept, query, *refs):
     keys, vals = refs[:4], refs[4:8]
     sums, weights, key_0, val_0, key_1, val_1, sems = refs[8:]
     rows = query.shape[0] // 2
-    head_dim = BLOCK
     _, z, y, _ = place_of()
     middle = kept.shape[0] // 2
     inner_j = jnp.where(y == 0, kept[middle + 2], kept[middle - 2])
@@ -295,9 +319,8 @@
             copy.wait()
         at = pl.ds(pl.multiple_of(frame * rows, 16), rows)
         found = jnp.zeros((rows, weights.shape[2]), jnp.float32)
-        for h in range(query.shape[1] // head_dim):
-            cols = slice(h * head_dim, (h + 1) * head_dim)
-            sums[frame, :, cols], total = attend(query[at, cols], key_all, val_all, mask, cols)
+        for h, (cols, part, total) in enumerate(attend(query, at, key_all, val_all, mask)):
+            sums[frame, :, cols] = part
             found = jnp.where(lane == h, total, found)
         weights[frame] = found
 
@@ -305,9 +328,8 @@
 def attend_late_kernel(far, kept, query, sums, weights, *refs):
     per = 1 + 2 * (far - 1)
     keys, vals = refs[:per], refs[per : 2 * per]
-    keep, send, key_0, val_0, key_1, val_1, sems = refs[2 * per :]
+    keep, send, result, key_0, val_0, key_1, val_1, sems = refs[2 * per :]
     rows = query.shape[0] // 2
-    head_dim = BLOCK
     depth = 1 << far
     _, z, y, c = place_of()
     middle = kept.shape[0] // 2
@@ -329,11 +351,8 @@
         first = rows + BLOCK if i == 0 else BLOCK
         used = first + BLOCK * len(runs_far)
         for kind, (pieces, dest) in enumerate(((keys, key_all), (vals, val_all))):
-            at_row = pieces[0].shape[0] - (rows + BLOCK)
-            if i == 0:
-                copies = [(pieces[0], at_row, first, 0)]
-            else:
-                copies = [(pieces[0], pl.multiple_of(at_row + crossing_j * (rows - BLOCK), 16), first, 0)]
+            row = 0 if i == 0 else pl.multiple_of(crossing_j * (rows - BLOCK), 16)
+            copies = [(pieces[0], row, first, 0)]
             for k in range(2 * (far - 2)):
                 copies.append((pieces[1 + k], pl.multiple_of(frame * BLOCK, BLOCK), BLOCK, first + k * BLOCK))
             made += gather(copies, dest, used, sems.at[i], kind)
@@ -365,18 +384,13 @@
 
         at = pl.ds(pl.multiple_of(frame * rows, 16), rows)
         before = weights[frame]
-        for h in range(query.shape[1] // head_dim):
-            cols = slice(h * head_dim, (h + 1) * head_dim)
-            more, total = attend(query[at, cols], key_all, val_all, mask, cols)
-            result = (sums[frame, :, cols] + more) / (before[:, h : h + 1] + total)
-
-            @pl.when(frame == c)
-            def _():
-                keep[:, cols] = result.astype(keep.dtype)
-
-            @pl.when(frame != c)
-            def _():
-                send[:, cols] = result.astype(send.dtype)
+        for h, (cols, more, total) in enumerate(attend(query, at, key_all, val_all, mask)):
+            done = (sums[frame, :, cols] + more) / (before[:, h : h + 1] + total)
+            result[frame, :, cols] = done.astype(result.dtype)
+    run_all([
+        pltpu.make_async_copy(result.at[frame], out, sems.at[0, 0, i])
+        for i, (frame, out) in enumerate(((c, keep), (1 - c, send)))
+    ])
 
 
 def body(hidden, queries, values, key_weight, query_gain, key_gain, rope_positions, block_mask):
@@ -409,7 +423,7 @@
     def around_z(array, k):
         return send(array, lambda g, z, y, c: (g, (z + k) % depth, y, c))
 
-    def call(name, kernel, outs, operands, scratch, ties=(), vmem=8, dtype=jnp.bfloat16):
+    def call(name, kernel, outs, operands, scratch, ties=(), vmem=4, dtype=jnp.bfloat16):
         n_in, n_ties = len(operands), len(ties)
 
         def run(*refs):
@@ -417,7 +431,10 @@
 
         return pl.pallas_call(
             run,
-            out_shape=[jax.ShapeDtypeStruct(shape, dtype) for shape in outs],
+            out_shape=[
+                jax.ShapeDtypeStruct(shape, dtype[i] if isinstance(dtype, list) else dtype)
+                for i, shape in enumerate(outs)
+            ],
             in_specs=[spec for spec, _ in operands] + [ANY] * n_ties,
             out_specs=[VMEM] * len(outs),
             scratch_shapes=scratch,
@@ -447,17 +464,7 @@
     for _ in range(1, depth):
         units.append(around_z(units[-1], 1))
     x_0, y_0, x_1, y_1 = to_x(unit), to_y(unit), to_x(units[1]), to_y(units[1])
-    low, high = call(
-        "turn_early",
-        functools.partial(
-            rows_kernel,
-            [(0, 0, span, 4, 0), (1, 0, span, 4, span), (2, span, span, 5, 0), (3, span, span, 5, span)],
-        ),
-        [(size, quarter)] * 2,
-        in_place(x_0, x_1, y_0, y_1),
-        [dma(4)],
-    )
-    low, high = to_y(low), to_x(high)
+    xy_0, xy_1 = to_x(y_0), to_x(y_1)
 
     positions = jnp.pad(rope_positions.T.astype(jnp.bfloat16), ((0, 0), (0, BLOCK - 3)))
     (packed,) = call(
@@ -466,9 +473,17 @@
         [(rows, model + width + BLOCK)],
         [(HBM, hidden), (HBM, values), (HBM, queries), (HBM, positions)],
         [dma(4)],
-        ties=[unit],
+        ties=[x_0, y_0, units[1]],
     )
     packed = to_mate(packed)
+    (value_inner,) = call(
+        "value_inner",
+        inner_kernel,
+        [(rows + BLOCK, half)],
+        [kept, (HBM, values), (ANY, packed)],
+        [dma(2)],
+    )
+    value_inner = to_y(value_inner)
     rest = depth - 2
     joined, value_both, positions = call(
         "join",
@@ -476,29 +491,29 @@
         [(rest * size, quarter), (2 * rows, half), (2 * rows, BLOCK)],
         [(HBM, values), (HBM, positions)] + in_place(packed, *units[2:]),
         [dma(rest + 4)],
-        ties=[low, high],
-    )
-    cosine, sine = rope_tables(positions[:, :3].astype(jnp.float32), head_dim)
-    (query_rot,) = call(
+        ties=[xy_0, xy_1, x_1, value_inner],
+    )
+    query_rot, cosine, sine = call(
         "query_rot",
         query_kernel,
-        [(2 * rows, half)],
-        [(HBM, queries), (ANY, packed), (VMEM, query_gain[None]), (VMEM, cosine), (VMEM, sine)],
+        [(2 * rows, half), (2 * rows, head_dim), (2 * rows, head_dim)],
+        [(HBM, queries), (ANY, packed), (VMEM, query_gain[None]), (VMEM, positions), (VMEM, rope_rows(head_dim))],
         [pltpu.VMEM((2 * rows, half), jnp.bfloat16), dma(2)],
-        vmem=24,
+        vmem=8,
+        dtype=[jnp.bfloat16, jnp.float32, jnp.float32],
     )
     x_rest, y_rest = to_x(joined), to_y(joined)
 
-    def exchange(name, both, with_inner, ties=()):
+    def exchange(name, both, ties=()):
         columns = both.shape[1]
         below, above = to_z(both, 1), to_z(both, -1)
         outs = [(2 * BLOCK, columns)] * 2 if far > 1 else []
         onward = call(
             name,
-            functools.partial(onward_kernel, far > 1, with_inner),
-            outs + [((rows + BLOCK) * (2 if with_inner else 1), columns)],
-            [kept] + in_place(both, below, above),
-            [dma(8)],
+            functools.partial(onward_kernel, far > 1),
+            outs + [(rows + BLOCK, columns)],
+            [kept] + in_place(below, above),
+            [dma(6)],
             ties=ties,
         )
         later = [to_y(onward[-1])]
@@ -513,7 +528,6 @@
                     later.append(to_z(jnp.concatenate(blocks, 0), -sign * step))
         return [both, below, above], later, onward[-1]
 
-    value_parts, value_later, _ = exchange("value_onward", value_both, True)
     cut = rest * size // 2
     late_low, late_high = call(
         "turn_late",
@@ -528,8 +542,7 @@
 
     sources_0 = [(0, 0, 0, 0, 0, size), (1, 0, 0, 1, 0, size), (2, 0, 1, 0, 0, size), (3, 0, 1, 1, 0, size)]
     sources_1 = [(0, 0, 0, 0, 0, size), (1, 0, 1, 0, 0, size)]
-    for k in range(2):
-        sources_1 += [(3, k * span, k, 1, 0, span), (4, k * span, k, 1, span, span)]
+    sources_1 += [(3, 0, 0, 1, 0, size), (4, 0, 1, 1, 0, size)]
     for k in range(rest):
         sources_0 += [(4, k * size, k + 2, 0, 0, size), (5, k * size, k + 2, 1, 0, size)]
         sources_1.append((2, k * size, k + 2, 0, 0, size))
@@ -551,22 +564,23 @@
                 dma(2 + len(sources)),
             ],
             ties=ties,
-            vmem=24,
+            vmem=12,
         )
 
     pieces = (unit, y_0, units[1], y_1, joined, y_rest)
     (first_half,) = keys_of("key_rot_0", sources_0, pieces, [(2 * rows, quarter)], [], [turned])
-    pieces = (x_0, x_1, x_rest, low, high, late_low, late_high)
+    value_parts, value_later, value_onward = exchange("value_onward", value_both, [first_half])
+    pieces = (x_0, x_1, x_rest, xy_0, xy_1, late_low, late_high)
     key_both, key_inner = keys_of(
         "key_rot_1",
         sources_1,
         pieces,
         [(2 * rows, half), (rows + BLOCK, half)],
         [first_half],
-        value_later[1:3],
+        [value_onward],
     )
     key_inner = to_y(key_inner)
-    key_parts, key_later, key_onward = exchange("key_onward", key_both, False)
+    key_parts, key_later, key_onward = exchange("key_onward", key_both)
 
     def padded(count):
         return -(-count // BLOCK) * BLOCK
@@ -578,10 +592,10 @@
         "attend_early",
         functools.partial(attend_early_kernel, depth),
         [(2, rows, half), (2, rows, BLOCK)],
-        [kept, (VMEM, query_rot)] + in_place(*key_parts, key_inner, *value_parts, value_later[0]),
+        [kept, (VMEM, query_rot)] + in_place(*key_parts, key_inner, *value_parts, value_inner),
         gathered(3 * rows + 3 * BLOCK, 2 * rows + 3 * BLOCK) + [pltpu.SemaphoreType.DMA((2, 2, 4))],
         ties=[key_onward],
-        vmem=32,
+        vmem=16,
         dtype=jnp.float32,
     )
     n_far = 2 * (far - 2) + 1
@@ -590,9 +604,10 @@
         functools.partial(attend_late_kernel, far),
         [(rows, half)] * 2,
         [kept, (VMEM, query_rot), (VMEM, sums), (VMEM, weights)] + in_place(*key_later, *value_later),
-        gathered(rows + (1 + n_far) * BLOCK, (1 + n_far) * BLOCK)
+        [pltpu.VMEM((2, rows, half), jnp.bfloat16)]
+        + gathered(rows + (1 + n_far) * BLOCK, (1 + n_far) * BLOCK)
         + [pltpu.SemaphoreType.DMA((2, 2, 1 + n_far))],
-        vmem=32,
+        vmem=12,
     )
     other = to_mate(other)
     return jnp.where(

time: 152 us -> 131 us (0.86)
  waiting for transfers between devices: 59.2 us -> 44.5 us
  local copies, waits for them, and re-layouts: 7.42 us -> 3.8 us
  Pallas kernels: 36.6 us -> 33.6 us
  starting transfers between devices: 43.8 us -> 46.2 us
  other arithmetic: 3.86 us -> 1.83 us
    ppermute x27 -> x28, waiting for transfers between devices: 59.2 us -> 44.5 us  [send(): return lax.ppermute(array, BOTH, routes(groups, n, where))]
    pallas_call x11, Pallas kernels: 36.6 us -> 33.6 us  [call(): pl.pallas_call(run, out_shape=[jax.ShapeDtypeStruct(shape, dtype[i] if is...]
    concatenate x1 -> x0, local copies, waits for them, and re-layouts: 2.4 us -> none  [rope_tables(): angles = jnp.concatenate(angles, axis=-1)]
    ppermute x27 -> x28, starting transfers between devices: 43.8 us -> 46.2 us  [send(): return lax.ppermute(array, BOTH, routes(groups, n, where))]
    mul x3 -> x0, other arithmetic: 1.99 us -> none  [the longest x2 1.13 us: rope_tables(): angle = positions[:, axis_id, None] * frequency[None, :]]
    unnamed x48 -> x18, local copies, waits for them, and re-layouts: 3.31 us -> 2.53 us
  transfers between devices with their start and end apart: 27 -> 28, of which waited for: 12 -> 17; matrix products, arithmetic and copies ran while one was open for 4% -> 1% of each run, Pallas kernels for 14% -> 16%
where the time goes in v3:
time: 131 us; the launch traced here: 130 us
  starting transfers between devices  46.2 us (35%)
  waiting for transfers between devices  44.5 us (34%)
  Pallas kernels  33.6 us (26%)
  local copies, waits for them, and re-layouts  3.8 us (3%)
  other arithmetic  1.83 us (1%)
    ppermute x28, starting transfers between devices, send(): return lax.ppermute(array, BOTH, routes(groups, n, where))  46.2 us
    ppermute x28, waiting for transfers between devices, send(): return lax.ppermute(array, BOTH, routes(groups, n, where))  44.5 us
    pallas_call x11, Pallas kernels, call(): pl.pallas_call(run, out_shape=[jax.ShapeDtypeStruct(shape, dtype[i] if is...  33.6 us
  transfers between devices with their start and end apart: 28, of which 17 were waited for; matrix products, arithmetic and copies ran while one was open for 1% of the time, Pallas kernels for 16%

profile of v3, /device:TPU:0, one launch (start us, length us, event | category | flops | bytes accessed | tf_op | source)
XLA Modules:
  0.0 130.2 jit_solution(4391543379704893014)
XLA Ops:
  2.7 3.0 %collective-permute-start.3 = (bf16[384,384]{1,0:T(8,128)(2,1)S(1)}, bf16[384,384]{1,0:T(8,128)(2,1)S(1)}, u32[]{:S(2)}, u32[]{:S(2)}) collective-permute-start(bf16[384,384]{1,0:T(8,128)(2,1)S(1)} %maximum_select_fusion.1.refs_6_), channel_id=1, source_target_pairs={{0,4},{1,5},{2,6},{3,7},{4,8},{5,9},{6,10},{7,11},{8,12},{9,13},{1... | collective-permute-start | bytes 884744 | tf_op jit(solution)/shard_map/ppermute | solution.py:409
  9.6 5.4 %collective-permute-done.3.refs_6_.refs_8_ = bf16[384,384]{1,0:T(8,128)(2,1)S(1)} collective-permute-done((bf16[384,384]{1,0:T(8,128)(2,1)S(1)}, bf16[384,384]{1,0:T(8,128)(2,1)S(1)}, u32[]{:S(2)}, u32[]{:S(2)}) %collective-permute-start.3) | collective-permute-done | bytes 294944 | tf_op jit(solution)/shard_map/ppermute | solution.py:409
  20.6 2.2 %collective-permute-done.4.refs_2_.refs_1_ = bf16[240,4736]{1,0:T(8,128)(2,1)S(1)} collective-permute-done((bf16[240,4736]{1,0:T(8,128)(2,1)S(1)}, bf16[240,4736]{1,0:T(8,128)(2,1)S(1)}, u32[]{:S(2)}, u32[]{:S(2)}) %collective-permute-start.4) | collective-permute-done | bytes 2273312 | tf_op jit(solution)/shard_map/ppermute | solution.py:409
  26.5 1.9 %collective-permute-done.8.refs_9_ = bf16[384,384]{1,0:T(8,128)(2,1)S(1)} collective-permute-done((bf16[384,384]{1,0:T(8,128)(2,1)S(1)}, bf16[384,384]{1,0:T(8,128)(2,1)S(1)}, u32[]{:S(2)}, u32[]{:S(2)}) %collective-permute-start.8) | collective-permute-done | bytes 294944 | tf_op jit(solution)/shard_map/ppermute | solution.py:409
  31.4 2.9 %collective-permute-done.10.refs_7_ = bf16[384,384]{1,0:T(8,128)(2,1)S(1)} collective-permute-done((bf16[384,384]{1,0:T(8,128)(2,1)S(1)}, bf16[384,384]{1,0:T(8,128)(2,1)S(1)}, u32[]{:S(2)}, u32[]{:S(2)}) %collective-permute-start.10) | collective-permute-done | bytes 294944 | tf_op jit(solution)/shard_map/ppermute | solution.py:409
  34.4 6.3 %collective-permute-done.7.refs_5_.refs_9_ = bf16[384,384]{1,0:T(8,128)(2,1)S(1)} collective-permute-done((bf16[384,384]{1,0:T(8,128)(2,1)S(1)}, bf16[384,384]{1,0:T(8,128)(2,1)S(1)}, u32[]{:S(2)}, u32[]{:S(2)}) %collective-permute-start.7) | collective-permute-done | bytes 294944 | tf_op jit(solution)/shard_map/ppermute | solution.py:409
  40.7 5.2 %collective-permute-done.9.refs_6_.refs_10_ = bf16[384,384]{1,0:T(8,128)(2,1)S(1)} collective-permute-done((bf16[384,384]{1,0:T(8,128)(2,1)S(1)}, bf16[384,384]{1,0:T(8,128)(2,1)S(1)}, u32[]{:S(2)}, u32[]{:S(2)}) %collective-permute-start.9) | collective-permute-done | bytes 294944 | tf_op jit(solution)/shard_map/ppermute | solution.py:409
  50.3 4.6 %collective-permute-start.16 = (bf16[480,768]{1,0:T(8,128)(2,1)S(1)}, bf16[480,768]{1,0:T(8,128)(2,1)S(1)}, u32[]{:S(2)}, u32[]{:S(2)}) collective-permute-start(bf16[480,768]{1,0:T(8,128)(2,1)S(1)} %get-tuple-element.32.refs_6_), channel_id=1, source_target_pairs={{0,4},{1,5},{2,6},{3,7},{4,8},{5,9},{6,10},{7,11},{8,12},{9,13},{1... | collective-permute-start | bytes 2211848 | tf_op jit(solution)/shard_map/ppermute | solution.py:409
  54.9 3.3 %query_rot.1 = (bf16[480,768]{1,0:T(8,128)(2,1)S(1)}, f32[480,128]{1,0:T(8,128)S(1)}, f32[480,128]{1,0:T(8,128)S(1)}) custom-call(bf16[240,1536]{1,0:T(8,128)(2,1)S(1)} %copy-done.4, bf16[240,4736]{1,0:T(8,128)(2,1)S(1)} %collective-permute-done.4.refs_2_.refs_1_, f32[1,128]{1,0:T(1,128)S(1)} %bitcast.7, bf16[480,128]{1,0:T(8,128)(2,1)S(1)} %get-tuple-element.25.refs_3_, ...), custom_call_target="tpu_custom_call" | custom-call | flops 1 | bytes 1 | tf_op jit(solution)/shard_map/query_rot/pallas_call | solution.py:432
  58.2 2.3 %collective-permute-done.13.refs_1_.refs_11_ = bf16[768,384]{1,0:T(8,128)(2,1)S(1)} collective-permute-done((bf16[768,384]{1,0:T(8,128)(2,1)S(1)}, bf16[768,384]{1,0:T(8,128)(2,1)S(1)}, u32[]{:S(2)}, u32[]{:S(2)}) %collective-permute-start.13) | collective-permute-done | bytes 589856 | tf_op jit(solution)/shard_map/ppermute | solution.py:409
  61.6 1.6 %collective-permute-start.15 = (bf16[384,384]{1,0:T(8,128)(2,1)S(1)}, bf16[384,384]{1,0:T(8,128)(2,1)S(1)}, u32[]{:S(2)}, u32[]{:S(2)}) collective-permute-start(bf16[384,384]{1,0:T(8,128)(2,1)S(1)} %get-tuple-element.31), channel_id=1, source_target_pairs={{0,16},{1,17},{2,18},{3,19},{4,20},{5,21},{6,22},{7,23},{8,24},{9,... | collective-permute-start | bytes 884744 | tf_op jit(solution)/shard_map/ppermute | solution.py:409
  64.0 4.6 %key_rot_0.1.refs_3_.refs_13_ = bf16[480,384]{1,0:T(8,128)(2,1)S(1)} custom-call(s32[31]{0:T(128)S(1)} %slice_bitcast_fusion.refs_0_, bf16[240,3072]{1,0:T(8,128)(2,1)S(1)} %copy-done.1, bf16[240,4736]{1,0:T(8,128)(2,1)S(1)} %collective-permute-done.4.refs_2_.refs_1_, f32[1,128]{1,0:T(1,128)S(1)} %bitcast.5, f32[480,128]{1,0:T(8,128)S(1)} %get-tuple-element.27.refs_4_, ...), custom_call_target="tpu_custom_call" | custom-call | flops 1 | bytes 1 | tf_op jit(solution)/shard_map/key_rot_0/pallas_call | solution.py:432
  68.8 2.1 %value_onward.1 = (bf16[256,768]{1,0:T(8,128)(2,1)S(1)}, bf16[256,768]{1,0:T(8,128)(2,1)S(1)}, bf16[368,768]{1,0:T(8,128)(2,1)S(1)}) custom-call(s32[31]{0:T(128)S(1)} %slice_bitcast_fusion.refs_0_, bf16[480,768]{1,0:T(8,128)(2,1)S(1)} %collective-permute-done.16.refs_1_.refs_7_, bf16[480,768]{1,0:T(8,128)(2,1)S(1)} %collective-permute-done.17.refs_2_.refs_8_, ...), custom_call_target="tpu_custom_call" | custom-call | flops 1 | bytes 1 | tf_op jit(solution)/shard_map/value_onward/pallas_call | solution.py:432
  70.9 5.6 %key_rot_1.1 = (bf16[480,768]{1,0:T(8,128)(2,1)S(1)}, bf16[368,768]{1,0:T(8,128)(2,1)S(1)}) custom-call(s32[31]{0:T(128)S(1)} %slice_bitcast_fusion.refs_0_, bf16[240,3072]{1,0:T(8,128)(2,1)S(1)} %copy-done.1, bf16[240,4736]{1,0:T(8,128)(2,1)S(1)} %collective-permute-done.4.refs_2_.refs_1_, f32[1,128]{1,0:T(1,128)S(1)} %bitcast.6, ...), custom_call_target="tpu_custom_call" | custom-call | flops 1 | bytes 1 | tf_op jit(solution)/shard_map/key_rot_1/pallas_call | solution.py:432
  77.8 5.1 %collective-permute-start.18 = (bf16[480,768]{1,0:T(8,128)(2,1)S(1)}, bf16[480,768]{1,0:T(8,128)(2,1)S(1)}, u32[]{:S(2)}, u32[]{:S(2)}) collective-permute-start(bf16[480,768]{1,0:T(8,128)(2,1)S(1)} %get-tuple-element.34.refs_2_), channel_id=1, source_target_pairs={{0,4},{1,5},{2,6},{3,7},{4,8},{5,9},{6,10},{7,11},{8,12},{9,13},{1... | collective-permute-start | bytes 2211848 | tf_op jit(solution)/shard_map/ppermute | solution.py:409
  83.8 3.9 %collective-permute-start.25 = (bf16[256,768]{1,0:T(8,128)(2,1)S(1)}, bf16[256,768]{1,0:T(8,128)(2,1)S(1)}, u32[]{:S(2)}, u32[]{:S(2)}) collective-permute-start(bf16[256,768]{1,0:T(8,128)(2,1)S(1)} %get-tuple-element.41), channel_id=1, source_target_pairs={{0,4},{1,5},{2,6},{3,7},{4,8},{5,9},{6,10},{7,11},{8,12},{9,13},{1... | collective-permute-start | bytes 1179656 | tf_op jit(solution)/shard_map/ppermute | solution.py:409
  88.9 5.8 %collective-permute-done.19.refs_2_.refs_4_ = bf16[480,768]{1,0:T(8,128)(2,1)S(1)} collective-permute-done((bf16[480,768]{1,0:T(8,128)(2,1)S(1)}, bf16[480,768]{1,0:T(8,128)(2,1)S(1)}, u32[]{:S(2)}, u32[]{:S(2)}) %collective-permute-start.19) | collective-permute-done | bytes 737312 | tf_op jit(solution)/shard_map/ppermute | solution.py:409
  94.8 5.0 %collective-permute-done.18.refs_1_.refs_3_ = bf16[480,768]{1,0:T(8,128)(2,1)S(1)} collective-permute-done((bf16[480,768]{1,0:T(8,128)(2,1)S(1)}, bf16[480,768]{1,0:T(8,128)(2,1)S(1)}, u32[]{:S(2)}, u32[]{:S(2)}) %collective-permute-start.18) | collective-permute-done | bytes 737312 | tf_op jit(solution)/shard_map/ppermute | solution.py:409
  99.8 2.1 %key_onward.1 = (bf16[256,768]{1,0:T(8,128)(2,1)S(1)}, bf16[256,768]{1,0:T(8,128)(2,1)S(1)}, bf16[368,768]{1,0:T(8,128)(2,1)S(1)}) custom-call(s32[31]{0:T(128)S(1)} %slice_bitcast_fusion.refs_0_, bf16[480,768]{1,0:T(8,128)(2,1)S(1)} %collective-permute-done.18.refs_1_.refs_3_, bf16[480,768]{1,0:T(8,128)(2,1)S(1)} %collective-permute-done.19.refs_2_.refs_4_), custom_call_target="tpu_custom_call" | custom-call | flops 1 | bytes 1 | tf_op jit(solution)/shard_map/key_onward/pallas_call | solution.py:432
  104.4 4.7 %collective-permute-start.22 = (bf16[256,768]{1,0:T(8,128)(2,1)S(1)}, bf16[256,768]{1,0:T(8,128)(2,1)S(1)}, u32[]{:S(2)}, u32[]{:S(2)}) collective-permute-start(bf16[256,768]{1,0:T(8,128)(2,1)S(1)} %get-tuple-element.39), channel_id=1, source_target_pairs={{0,4},{1,5},{2,6},{3,7},{4,8},{5,9},{6,10},{7,11},{8,12},{9,13},{1... | collective-permute-start | bytes 1179656 | tf_op jit(solution)/shard_map/ppermute | solution.py:409
  110.6 8.6 %attend_early.1 = (f32[2,240,768]{2,1,0:T(8,128)S(1)}, f32[2,240,128]{2,1,0:T(8,128)S(1)}) custom-call(s32[31]{0:T(128)S(1)} %slice_bitcast_fusion.refs_0_, bf16[480,768]{1,0:T(8,128)(2,1)S(1)} %get-tuple-element.26.refs_2_.refs_1_, bf16[480,768]{1,0:T(8,128)(2,1)S(1)} %get-tuple-element.34.refs_2_, ...), custom_call_target="tpu_custom_call" | custom-call | flops 1 | bytes 1 | tf_op jit(solution)/shard_map/attend_early/pallas_call | solution.py:432
  119.2 2.1 %collective-permute-done.23.refs_6_ = bf16[256,768]{1,0:T(8,128)(2,1)S(1)} collective-permute-done((bf16[256,768]{1,0:T(8,128)(2,1)S(1)}, bf16[256,768]{1,0:T(8,128)(2,1)S(1)}, u32[]{:S(2)}, u32[]{:S(2)}) %collective-permute-start.23) | collective-permute-done | bytes 393248 | tf_op jit(solution)/shard_map/ppermute | solution.py:409
  121.3 6.1 %attend_late.1 = (bf16[240,768]{1,0:T(8,128)(2,1)S(1)}, bf16[240,768]{1,0:T(8,128)(2,1)S(1)}) custom-call(s32[31]{0:T(128)S(1)} %slice_bitcast_fusion.refs_0_, bf16[480,768]{1,0:T(8,128)(2,1)S(1)} %get-tuple-element.26.refs_2_.refs_1_, f32[2,240,768]{2,1,0:T(8,128)S(1)} %get-tuple-element.37.refs_2_, f32[2,240,128]{2,1,0:T(8,128)S(1)} %get-tuple-element.38.refs_3_, ...), custom_call_target="tpu_custom_call" | custom-call | flops 1 | bytes 1 | tf_op jit(solution)/shard_map/attend_late/pallas_call | solution.py:432
  127.4 1.7 %collective-permute-done.27 = bf16[240,768]{1,0:T(8,128)(2,1)S(1)} collective-permute-done((bf16[240,768]{1,0:T(8,128)(2,1)S(1)}, bf16[240,768]{1,0:T(8,128)(2,1)S(1)}, u32[]{:S(2)}, u32[]{:S(2)}) %collective-permute-start.27) | collective-permute-done | bytes 368672 | tf_op jit(solution)/shard_map/ppermute | solution.py:409
  (68 shorter events, 33.9 us)
Async XLA Ops:
  2.7 12.3 %collective-permute-start.3 = (bf16[384,384]{1,0:T(8,128)(2,1)S(1)}, bf16[384,384]{1,0:T(8,128)(2,1)S(1)}, u32[]{:S(2)}, u32[]{:S(2)}) collective-permute-start(bf16[384,384]{1,0:T(8,128)(2,1)S(1)} %maximum_select_fusion.1.refs_6_), channel_id=1, source_target_pairs={{0,4},{1,5},{2,6},{3,7},{4,8},{5,9},{6,10},{7,11},{8,12},{9,13},{1... | collective-permute-start | bytes 884744 | tf_op jit(solution)/shard_map/ppermute | solution.py:409
  5.7 9.3 %collective-permute-start.2 = (bf16[384,384]{1,0:T(8,128)(2,1)S(1)}, bf16[384,384]{1,0:T(8,128)(2,1)S(1)}, u32[]{:S(2)}, u32[]{:S(2)}) collective-permute-start(bf16[384,384]{1,0:T(8,128)(2,1)S(1)} %maximum_select_fusion.1.refs_6_), channel_id=1, source_target_pairs={{0,2},{1,3},{2,0},{3,1},{4,6},{5,7},{6,4},{7,5},{8,10},{9,11},{10,... | collective-permute-start | bytes 884744 | tf_op jit(solution)/shard_map/ppermute | solution.py:409
  7.2 8.5 %collective-permute-start.1 = (bf16[384,384]{1,0:T(8,128)(2,1)S(1)}, bf16[384,384]{1,0:T(8,128)(2,1)S(1)}, u32[]{:S(2)}, u32[]{:S(2)}) collective-permute-start(bf16[384,384]{1,0:T(8,128)(2,1)S(1)} %maximum_select_fusion.1.refs_6_), channel_id=1, source_target_pairs={{0,16},{1,17},{2,18},{3,19},{4,20},{5,21},{6,22},{7,23},{8,24},{9,... | collective-permute-start | bytes 884744 | tf_op jit(solution)/shard_map/ppermute | solution.py:409
  18.5 9.9 %collective-permute-start.8 = (bf16[384,384]{1,0:T(8,128)(2,1)S(1)}, bf16[384,384]{1,0:T(8,128)(2,1)S(1)}, u32[]{:S(2)}, u32[]{:S(2)}) collective-permute-start(bf16[384,384]{1,0:T(8,128)(2,1)S(1)} %collective-permute-done.3.refs_6_.refs_8_), channel_id=1, source_target_pairs={{0,2},{1,3},{2,0},{3,1},{4,6},{5,7},{6,4},{7,5},{8,10},{9,11},{10,... | collective-permute-start | bytes 884744 | tf_op jit(solution)/shard_map/ppermute | solution.py:409
  19.4 10.9 %collective-permute-start.5 = (bf16[384,384]{1,0:T(8,128)(2,1)S(1)}, bf16[384,384]{1,0:T(8,128)(2,1)S(1)}, u32[]{:S(2)}, u32[]{:S(2)}) collective-permute-start(bf16[384,384]{1,0:T(8,128)(2,1)S(1)} %collective-permute-done.3.refs_6_.refs_8_), channel_id=1, source_target_pairs={{0,4},{1,5},{2,6},{3,7},{4,8},{5,9},{6,10},{7,11},{8,12},{9,13},{1... | collective-permute-start | bytes 884744 | tf_op jit(solution)/shard_map/ppermute | solution.py:409
  23.6 22.3 %collective-permute-start.11 = (bf16[368,768]{1,0:T(8,128)(2,1)S(1)}, bf16[368,768]{1,0:T(8,128)(2,1)S(1)}, u32[]{:S(2)}, u32[]{:S(2)}) collective-permute-start(bf16[368,768]{1,0:T(8,128)(2,1)S(1)} %value_inner.1), channel_id=1, source_target_pairs={{0,2},{1,3},{2,0},{3,1},{4,6},{5,7},{6,4},{7,5},{8,10},{9,11},{10,... | collective-permute-start | bytes 1695752 | tf_op jit(solution)/shard_map/ppermute | solution.py:409
  24.5 9.9 %collective-permute-start.10 = (bf16[384,384]{1,0:T(8,128)(2,1)S(1)}, bf16[384,384]{1,0:T(8,128)(2,1)S(1)}, u32[]{:S(2)}, u32[]{:S(2)}) collective-permute-start(bf16[384,384]{1,0:T(8,128)(2,1)S(1)} %collective-permute-done.3.refs_6_.refs_8_), channel_id=1, source_target_pairs={{0,16},{1,17},{2,18},{3,19},{4,20},{5,21},{6,22},{7,23},{8,24},{9,... | collective-permute-start | bytes 884744 | tf_op jit(solution)/shard_map/ppermute | solution.py:409
  26.0 14.7 %collective-permute-start.7 = (bf16[384,384]{1,0:T(8,128)(2,1)S(1)}, bf16[384,384]{1,0:T(8,128)(2,1)S(1)}, u32[]{:S(2)}, u32[]{:S(2)}) collective-permute-start(bf16[384,384]{1,0:T(8,128)(2,1)S(1)} %collective-permute-done.2.refs_5_.refs_7_), channel_id=1, source_target_pairs={{0,16},{1,17},{2,18},{3,19},{4,20},{5,21},{6,22},{7,23},{8,24},{9,... | collective-permute-start | bytes 884744 | tf_op jit(solution)/shard_map/ppermute | solution.py:409
  28.4 17.5 %collective-permute-start.9 = (bf16[384,384]{1,0:T(8,128)(2,1)S(1)}, bf16[384,384]{1,0:T(8,128)(2,1)S(1)}, u32[]{:S(2)}, u32[]{:S(2)}) collective-permute-start(bf16[384,384]{1,0:T(8,128)(2,1)S(1)} %collective-permute-done.8.refs_9_), channel_id=1, source_target_pairs={{0,16},{1,17},{2,18},{3,19},{4,20},{5,21},{6,22},{7,23},{8,24},{9,... | collective-permute-start | bytes 884744 | tf_op jit(solution)/shard_map/ppermute | solution.py:409
  30.3 15.6 %collective-permute-start.6 = (bf16[384,384]{1,0:T(8,128)(2,1)S(1)}, bf16[384,384]{1,0:T(8,128)(2,1)S(1)}, u32[]{:S(2)}, u32[]{:S(2)}) collective-permute-start(bf16[384,384]{1,0:T(8,128)(2,1)S(1)} %collective-permute-done.5.refs_3_), channel_id=1, source_target_pairs={{0,4},{1,5},{2,6},{3,7},{4,8},{5,9},{6,10},{7,11},{8,12},{9,13},{1... | collective-permute-start | bytes 884744 | tf_op jit(solution)/shard_map/ppermute | solution.py:409
  46.2 14.3 %collective-permute-start.13 = (bf16[768,384]{1,0:T(8,128)(2,1)S(1)}, bf16[768,384]{1,0:T(8,128)(2,1)S(1)}, u32[]{:S(2)}, u32[]{:S(2)}) collective-permute-start(bf16[768,384]{1,0:T(8,128)(2,1)S(1)} %get-tuple-element.29.refs_10_), channel_id=1, source_target_pairs={{0,2},{1,3},{2,0},{3,1},{4,6},{5,7},{6,4},{7,5},{8,10},{9,11},{10,... | collective-permute-start | bytes 1769480 | tf_op jit(solution)/shard_map/ppermute | solution.py:409
  47.5 13.9 %collective-permute-start.12 = (bf16[768,384]{1,0:T(8,128)(2,1)S(1)}, bf16[768,384]{1,0:T(8,128)(2,1)S(1)}, u32[]{:S(2)}, u32[]{:S(2)}) collective-permute-start(bf16[768,384]{1,0:T(8,128)(2,1)S(1)} %get-tuple-element.29.refs_10_), channel_id=1, source_target_pairs={{0,16},{1,17},{2,18},{3,19},{4,20},{5,21},{6,22},{7,23},{8,24},{9,... | collective-permute-start | bytes 1769480 | tf_op jit(solution)/shard_map/ppermute | solution.py:409
  49.0 19.7 %collective-permute-start.17 = (bf16[480,768]{1,0:T(8,128)(2,1)S(1)}, bf16[480,768]{1,0:T(8,128)(2,1)S(1)}, u32[]{:S(2)}, u32[]{:S(2)}) collective-permute-start(bf16[480,768]{1,0:T(8,128)(2,1)S(1)} %get-tuple-element.32.refs_6_), channel_id=1, source_target_pairs={{4,0},{5,1},{6,2},{7,3},{8,4},{9,5},{10,6},{11,7},{12,8},{13,9},{1... | collective-permute-start | bytes 2211848 | tf_op jit(solution)/shard_map/ppermute | solution.py:409
  50.3 18.6 %collective-permute-start.16 = (bf16[480,768]{1,0:T(8,128)(2,1)S(1)}, bf16[480,768]{1,0:T(8,128)(2,1)S(1)}, u32[]{:S(2)}, u32[]{:S(2)}) collective-permute-start(bf16[480,768]{1,0:T(8,128)(2,1)S(1)} %get-tuple-element.32.refs_6_), channel_id=1, source_target_pairs={{0,4},{1,5},{2,6},{3,7},{4,8},{5,9},{6,10},{7,11},{8,12},{9,13},{1... | collective-permute-start | bytes 2211848 | tf_op jit(solution)/shard_map/ppermute | solution.py:409
  61.6 9.4 %collective-permute-start.15 = (bf16[384,384]{1,0:T(8,128)(2,1)S(1)}, bf16[384,384]{1,0:T(8,128)(2,1)S(1)}, u32[]{:S(2)}, u32[]{:S(2)}) collective-permute-start(bf16[384,384]{1,0:T(8,128)(2,1)S(1)} %get-tuple-element.31), channel_id=1, source_target_pairs={{0,16},{1,17},{2,18},{3,19},{4,20},{5,21},{6,22},{7,23},{8,24},{9,... | collective-permute-start | bytes 884744 | tf_op jit(solution)/shard_map/ppermute | solution.py:409
  76.5 18.3 %collective-permute-start.19 = (bf16[480,768]{1,0:T(8,128)(2,1)S(1)}, bf16[480,768]{1,0:T(8,128)(2,1)S(1)}, u32[]{:S(2)}, u32[]{:S(2)}) collective-permute-start(bf16[480,768]{1,0:T(8,128)(2,1)S(1)} %get-tuple-element.34.refs_2_), channel_id=1, source_target_pairs={{4,0},{5,1},{6,2},{7,3},{8,4},{9,5},{10,6},{11,7},{12,8},{13,9},{1... | collective-permute-start | bytes 2211848 | tf_op jit(solution)/shard_map/ppermute | solution.py:409
  77.8 21.9 %collective-permute-start.18 = (bf16[480,768]{1,0:T(8,128)(2,1)S(1)}, bf16[480,768]{1,0:T(8,128)(2,1)S(1)}, u32[]{:S(2)}, u32[]{:S(2)}) collective-permute-start(bf16[480,768]{1,0:T(8,128)(2,1)S(1)} %get-tuple-element.34.refs_2_), channel_id=1, source_target_pairs={{0,4},{1,5},{2,6},{3,7},{4,8},{5,9},{6,10},{7,11},{8,12},{9,13},{1... | collective-permute-start | bytes 2211848 | tf_op jit(solution)/shard_map/ppermute | solution.py:409
  82.9 26.2 %collective-permute-start.20 = (bf16[368,768]{1,0:T(8,128)(2,1)S(1)}, bf16[368,768]{1,0:T(8,128)(2,1)S(1)}, u32[]{:S(2)}, u32[]{:S(2)}) collective-permute-start(bf16[368,768]{1,0:T(8,128)(2,1)S(1)} %get-tuple-element.35), channel_id=1, source_target_pairs={{0,2},{1,3},{2,0},{3,1},{4,6},{5,7},{6,4},{7,5},{8,10},{9,11},{10,... | collective-permute-start | bytes 1695752 | tf_op jit(solution)/shard_map/ppermute | solution.py:409
  83.8 20.6 %collective-permute-start.25 = (bf16[256,768]{1,0:T(8,128)(2,1)S(1)}, bf16[256,768]{1,0:T(8,128)(2,1)S(1)}, u32[]{:S(2)}, u32[]{:S(2)}) collective-permute-start(bf16[256,768]{1,0:T(8,128)(2,1)S(1)} %get-tuple-element.41), channel_id=1, source_target_pairs={{0,4},{1,5},{2,6},{3,7},{4,8},{5,9},{6,10},{7,11},{8,12},{9,13},{1... | collective-permute-start | bytes 1179656 | tf_op jit(solution)/shard_map/ppermute | solution.py:409
  87.7 31.5 %collective-permute-start.24 = (bf16[368,768]{1,0:T(8,128)(2,1)S(1)}, bf16[368,768]{1,0:T(8,128)(2,1)S(1)}, u32[]{:S(2)}, u32[]{:S(2)}) collective-permute-start(bf16[368,768]{1,0:T(8,128)(2,1)S(1)} %get-tuple-element.33.refs_14_), channel_id=1, source_target_pairs={{0,2},{1,3},{2,0},{3,1},{4,6},{5,7},{6,4},{7,5},{8,10},{9,11},{10,... | collective-permute-start | bytes 1695752 | tf_op jit(solution)/shard_map/ppermute | solution.py:409
  101.8 19.5 %collective-permute-start.21 = (bf16[368,768]{1,0:T(8,128)(2,1)S(1)}, bf16[368,768]{1,0:T(8,128)(2,1)S(1)}, u32[]{:S(2)}, u32[]{:S(2)}) collective-permute-start(bf16[368,768]{1,0:T(8,128)(2,1)S(1)} %get-tuple-element.36.refs_10_), channel_id=1, source_target_pairs={{0,2},{1,3},{2,0},{3,1},{4,6},{5,7},{6,4},{7,5},{8,10},{9,11},{10,... | collective-permute-start | bytes 1695752 | tf_op jit(solution)/shard_map/ppermute | solution.py:409
  102.7 16.4 %collective-permute-start.26 = (bf16[256,768]{1,0:T(8,128)(2,1)S(1)}, bf16[256,768]{1,0:T(8,128)(2,1)S(1)}, u32[]{:S(2)}, u32[]{:S(2)}) collective-permute-start(bf16[256,768]{1,0:T(8,128)(2,1)S(1)} %get-tuple-element.42), channel_id=1, source_target_pairs={{4,0},{5,1},{6,2},{7,3},{8,4},{9,5},{10,6},{11,7},{12,8},{13,9},{1... | collective-permute-start | bytes 1179656 | tf_op jit(solution)/shard_map/ppermute | solution.py:409
  104.4 14.8 %collective-permute-start.22 = (bf16[256,768]{1,0:T(8,128)(2,1)S(1)}, bf16[256,768]{1,0:T(8,128)(2,1)S(1)}, u32[]{:S(2)}, u32[]{:S(2)}) collective-permute-start(bf16[256,768]{1,0:T(8,128)(2,1)S(1)} %get-tuple-element.39), channel_id=1, source_target_pairs={{0,4},{1,5},{2,6},{3,7},{4,8},{5,9},{6,10},{7,11},{8,12},{9,13},{1... | collective-permute-start | bytes 1179656 | tf_op jit(solution)/shard_map/ppermute | solution.py:409
  109.1 12.2 %collective-permute-start.23 = (bf16[256,768]{1,0:T(8,128)(2,1)S(1)}, bf16[256,768]{1,0:T(8,128)(2,1)S(1)}, u32[]{:S(2)}, u32[]{:S(2)}) collective-permute-start(bf16[256,768]{1,0:T(8,128)(2,1)S(1)} %get-tuple-element.40), channel_id=1, source_target_pairs={{4,0},{5,1},{6,2},{7,3},{8,4},{9,5},{10,6},{11,7},{12,8},{13,9},{1... | collective-permute-start | bytes 1179656 | tf_op jit(solution)/shard_map/ppermute | solution.py:409
  (13 other events, 150.4 us)

commit v4 on v3

--- a/solution.py
+++ b/solution.py
@@ -16,7 +16,6 @@
 VMEM = pl.BlockSpec(memory_space=pltpu.VMEM)
 SMEM = pl.BlockSpec(memory_space=pltpu.SMEM)
 ANY = pl.BlockSpec(memory_space=pl.ANY)
-HBM = pl.BlockSpec(memory_space=pltpu.HBM)
 SMALL = pl.CostEstimate(flops=1, bytes_accessed=1, transcendentals=0)
 
 
@@ -69,52 +68,42 @@
     return lax.axis_index("group") % 2, tm // 4, tm // 2 % 2, tm % 2
 
 
-def run_all(copies):
-    for copy in copies:
-        copy.start()
-    for copy in copies:
-        copy.wait()
-
-
-def copy_rows(moves, sems):
-    run_all([
-        pltpu.make_async_copy(
-            source.at[pl.ds(at, count)], target.at[pl.ds(to, count)], sems.at[i]
-        )
-        for i, (source, at, count, target, to) in enumerate(moves)
-    ])
-
-
-def pack_kernel(hidden, values, queries, positions, out, sems):
-    model, width = hidden.shape[1], values.shape[1] // 2
+def copy_rows(moves):
+    for source, at, count, target, to in moves:
+        target[pl.ds(to, count), :] = source[pl.ds(at, count), :]
+
+
+def pack_kernel(values, queries, positions, out):
+    width = values.shape[1] // 2
     _, _, _, c = place_of()
     theirs = pl.ds(pl.multiple_of((1 - c) * width, BLOCK), width)
-    run_all([
-        pltpu.make_async_copy(hidden, out.at[:, pl.ds(0, model)], sems.at[0]),
-        pltpu.make_async_copy(values.at[:, theirs], out.at[:, pl.ds(model, width)], sems.at[1]),
-        pltpu.make_async_copy(queries.at[:, theirs], out.at[:, pl.ds(model + width, width)], sems.at[2]),
-        pltpu.make_async_copy(positions, out.at[:, pl.ds(model + 2 * width, BLOCK)], sems.at[3]),
-    ])
-
-
-def pair_of(own, packed, width):
+    out[:, :width] = values[:, theirs]
+    out[:, width : 2 * width] = queries[:, theirs]
+    out[:, 2 * width :] = positions[...]
+
+
+def pair_of(own, packed, part, width):
     _, _, _, c = place_of()
-    model = packed.shape[1] - BLOCK - 2 * width
-    return own.at[:, pl.ds(pl.multiple_of(c * width, BLOCK), width)], packed.at[:, pl.ds(model, width)]
+    mine = own.at[:, pl.ds(pl.multiple_of(c * width, BLOCK), width)]
+    return mine, packed.at[:, part * width : (part + 1) * width]
+
+
+def starts(rows):
+    _, _, _, c = place_of()
+    return pl.multiple_of(c * rows, 16), pl.multiple_of((1 - c) * rows, 16)
 
 
 def join_kernel(values, positions, packed, *refs):
-    units, (joined, both, places, sems) = refs[:-4], refs[-4:]
+    units, (joined, both, places) = refs[:-3], refs[-3:]
     rows, width = values.shape[0], both.shape[1]
     size = units[0].shape[0]
-    _, _, _, c = place_of()
-    own, mate = pair_of(values, packed, width)
-    last = packed.at[:, pl.ds(packed.shape[1] - BLOCK, BLOCK)]
-    first_at, second_at = pl.multiple_of(c * rows, 16), pl.multiple_of((1 - c) * rows, 16)
+    own, mate = pair_of(values, packed, 0, width)
+    last = packed.at[:, 2 * width :]
+    first_at, second_at = starts(rows)
     moves = [(unit, 0, size, joined, k * size) for k, unit in enumerate(units)]
     moves += [(own, 0, rows, both, first_at), (mate, 0, rows, both, second_at)]
     moves += [(positions, 0, rows, places, first_at), (last, 0, rows, places, second_at)]
-    copy_rows(moves, sems)
+    copy_rows(moves)
 
 
 def take_inner(kept, y, both, inner):
@@ -127,25 +116,24 @@
     inner[rows:, :] = both[pl.ds(pl.multiple_of(block, 16), BLOCK), :]
 
 
-def inner_kernel(kept, values, packed, inner, sems):
+def inner_kernel(kept, values, packed, inner):
     rows, width = values.shape[0], inner.shape[1]
     _, _, y, c = place_of()
-    own, mate = pair_of(values, packed, width)
+    own, mate = pair_of(values, packed, 0, width)
     middle = kept.shape[0] // 2
     j = jnp.where(y == 0, kept[middle - 2], kept[middle + 2])
     block = pl.multiple_of(j * (rows - BLOCK), 16)
 
     @pl.when(c == 1 - y)
     def _():
-        copy_rows([(own, 0, rows, inner, 0), (mate, block, BLOCK, inner, rows)], sems)
+        copy_rows([(own, 0, rows, inner, 0), (mate, block, BLOCK, inner, rows)])
 
     @pl.when(c == y)
     def _():
-        copy_rows([(mate, 0, rows, inner, 0), (own, block, BLOCK, inner, rows)], sems)
-
-
-def onward_kernel(forward, kept, below, above, *refs):
-    outs, sems = refs[:-1], refs[-1]
+        copy_rows([(mate, 0, rows, inner, 0), (own, block, BLOCK, inner, rows)])
+
+
+def onward_kernel(forward, kept, below, above, *outs):
     rows = below.shape[0] // 2
     shift = rows - BLOCK
     middle = kept.shape[0] // 2
@@ -154,94 +142,71 @@
     def start(j, frame):
         return pl.multiple_of(frame * rows + j * shift, 16)
 
-    moves = []
     if forward:
         for out, source, j in ((outs[0], below, kept[middle - 8]), (outs[1], above, kept[middle + 8])):
-            moves += [(source, start(j, f), BLOCK, out, f * BLOCK) for f in range(2)]
+            copy_rows([(source, start(j, f), BLOCK, out, f * BLOCK) for f in range(2)])
     to = outs[-1]
-    up = [(below, rows, rows, to, 0), (below, start(kept[middle - 2], 0), BLOCK, to, rows)]
-    down = [(above, 0, rows, to, 0), (above, start(kept[middle + 2], 1), BLOCK, to, rows)]
 
     @pl.when(y == 1)
     def _():
-        copy_rows(moves + up, sems)
+        copy_rows([(below, rows, rows, to, 0), (below, start(kept[middle - 2], 0), BLOCK, to, rows)])
 
     @pl.when(y == 0)
     def _():
-        copy_rows(moves + down, sems)
+        copy_rows([(above, 0, rows, to, 0), (above, start(kept[middle + 2], 1), BLOCK, to, rows)])
 
 
 def rows_kernel(plan, *refs):
-    sems = refs[-1]
-    copy_rows([(refs[a], at, n, refs[b], to) for a, at, n, b, to in plan], sems)
-
-
-def query_kernel(queries, packed, gain, positions, lanes, out, cosine, sine, held, sems):
-    rows, width = queries.shape[0], held.shape[1]
+    copy_rows([(refs[a], at, n, refs[b], to) for a, at, n, b, to in plan])
+
+
+def query_kernel(queries, packed, gain, positions, lanes, out, cosine, sine):
+    rows, width = queries.shape[0], out.shape[1]
     head_dim = gain.shape[1]
-    model = packed.shape[1] - BLOCK - 2 * width
-    _, _, _, c = place_of()
-    own = queries.at[:, pl.ds(pl.multiple_of(c * width, BLOCK), width)]
-    mate = packed.at[:, pl.ds(model + width, width)]
-    first_at, second_at = pl.multiple_of(c * rows, 16), pl.multiple_of((1 - c) * rows, 16)
-    copy_rows([(own, 0, rows, held, first_at), (mate, 0, rows, held, second_at)], sems)
     time, row, col = (positions[:, i : i + 1].astype(jnp.float32) for i in range(3))
     axis = lanes[1:2, :]
     angle = jnp.where(axis == 0.0, time, jnp.where(axis == 1.0, row, col)) * lanes[0:1, :]
     cosine[...] = jnp.cos(angle)
     sine[...] = jnp.sin(angle) * lanes[2:3, :]
-    for h in range(width // head_dim):
-        cols = slice(h * head_dim, (h + 1) * head_dim)
-        u = held[:, cols].astype(jnp.float32)
-        out[:, cols] = norm_rotate(u, gain[...], cosine[...], sine[...]).astype(out.dtype)
-
-
-def key_kernel(sources, n_pieces, kept, own, packed, gain, cosine, sine, *refs):
-    pieces, (out, hidden, weight, sems) = refs[:n_pieces], refs[-4:]
-    x, z, y, c = place_of()
+    for source, at in zip(pair_of(queries, packed, 1, width), starts(rows)):
+        held = source[...]
+        here = pl.ds(at, rows)
+        cos_t, sin_t = cosine[here, :], sine[here, :]
+        for h in range(width // head_dim):
+            cols = slice(h * head_dim, (h + 1) * head_dim)
+            u = held[:, cols].astype(jnp.float32)
+            out[here, cols] = norm_rotate(u, gain[...], cos_t, sin_t).astype(out.dtype)
+
+
+def key_kernel(sources, n_pieces, kept, own, mate, gain, cosine, sine, *refs):
+    pieces, (out, weight) = refs[:n_pieces], refs[-2:]
+    x, z, y, _ = place_of()
     rows, model = own.shape
     head_dim = gain.shape[1]
     span = sum(source[5] for source in sources if source[2] == 0 and source[3] == 0)
     depth = model // (2 * span)
-    mate = packed.at[:, pl.ds(0, model)]
-    copies = []
-    for i, (source, slot) in enumerate(((own, c), (mate, 1 - c))):
-        at = pl.ds(pl.multiple_of(slot * rows, 16), rows)
-        copies.append(pltpu.make_async_copy(source, hidden.at[at], sems.at[i]))
-    for i, (piece, first, below, other_y, to, count) in enumerate(sources):
+    for piece, first, below, other_y, to, count in sources:
         pair = lax.rem(z + depth - below, depth) * 2 + (1 - y if other_y else y)
-        at = pl.ds(pl.multiple_of(pair * span + to, 16), count)
-        copies.append(
-            pltpu.make_async_copy(pieces[piece].at[pl.ds(first, count)], weight.at[at], sems.at[2 + i])
-        )
-    run_all(copies)
-    raw = jnp.dot(hidden[...], weight[...], preferred_element_type=jnp.float32)
-    for h in range(weight.shape[1] // head_dim):
-        cols = slice(h * head_dim, (h + 1) * head_dim)
-        out[:, cols] = norm_rotate(raw[:, cols], gain[...], cosine[...], sine[...]).astype(out.dtype)
-    if len(refs) > n_pieces + 4:
+        copy_rows([(pieces[piece], first, count, weight, pl.multiple_of(pair * span + to, 16))])
+    for source, at in zip((own, mate), starts(rows)):
+        raw = jnp.dot(source[...], weight[...], preferred_element_type=jnp.float32)
+        here = pl.ds(at, rows)
+        cos_t, sin_t = cosine[here, :], sine[here, :]
+        for h in range(weight.shape[1] // head_dim):
+            cols = slice(h * head_dim, (h + 1) * head_dim)
+            out[here, cols] = norm_rotate(raw[:, cols], gain[...], cos_t, sin_t).astype(out.dtype)
+    if len(refs) > n_pieces + 2:
         first, both, inner = refs[n_pieces : n_pieces + 3]
         width = out.shape[1]
-        run_all([
-            pltpu.make_async_copy(
-                half, both.at[:, pl.ds(pl.multiple_of(at * width, BLOCK), width)], sems.at[i]
-            )
-            for i, (half, at) in enumerate(((first, x), (out, 1 - x)))
-        ])
+        for half, at in ((first, x), (out, 1 - x)):
+            both[:, pl.ds(pl.multiple_of(at * width, BLOCK), width)] = half[...]
         take_inner(kept, y, both, inner)
 
 
-def gather(copies, dest, used, sems, kind):
-    made = []
-    for i, (piece, row, count, at) in enumerate(copies):
-        copy = pltpu.make_async_copy(
-            piece.at[pl.ds(row, count)], dest.at[pl.ds(at, count)], sems.at[kind, i]
-        )
-        copy.start()
-        made.append(copy)
+def gather(copies, dest, used):
+    copy_rows([(piece, row, count, dest, at) for piece, row, count, at in copies])
     if used < dest.shape[0]:
         dest[used:, :] = jnp.zeros((dest.shape[0] - used, dest.shape[1]), dest.dtype)
-    return made
 
 
 def key_mask(runs, total, overlap):
@@ -256,31 +221,23 @@
 
 def attend(query, at, keys, vals, mask):
     head_dim = BLOCK
-    heads = range(query.shape[1] // head_dim)
     scale = jnp.float32(head_dim ** (-0.5) * np.log2(np.e))
-    cols = [slice(h * head_dim, (h + 1) * head_dim) for h in heads]
-
-    def scores(h):
-        return lax.dot_general(
-            query[at, cols[h]],
-            keys[:, cols[h]],
-            (((1,), (1,)), ((), ())),
-            preferred_element_type=jnp.float32,
+    for h in range(query.shape[1] // head_dim):
+        cols = slice(h * head_dim, (h + 1) * head_dim)
+        scores = lax.dot_general(
+            query[at, cols], keys[:, cols], (((1,), (1,)), ((), ())), preferred_element_type=jnp.float32
         )
-
-    ahead = scores(0)
-    for h in heads:
-        now, ahead = ahead, scores(h + 1) if h + 1 in heads else None
-        weights = jnp.exp2(now * scale) * mask
+        weights = jnp.exp2(scores * scale) * mask
         total = jnp.sum(weights, axis=1, keepdims=True)
-        yield cols[h], jnp.dot(
-            weights.astype(jnp.bfloat16), vals[:, cols[h]], preferred_element_type=jnp.float32
-        ), total
+        part = jnp.dot(
+            weights.astype(jnp.bfloat16), vals[:, cols], preferred_element_type=jnp.float32
+        )
+        yield cols, part, total
 
 
 def attend_early_kernel(depth, kept, query, *refs):
     keys, vals = refs[:4], refs[4:8]
-    sums, weights, key_0, val_0, key_1, val_1, sems = refs[8:]
+    sums, weights, key_0, val_0, key_1, val_1 = refs[8:]
     rows = query.shape[0] // 2
     _, z, y, _ = place_of()
     middle = kept.shape[0] // 2
@@ -306,17 +263,14 @@
 
     work = []
     for i, (frame, key_all, val_all) in enumerate(((near, key_0, val_0), (other, key_1, val_1))):
-        made = []
-        for kind, (pieces, dest) in enumerate(((keys, key_all), (vals, val_all))):
+        for pieces, dest in ((keys, key_all), (vals, val_all)):
             copies, used = plan(pieces, frame, i == 0)
-            made += gather(copies, dest, used, sems.at[i], kind)
+            gather(copies, dest, used)
         runs = [(2 * rows, None, 1)] + ([(rows, None, 1)] if i == 0 else [])
         runs += [(BLOCK, inner_j, 1), (BLOCK, low_j, low_ok), (BLOCK, high_j, high_ok)]
-        work.append((frame, key_all, val_all, made, key_mask(runs, key_all.shape[0], 2 * BLOCK - rows)))
+        work.append((frame, key_all, val_all, key_mask(runs, key_all.shape[0], 2 * BLOCK - rows)))
     lane = lax.broadcasted_iota(jnp.int32, (1, weights.shape[2]), 1)
-    for frame, key_all, val_all, made, mask in work:
-        for copy in made:
-            copy.wait()
+    for frame, key_all, val_all, mask in work:
         at = pl.ds(pl.multiple_of(frame * rows, 16), rows)
         found = jnp.zeros((rows, weights.shape[2]), jnp.float32)
         for h, (cols, part, total) in enumerate(attend(query, at, key_all, val_all, mask)):
@@ -328,7 +282,7 @@
 def attend_late_kernel(far, kept, query, sums, weights, *refs):
     per = 1 + 2 * (far - 1)
     keys, vals = refs[:per], refs[per : 2 * per]
-    keep, send, result, key_0, val_0, key_1, val_1, sems = refs[2 * per :]
+    keep, send, key_0, val_0, key_1, val_1, result = refs[2 * per :]
     rows = query.shape[0] // 2
     depth = 1 << far
     _, z, y, c = place_of()
@@ -347,50 +301,29 @@
 
     work = []
     for i, (frame, key_all, val_all) in enumerate(((near, key_0, val_0), (other, key_1, val_1))):
-        made, lasts = [], []
         first = rows + BLOCK if i == 0 else BLOCK
         used = first + BLOCK * len(runs_far)
-        for kind, (pieces, dest) in enumerate(((keys, key_all), (vals, val_all))):
+        for pieces, dest in ((keys, key_all), (vals, val_all)):
             row = 0 if i == 0 else pl.multiple_of(crossing_j * (rows - BLOCK), 16)
+            at_frame = pl.multiple_of(frame * BLOCK, BLOCK)
             copies = [(pieces[0], row, first, 0)]
             for k in range(2 * (far - 2)):
-                copies.append((pieces[1 + k], pl.multiple_of(frame * BLOCK, BLOCK), BLOCK, first + k * BLOCK))
-            made += gather(copies, dest, used, sems.at[i], kind)
-            for piece, taken in ((pieces[-2], use_below), (pieces[-1], jnp.logical_not(use_below))):
-                copy = pltpu.make_async_copy(
-                    piece.at[pl.ds(pl.multiple_of(frame * BLOCK, BLOCK), BLOCK)],
-                    dest.at[pl.ds(used - BLOCK, BLOCK)],
-                    sems.at[i, kind, len(copies)],
-                )
-                lasts.append((copy, taken))
-        for copy, taken in lasts:
-
-            @pl.when(taken)
-            def _():
-                copy.start()
-
+                copies.append((pieces[1 + k], at_frame, BLOCK, first + k * BLOCK))
+            gather(copies, dest, used)
+            here = pl.ds(at_frame, BLOCK)
+            dest[used - BLOCK : used, :] = jnp.where(use_below, pieces[-2][here, :], pieces[-1][here, :])
         runs = [(rows, None, crossing_ok)] if i == 0 else []
         runs += [(BLOCK, crossing_j, crossing_ok)] + runs_far
         mask = key_mask(runs, key_all.shape[0], 2 * BLOCK - rows)
-        work.append((frame, key_all, val_all, made, lasts, mask))
-    for frame, key_all, val_all, made, lasts, mask in work:
-        for copy in made:
-            copy.wait()
-        for copy, taken in lasts:
-
-            @pl.when(taken)
-            def _():
-                copy.wait()
-
+        work.append((frame, key_all, val_all, mask))
+    for frame, key_all, val_all, mask in work:
         at = pl.ds(pl.multiple_of(frame * rows, 16), rows)
         before = weights[frame]
         for h, (cols, more, total) in enumerate(attend(query, at, key_all, val_all, mask)):
             done = (sums[frame, :, cols] + more) / (before[:, h : h + 1] + total)
             result[frame, :, cols] = done.astype(result.dtype)
-    run_all([
-        pltpu.make_async_copy(result.at[frame], out, sems.at[0, 0, i])
-        for i, (frame, out) in enumerate(((c, keep), (1 - c, send)))
-    ])
+    keep[...] = result[c]
+    send[...] = result[1 - c]
 
 
 def body(hidden, queries, values, key_weight, query_gain, key_gain, rope_positions, block_mask):
@@ -443,11 +376,8 @@
             name=name,
         )(*[array for _, array in operands], *ties)
 
-    def dma(count):
-        return pltpu.SemaphoreType.DMA((count,))
-
-    def in_place(*arrays):
-        return [(ANY, array) for array in arrays]
+    def here(*arrays):
+        return [(VMEM, array) for array in arrays]
 
     def by_core(own, mate):
         return jnp.where(c == 0, jnp.concatenate([own, mate], 0), jnp.concatenate([mate, own], 0))
@@ -470,18 +400,19 @@
     (packed,) = call(
         "pack",
         pack_kernel,
-        [(rows, model + width + BLOCK)],
-        [(HBM, hidden), (HBM, values), (HBM, queries), (HBM, positions)],
-        [dma(4)],
+        [(rows, width + BLOCK)],
+        here(values, queries, positions),
+        [],
         ties=[x_0, y_0, units[1]],
     )
-    packed = to_mate(packed)
+    packed, hidden_mate = to_mate(packed), to_mate(hidden)
     (value_inner,) = call(
         "value_inner",
         inner_kernel,
         [(rows + BLOCK, half)],
-        [kept, (HBM, values), (ANY, packed)],
-        [dma(2)],
+        [kept] + here(values, packed),
+        [],
+        ties=[hidden_mate],
     )
     value_inner = to_y(value_inner)
     rest = depth - 2
@@ -489,16 +420,16 @@
         "join",
         join_kernel,
         [(rest * size, quarter), (2 * rows, half), (2 * rows, BLOCK)],
-        [(HBM, values), (HBM, positions)] + in_place(packed, *units[2:]),
-        [dma(rest + 4)],
+        here(values, positions, packed, *units[2:]),
+        [],
         ties=[xy_0, xy_1, x_1, value_inner],
     )
     query_rot, cosine, sine = call(
         "query_rot",
         query_kernel,
         [(2 * rows, half), (2 * rows, head_dim), (2 * rows, head_dim)],
-        [(HBM, queries), (ANY, packed), (VMEM, query_gain[None]), (VMEM, positions), (VMEM, rope_rows(head_dim))],
-        [pltpu.VMEM((2 * rows, half), jnp.bfloat16), dma(2)],
+        here(queries, packed, query_gain[None], positions, rope_rows(head_dim)),
+        [],
         vmem=8,
         dtype=[jnp.bfloat16, jnp.float32, jnp.float32],
     )
@@ -512,8 +443,8 @@
             name,
             functools.partial(onward_kernel, far > 1),
             outs + [(rows + BLOCK, columns)],
-            [kept] + in_place(below, above),
-            [dma(6)],
+            [kept] + here(below, above),
+            [],
             ties=ties,
         )
         later = [to_y(onward[-1])]
@@ -533,8 +464,8 @@
         "turn_late",
         functools.partial(rows_kernel, [(0, 0, cut, 2, 0), (1, cut, cut, 3, 0)]),
         [(cut, quarter)] * 2,
-        in_place(x_rest, y_rest),
-        [dma(2)],
+        here(x_rest, y_rest),
+        [],
         ties=[query_rot],
     )
     turned = late_low
@@ -555,14 +486,10 @@
             name,
             functools.partial(key_kernel, sources, len(pieces)),
             outs,
-            [kept, (HBM, hidden), (ANY, packed), (VMEM, key_gain[None]), (VMEM, cosine), (VMEM, sine)]
-            + in_place(*pieces) + [(VMEM, array) for array in extra],
+            [kept]
+            + here(hidden, hidden_mate, key_gain[None], cosine, sine, *pieces, *extra),
             ([pltpu.VMEM((2 * rows, quarter), jnp.bfloat16)] if extra else [])
-            + [
-                pltpu.VMEM((2 * rows, model), jnp.bfloat16),
-                pltpu.VMEM((model, quarter), jnp.bfloat16),
-                dma(2 + len(sources)),
-            ],
+            + [pltpu.VMEM((model, quarter), jnp.bfloat16)],
             ties=ties,
             vmem=12,
         )
@@ -592,8 +519,8 @@
         "attend_early",
         functools.partial(attend_early_kernel, depth),
         [(2, rows, half), (2, rows, BLOCK)],
-        [kept, (VMEM, query_rot)] + in_place(*key_parts, key_inner, *value_parts, value_inner),
-        gathered(3 * rows + 3 * BLOCK, 2 * rows + 3 * BLOCK) + [pltpu.SemaphoreType.DMA((2, 2, 4))],
+        [kept, (VMEM, query_rot)] + here(*key_parts, key_inner, *value_parts, value_inner),
+        gathered(3 * rows + 3 * BLOCK, 2 * rows + 3 * BLOCK),
         ties=[key_onward],
         vmem=16,
         dtype=jnp.float32,
@@ -603,10 +530,9 @@
         "attend_late",
         functools.partial(attend_late_kernel, far),
         [(rows, half)] * 2,
-        [kept, (VMEM, query_rot), (VMEM, sums), (VMEM, weights)] + in_place(*key_later, *value_later),
-        [pltpu.VMEM((2, rows, half), jnp.bfloat16)]
-        + gathered(rows + (1 + n_far) * BLOCK, (1 + n_far) * BLOCK)
-        + [pltpu.SemaphoreType.DMA((2, 2, 1 + n_far))],
+        [kept, (VMEM, query_rot), (VMEM, sums), (VMEM, weights)] + here(*key_later, *value_later),
+        gathered(rows + (1 + n_far) * BLOCK, (1 + n_far) * BLOCK)
+        + [pltpu.VMEM((2, rows, half), jnp.bfloat16)],
         vmem=12,
     )
     other = to_mate(other)

time: 131 us -> 121 us (0.924)
  Pallas kernels: 33.6 us -> 20.8 us
  waiting for transfers between devices: 44.5 us -> 49.1 us
  local copies, waits for them, and re-layouts: 3.8 us -> 2.36 us
    pallas_call x11, Pallas kernels: 33.6 us -> 20.8 us  [call(): pl.pallas_call(run, out_shape=[jax.ShapeDtypeStruct(shape, dtype[i] if is...]
    ppermute x28 -> x29, waiting for transfers between devices: 44.5 us -> 49.1 us  [send(): return lax.ppermute(array, BOTH, routes(groups, n, where))]
    unnamed x18 -> x16, local copies, waits for them, and re-layouts: 2.53 us -> 1.16 us
    ppermute x28 -> x29, starting transfers between devices: 46.2 us -> 46 us  [send(): return lax.ppermute(array, BOTH, routes(groups, n, where))]
  transfers between devices with their start and end apart: 28 -> 29, of which waited for: 17 -> 19; matrix products, arithmetic and copies ran while one was open for 1% -> 2% of each run, Pallas kernels for 16% -> 11%
where the time goes in v4:
time: 121 us; the launch traced here: 120 us
  waiting for transfers between devices  49.1 us (41%)
  starting transfers between devices  46 us (38%)
  Pallas kernels  20.8 us (17%)
  local copies, waits for them, and re-layouts  2.36 us (2%)
  other arithmetic  1.81 us (1%)
    ppermute x29, waiting for transfers between devices, send(): return lax.ppermute(array, BOTH, routes(groups, n, where))  49.1 us
    ppermute x29, starting transfers between devices, send(): return lax.ppermute(array, BOTH, routes(groups, n, where))  46 us
    pallas_call x11, Pallas kernels, call(): pl.pallas_call(run, out_shape=[jax.ShapeDtypeStruct(shape, dtype[i] if is...  20.8 us
  transfers between devices with their start and end apart: 29, of which 19 were waited for; matrix products, arithmetic and copies ran while one was open for 2% of the time, Pallas kernels for 11%

profile of v4, /device:TPU:0, one launch (start us, length us, event | category | flops | bytes accessed | tf_op | source)
XLA Modules:
  0.0 120.4 jit_solution(16358025859600996847)
XLA Ops:
  1.7 1.9 %collective-permute-done = bf16[192,384]{1,0:T(8,128)(2,1)S(1)} collective-permute-done((bf16[192,384]{1,0:T(8,128)(2,1)S(1)}, bf16[192,384]{1,0:T(8,128)(2,1)S(1)}, u32[]{:S(2)}, u32[]{:S(2)}) %collective-permute-start) | collective-permute-done | bytes 147488 | tf_op jit(solution)/shard_map/ppermute | solution.py:342
  3.7 3.0 %collective-permute-start.3 = (bf16[384,384]{1,0:T(8,128)(2,1)S(1)}, bf16[384,384]{1,0:T(8,128)(2,1)S(1)}, u32[]{:S(2)}, u32[]{:S(2)}) collective-permute-start(bf16[384,384]{1,0:T(8,128)(2,1)S(1)} %maximum_select_fusion.1.refs_6_), channel_id=1, source_target_pairs={{0,4},{1,5},{2,6},{3,7},{4,8},{5,9},{6,10},{7,11},{8,12},{9,13},{1... | collective-permute-start | bytes 884744 | tf_op jit(solution)/shard_map/ppermute | solution.py:342
  6.6 1.5 %collective-permute-start.2 = (bf16[384,384]{1,0:T(8,128)(2,1)S(1)}, bf16[384,384]{1,0:T(8,128)(2,1)S(1)}, u32[]{:S(2)}, u32[]{:S(2)}) collective-permute-start(bf16[384,384]{1,0:T(8,128)(2,1)S(1)} %maximum_select_fusion.1.refs_6_), channel_id=1, source_target_pairs={{0,2},{1,3},{2,0},{3,1},{4,6},{5,7},{6,4},{7,5},{8,10},{9,11},{10,... | collective-permute-start | bytes 884744 | tf_op jit(solution)/shard_map/ppermute | solution.py:342
  10.6 5.4 %collective-permute-done.3.refs_5_.refs_8_ = bf16[384,384]{1,0:T(8,128)(2,1)S(1)} collective-permute-done((bf16[384,384]{1,0:T(8,128)(2,1)S(1)}, bf16[384,384]{1,0:T(8,128)(2,1)S(1)}, u32[]{:S(2)}, u32[]{:S(2)}) %collective-permute-start.3) | collective-permute-done | bytes 294944 | tf_op jit(solution)/shard_map/ppermute | solution.py:342
  24.4 3.4 %collective-permute-done.8.refs_9_ = bf16[384,384]{1,0:T(8,128)(2,1)S(1)} collective-permute-done((bf16[384,384]{1,0:T(8,128)(2,1)S(1)}, bf16[384,384]{1,0:T(8,128)(2,1)S(1)}, u32[]{:S(2)}, u32[]{:S(2)}) %collective-permute-start.8) | collective-permute-done | bytes 294944 | tf_op jit(solution)/shard_map/ppermute | solution.py:342
  32.3 6.3 %collective-permute-done.7.refs_5_.refs_9_ = bf16[384,384]{1,0:T(8,128)(2,1)S(1)} collective-permute-done((bf16[384,384]{1,0:T(8,128)(2,1)S(1)}, bf16[384,384]{1,0:T(8,128)(2,1)S(1)}, u32[]{:S(2)}, u32[]{:S(2)}) %collective-permute-start.7) | collective-permute-done | bytes 294944 | tf_op jit(solution)/shard_map/ppermute | solution.py:342
  38.6 4.9 %collective-permute-done.9.refs_6_.refs_10_ = bf16[384,384]{1,0:T(8,128)(2,1)S(1)} collective-permute-done((bf16[384,384]{1,0:T(8,128)(2,1)S(1)}, bf16[384,384]{1,0:T(8,128)(2,1)S(1)}, u32[]{:S(2)}, u32[]{:S(2)}) %collective-permute-start.9) | collective-permute-done | bytes 294944 | tf_op jit(solution)/shard_map/ppermute | solution.py:342
  44.6 1.5 %collective-permute-start.13 = (bf16[768,384]{1,0:T(8,128)(2,1)S(1)}, bf16[768,384]{1,0:T(8,128)(2,1)S(1)}, u32[]{:S(2)}, u32[]{:S(2)}) collective-permute-start(bf16[768,384]{1,0:T(8,128)(2,1)S(1)} %get-tuple-element.29.refs_10_), channel_id=1, source_target_pairs={{0,16},{1,17},{2,18},{3,19},{4,20},{5,21},{6,22},{7,23},{8,24},{9,... | collective-permute-start | bytes 1769480 | tf_op jit(solution)/shard_map/ppermute | solution.py:342
  47.3 4.6 %collective-permute-start.17 = (bf16[480,768]{1,0:T(8,128)(2,1)S(1)}, bf16[480,768]{1,0:T(8,128)(2,1)S(1)}, u32[]{:S(2)}, u32[]{:S(2)}) collective-permute-start(bf16[480,768]{1,0:T(8,128)(2,1)S(1)} %get-tuple-element.32.refs_6_), channel_id=1, source_target_pairs={{0,4},{1,5},{2,6},{3,7},{4,8},{5,9},{6,10},{7,11},{8,12},{9,13},{1... | collective-permute-start | bytes 2211848 | tf_op jit(solution)/shard_map/ppermute | solution.py:342
  52.0 3.8 %query_rot.1 = (bf16[480,768]{1,0:T(8,128)(2,1)S(1)}, f32[480,128]{1,0:T(8,128)S(1)}, f32[480,128]{1,0:T(8,128)S(1)}) custom-call(bf16[240,1536]{1,0:T(8,128)(2,1)S(1)} %copy-done.3, bf16[240,1664]{1,0:T(8,128)(2,1)S(1)} %collective-permute-done.4.refs_2_.refs_1_, f32[1,128]{1,0:T(1,128)S(1)} %bitcast.7, bf16[480,128]{1,0:T(8,128)(2,1)S(1)} %get-tuple-element.25.refs_3_, ...), custom_call_target="tpu_custom_call" | custom-call | flops 1 | bytes 1 | tf_op jit(solution)/shard_map/query_rot/pallas_call | solution.py:365
  55.8 1.9 %collective-permute-done.14.refs_1_.refs_11_ = bf16[768,384]{1,0:T(8,128)(2,1)S(1)} collective-permute-done((bf16[768,384]{1,0:T(8,128)(2,1)S(1)}, bf16[768,384]{1,0:T(8,128)(2,1)S(1)}, u32[]{:S(2)}, u32[]{:S(2)}) %collective-permute-start.14) | collective-permute-done | bytes 589856 | tf_op jit(solution)/shard_map/ppermute | solution.py:342
  58.6 1.6 %collective-permute-start.16 = (bf16[384,384]{1,0:T(8,128)(2,1)S(1)}, bf16[384,384]{1,0:T(8,128)(2,1)S(1)}, u32[]{:S(2)}, u32[]{:S(2)}) collective-permute-start(bf16[384,384]{1,0:T(8,128)(2,1)S(1)} %get-tuple-element.31), channel_id=1, source_target_pairs={{0,16},{1,17},{2,18},{3,19},{4,20},{5,21},{6,22},{7,23},{8,24},{9,... | collective-permute-start | bytes 884744 | tf_op jit(solution)/shard_map/ppermute | solution.py:342
  61.0 3.0 %key_rot_0.1.refs_3_.refs_13_ = bf16[480,384]{1,0:T(8,128)(2,1)S(1)} custom-call(s32[31]{0:T(128)S(1)} %slice_bitcast_fusion.refs_0_, bf16[240,3072]{1,0:T(8,128)(2,1)S(1)} %copy-done.1, bf16[240,3072]{1,0:T(8,128)(2,1)S(1)} %collective-permute-done.11.refs_3_.refs_2_, f32[1,128]{1,0:T(1,128)S(1)} %bitcast.5, f32[480,128]{1,0:T(8,128)S(1)} %get-tuple-element.27.refs_4_, ...), custom_call_target="tpu_custom_call" | custom-call | flops 1 | bytes 1 | tf_op jit(solution)/shard_map/key_rot_0/pallas_call | solution.py:365
  66.8 3.1 %key_rot_1.1 = (bf16[480,768]{1,0:T(8,128)(2,1)S(1)}, bf16[368,768]{1,0:T(8,128)(2,1)S(1)}) custom-call(s32[31]{0:T(128)S(1)} %slice_bitcast_fusion.refs_0_, bf16[240,3072]{1,0:T(8,128)(2,1)S(1)} %copy-done.1, bf16[240,3072]{1,0:T(8,128)(2,1)S(1)} %collective-permute-done.11.refs_3_.refs_2_, f32[1,128]{1,0:T(1,128)S(1)} %bitcast.6, ...), custom_call_target="tpu_custom_call" | custom-call | flops 1 | bytes 1 | tf_op jit(solution)/shard_map/key_rot_1/pallas_call | solution.py:365
  71.2 4.8 %collective-permute-start.19 = (bf16[480,768]{1,0:T(8,128)(2,1)S(1)}, bf16[480,768]{1,0:T(8,128)(2,1)S(1)}, u32[]{:S(2)}, u32[]{:S(2)}) collective-permute-start(bf16[480,768]{1,0:T(8,128)(2,1)S(1)} %get-tuple-element.34.refs_2_), channel_id=1, source_target_pairs={{0,4},{1,5},{2,6},{3,7},{4,8},{5,9},{6,10},{7,11},{8,12},{9,13},{1... | collective-permute-start | bytes 2211848 | tf_op jit(solution)/shard_map/ppermute | solution.py:342
  77.0 3.9 %collective-permute-start.26 = (bf16[256,768]{1,0:T(8,128)(2,1)S(1)}, bf16[256,768]{1,0:T(8,128)(2,1)S(1)}, u32[]{:S(2)}, u32[]{:S(2)}) collective-permute-start(bf16[256,768]{1,0:T(8,128)(2,1)S(1)} %get-tuple-element.41), channel_id=1, source_target_pairs={{0,4},{1,5},{2,6},{3,7},{4,8},{5,9},{6,10},{7,11},{8,12},{9,13},{1... | collective-permute-start | bytes 1179656 | tf_op jit(solution)/shard_map/ppermute | solution.py:342
  82.1 5.9 %collective-permute-done.20.refs_2_.refs_4_ = bf16[480,768]{1,0:T(8,128)(2,1)S(1)} collective-permute-done((bf16[480,768]{1,0:T(8,128)(2,1)S(1)}, bf16[480,768]{1,0:T(8,128)(2,1)S(1)}, u32[]{:S(2)}, u32[]{:S(2)}) %collective-permute-start.20) | collective-permute-done | bytes 737312 | tf_op jit(solution)/shard_map/ppermute | solution.py:342
  88.0 4.9 %collective-permute-done.19.refs_1_.refs_3_ = bf16[480,768]{1,0:T(8,128)(2,1)S(1)} collective-permute-done((bf16[480,768]{1,0:T(8,128)(2,1)S(1)}, bf16[480,768]{1,0:T(8,128)(2,1)S(1)}, u32[]{:S(2)}, u32[]{:S(2)}) %collective-permute-start.19) | collective-permute-done | bytes 737312 | tf_op jit(solution)/shard_map/ppermute | solution.py:342
  95.8 1.8 %collective-permute-done.26.refs_8_ = bf16[256,768]{1,0:T(8,128)(2,1)S(1)} collective-permute-done((bf16[256,768]{1,0:T(8,128)(2,1)S(1)}, bf16[256,768]{1,0:T(8,128)(2,1)S(1)}, u32[]{:S(2)}, u32[]{:S(2)}) %collective-permute-start.26) | collective-permute-done | bytes 393248 | tf_op jit(solution)/shard_map/ppermute | solution.py:342
  97.6 4.6 %collective-permute-start.23 = (bf16[256,768]{1,0:T(8,128)(2,1)S(1)}, bf16[256,768]{1,0:T(8,128)(2,1)S(1)}, u32[]{:S(2)}, u32[]{:S(2)}) collective-permute-start(bf16[256,768]{1,0:T(8,128)(2,1)S(1)} %get-tuple-element.39), channel_id=1, source_target_pairs={{0,4},{1,5},{2,6},{3,7},{4,8},{5,9},{6,10},{7,11},{8,12},{9,13},{1... | collective-permute-start | bytes 1179656 | tf_op jit(solution)/shard_map/ppermute | solution.py:342
  103.5 4.4 %attend_early.1 = (f32[2,240,768]{2,1,0:T(8,128)S(1)}, f32[2,240,128]{2,1,0:T(8,128)S(1)}) custom-call(s32[31]{0:T(128)S(1)} %slice_bitcast_fusion.refs_0_, bf16[480,768]{1,0:T(8,128)(2,1)S(1)} %get-tuple-element.26.refs_2_.refs_1_, bf16[480,768]{1,0:T(8,128)(2,1)S(1)} %get-tuple-element.34.refs_2_, ...), custom_call_target="tpu_custom_call" | custom-call | flops 1 | bytes 1 | tf_op jit(solution)/shard_map/attend_early/pallas_call | solution.py:365
  107.9 5.2 %collective-permute-done.24.refs_6_ = bf16[256,768]{1,0:T(8,128)(2,1)S(1)} collective-permute-done((bf16[256,768]{1,0:T(8,128)(2,1)S(1)}, bf16[256,768]{1,0:T(8,128)(2,1)S(1)}, u32[]{:S(2)}, u32[]{:S(2)}) %collective-permute-start.24) | collective-permute-done | bytes 393248 | tf_op jit(solution)/shard_map/ppermute | solution.py:342
  113.1 4.5 %attend_late.1 = (bf16[240,768]{1,0:T(8,128)(2,1)S(1)}, bf16[240,768]{1,0:T(8,128)(2,1)S(1)}) custom-call(s32[31]{0:T(128)S(1)} %slice_bitcast_fusion.refs_0_, bf16[480,768]{1,0:T(8,128)(2,1)S(1)} %get-tuple-element.26.refs_2_.refs_1_, f32[2,240,768]{2,1,0:T(8,128)S(1)} %get-tuple-element.37.refs_2_, f32[2,240,128]{2,1,0:T(8,128)S(1)} %get-tuple-element.38.refs_3_, ...), custom_call_target="tpu_custom_call" | custom-call | flops 1 | bytes 1 | tf_op jit(solution)/shard_map/attend_late/pallas_call | solution.py:365
  117.7 1.7 %collective-permute-done.28 = bf16[240,768]{1,0:T(8,128)(2,1)S(1)} collective-permute-done((bf16[240,768]{1,0:T(8,128)(2,1)S(1)}, bf16[240,768]{1,0:T(8,128)(2,1)S(1)}, u32[]{:S(2)}, u32[]{:S(2)}) %collective-permute-start.28) | collective-permute-done | bytes 368672 | tf_op jit(solution)/shard_map/ppermute | solution.py:342
  (68 shorter events, 32.6 us)
Async XLA Ops:
  0.0 20.2 %collective-permute-start.11 = (bf16[240,3072]{1,0:T(8,128)(2,1)}, bf16[240,3072]{1,0:T(8,128)(2,1)S(1)}, u32[]{:S(2)}, u32[]{:S(2)}) collective-permute-start(bf16[240,3072]{1,0:T(8,128)(2,1)} %refs_1_.7), channel_id=1, source_target_pairs={{0,1},{1,0},{2,3},{3,2},{4,5},{5,4},{6,7},{7,6},{8,9},{9,8},{10,11... | collective-permute-start | bytes 4423688 | tf_op jit(solution)/shard_map/ppermute | solution.py:342
  3.7 12.3 %collective-permute-start.3 = (bf16[384,384]{1,0:T(8,128)(2,1)S(1)}, bf16[384,384]{1,0:T(8,128)(2,1)S(1)}, u32[]{:S(2)}, u32[]{:S(2)}) collective-permute-start(bf16[384,384]{1,0:T(8,128)(2,1)S(1)} %maximum_select_fusion.1.refs_6_), channel_id=1, source_target_pairs={{0,4},{1,5},{2,6},{3,7},{4,8},{5,9},{6,10},{7,11},{8,12},{9,13},{1... | collective-permute-start | bytes 884744 | tf_op jit(solution)/shard_map/ppermute | solution.py:342
  6.6 9.3 %collective-permute-start.2 = (bf16[384,384]{1,0:T(8,128)(2,1)S(1)}, bf16[384,384]{1,0:T(8,128)(2,1)S(1)}, u32[]{:S(2)}, u32[]{:S(2)}) collective-permute-start(bf16[384,384]{1,0:T(8,128)(2,1)S(1)} %maximum_select_fusion.1.refs_6_), channel_id=1, source_target_pairs={{0,2},{1,3},{2,0},{3,1},{4,6},{5,7},{6,4},{7,5},{8,10},{9,11},{10,... | collective-permute-start | bytes 884744 | tf_op jit(solution)/shard_map/ppermute | solution.py:342
  8.2 8.5 %collective-permute-start.1 = (bf16[384,384]{1,0:T(8,128)(2,1)S(1)}, bf16[384,384]{1,0:T(8,128)(2,1)S(1)}, u32[]{:S(2)}, u32[]{:S(2)}) collective-permute-start(bf16[384,384]{1,0:T(8,128)(2,1)S(1)} %maximum_select_fusion.1.refs_6_), channel_id=1, source_target_pairs={{0,16},{1,17},{2,18},{3,19},{4,20},{5,21},{6,22},{7,23},{8,24},{9,... | collective-permute-start | bytes 884744 | tf_op jit(solution)/shard_map/ppermute | solution.py:342
  17.9 9.9 %collective-permute-start.8 = (bf16[384,384]{1,0:T(8,128)(2,1)S(1)}, bf16[384,384]{1,0:T(8,128)(2,1)S(1)}, u32[]{:S(2)}, u32[]{:S(2)}) collective-permute-start(bf16[384,384]{1,0:T(8,128)(2,1)S(1)} %collective-permute-done.3.refs_5_.refs_8_), channel_id=1, source_target_pairs={{0,2},{1,3},{2,0},{3,1},{4,6},{5,7},{6,4},{7,5},{8,10},{9,11},{10,... | collective-permute-start | bytes 884744 | tf_op jit(solution)/shard_map/ppermute | solution.py:342
  18.8 10.9 %collective-permute-start.5 = (bf16[384,384]{1,0:T(8,128)(2,1)S(1)}, bf16[384,384]{1,0:T(8,128)(2,1)S(1)}, u32[]{:S(2)}, u32[]{:S(2)}) collective-permute-start(bf16[384,384]{1,0:T(8,128)(2,1)S(1)} %collective-permute-done.3.refs_5_.refs_8_), channel_id=1, source_target_pairs={{0,4},{1,5},{2,6},{3,7},{4,8},{5,9},{6,10},{7,11},{8,12},{9,13},{1... | collective-permute-start | bytes 884744 | tf_op jit(solution)/shard_map/ppermute | solution.py:342
  20.9 22.6 %collective-permute-start.12 = (bf16[368,768]{1,0:T(8,128)(2,1)S(1)}, bf16[368,768]{1,0:T(8,128)(2,1)S(1)}, u32[]{:S(2)}, u32[]{:S(2)}) collective-permute-start(bf16[368,768]{1,0:T(8,128)(2,1)S(1)} %value_inner.1), channel_id=1, source_target_pairs={{0,2},{1,3},{2,0},{3,1},{4,6},{5,7},{6,4},{7,5},{8,10},{9,11},{10,... | collective-permute-start | bytes 1695752 | tf_op jit(solution)/shard_map/ppermute | solution.py:342
  22.3 9.9 %collective-permute-start.10 = (bf16[384,384]{1,0:T(8,128)(2,1)S(1)}, bf16[384,384]{1,0:T(8,128)(2,1)S(1)}, u32[]{:S(2)}, u32[]{:S(2)}) collective-permute-start(bf16[384,384]{1,0:T(8,128)(2,1)S(1)} %collective-permute-done.3.refs_5_.refs_8_), channel_id=1, source_target_pairs={{0,16},{1,17},{2,18},{3,19},{4,20},{5,21},{6,22},{7,23},{8,24},{9,... | collective-permute-start | bytes 884744 | tf_op jit(solution)/shard_map/ppermute | solution.py:342
  23.8 14.8 %collective-permute-start.7 = (bf16[384,384]{1,0:T(8,128)(2,1)S(1)}, bf16[384,384]{1,0:T(8,128)(2,1)S(1)}, u32[]{:S(2)}, u32[]{:S(2)}) collective-permute-start(bf16[384,384]{1,0:T(8,128)(2,1)S(1)} %collective-permute-done.2.refs_4_.refs_7_), channel_id=1, source_target_pairs={{0,16},{1,17},{2,18},{3,19},{4,20},{5,21},{6,22},{7,23},{8,24},{9,... | collective-permute-start | bytes 884744 | tf_op jit(solution)/shard_map/ppermute | solution.py:342
  27.8 15.7 %collective-permute-start.9 = (bf16[384,384]{1,0:T(8,128)(2,1)S(1)}, bf16[384,384]{1,0:T(8,128)(2,1)S(1)}, u32[]{:S(2)}, u32[]{:S(2)}) collective-permute-start(bf16[384,384]{1,0:T(8,128)(2,1)S(1)} %collective-permute-done.8.refs_9_), channel_id=1, source_target_pairs={{0,16},{1,17},{2,18},{3,19},{4,20},{5,21},{6,22},{7,23},{8,24},{9,... | collective-permute-start | bytes 884744 | tf_op jit(solution)/shard_map/ppermute | solution.py:342
  29.7 13.8 %collective-permute-start.6 = (bf16[384,384]{1,0:T(8,128)(2,1)S(1)}, bf16[384,384]{1,0:T(8,128)(2,1)S(1)}, u32[]{:S(2)}, u32[]{:S(2)}) collective-permute-start(bf16[384,384]{1,0:T(8,128)(2,1)S(1)} %collective-permute-done.5.refs_3_), channel_id=1, source_target_pairs={{0,4},{1,5},{2,6},{3,7},{4,8},{5,9},{6,10},{7,11},{8,12},{9,13},{1... | collective-permute-start | bytes 884744 | tf_op jit(solution)/shard_map/ppermute | solution.py:342
  43.6 14.0 %collective-permute-start.14 = (bf16[768,384]{1,0:T(8,128)(2,1)S(1)}, bf16[768,384]{1,0:T(8,128)(2,1)S(1)}, u32[]{:S(2)}, u32[]{:S(2)}) collective-permute-start(bf16[768,384]{1,0:T(8,128)(2,1)S(1)} %get-tuple-element.29.refs_10_), channel_id=1, source_target_pairs={{0,2},{1,3},{2,0},{3,1},{4,6},{5,7},{6,4},{7,5},{8,10},{9,11},{10,... | collective-permute-start | bytes 1769480 | tf_op jit(solution)/shard_map/ppermute | solution.py:342
  44.6 13.9 %collective-permute-start.13 = (bf16[768,384]{1,0:T(8,128)(2,1)S(1)}, bf16[768,384]{1,0:T(8,128)(2,1)S(1)}, u32[]{:S(2)}, u32[]{:S(2)}) collective-permute-start(bf16[768,384]{1,0:T(8,128)(2,1)S(1)} %get-tuple-element.29.refs_10_), channel_id=1, source_target_pairs={{0,16},{1,17},{2,18},{3,19},{4,20},{5,21},{6,22},{7,23},{8,24},{9,... | collective-permute-start | bytes 1769480 | tf_op jit(solution)/shard_map/ppermute | solution.py:342
  46.1 18.7 %collective-permute-start.18 = (bf16[480,768]{1,0:T(8,128)(2,1)S(1)}, bf16[480,768]{1,0:T(8,128)(2,1)S(1)}, u32[]{:S(2)}, u32[]{:S(2)}) collective-permute-start(bf16[480,768]{1,0:T(8,128)(2,1)S(1)} %get-tuple-element.32.refs_6_), channel_id=1, source_target_pairs={{4,0},{5,1},{6,2},{7,3},{8,4},{9,5},{10,6},{11,7},{12,8},{13,9},{1... | collective-permute-start | bytes 2211848 | tf_op jit(solution)/shard_map/ppermute | solution.py:342
  47.3 18.6 %collective-permute-start.17 = (bf16[480,768]{1,0:T(8,128)(2,1)S(1)}, bf16[480,768]{1,0:T(8,128)(2,1)S(1)}, u32[]{:S(2)}, u32[]{:S(2)}) collective-permute-start(bf16[480,768]{1,0:T(8,128)(2,1)S(1)} %get-tuple-element.32.refs_6_), channel_id=1, source_target_pairs={{0,4},{1,5},{2,6},{3,7},{4,8},{5,9},{6,10},{7,11},{8,12},{9,13},{1... | collective-permute-start | bytes 2211848 | tf_op jit(solution)/shard_map/ppermute | solution.py:342
  69.9 18.1 %collective-permute-start.20 = (bf16[480,768]{1,0:T(8,128)(2,1)S(1)}, bf16[480,768]{1,0:T(8,128)(2,1)S(1)}, u32[]{:S(2)}, u32[]{:S(2)}) collective-permute-start(bf16[480,768]{1,0:T(8,128)(2,1)S(1)} %get-tuple-element.34.refs_2_), channel_id=1, source_target_pairs={{4,0},{5,1},{6,2},{7,3},{8,4},{9,5},{10,6},{11,7},{12,8},{13,9},{1... | collective-permute-start | bytes 2211848 | tf_op jit(solution)/shard_map/ppermute | solution.py:342
  71.2 21.7 %collective-permute-start.19 = (bf16[480,768]{1,0:T(8,128)(2,1)S(1)}, bf16[480,768]{1,0:T(8,128)(2,1)S(1)}, u32[]{:S(2)}, u32[]{:S(2)}) collective-permute-start(bf16[480,768]{1,0:T(8,128)(2,1)S(1)} %get-tuple-element.34.refs_2_), channel_id=1, source_target_pairs={{0,4},{1,5},{2,6},{3,7},{4,8},{5,9},{6,10},{7,11},{8,12},{9,13},{1... | collective-permute-start | bytes 2211848 | tf_op jit(solution)/shard_map/ppermute | solution.py:342
  76.1 26.1 %collective-permute-start.21 = (bf16[368,768]{1,0:T(8,128)(2,1)S(1)}, bf16[368,768]{1,0:T(8,128)(2,1)S(1)}, u32[]{:S(2)}, u32[]{:S(2)}) collective-permute-start(bf16[368,768]{1,0:T(8,128)(2,1)S(1)} %get-tuple-element.35), channel_id=1, source_target_pairs={{0,2},{1,3},{2,0},{3,1},{4,6},{5,7},{6,4},{7,5},{8,10},{9,11},{10,... | collective-permute-start | bytes 1695752 | tf_op jit(solution)/shard_map/ppermute | solution.py:342
  77.0 20.6 %collective-permute-start.26 = (bf16[256,768]{1,0:T(8,128)(2,1)S(1)}, bf16[256,768]{1,0:T(8,128)(2,1)S(1)}, u32[]{:S(2)}, u32[]{:S(2)}) collective-permute-start(bf16[256,768]{1,0:T(8,128)(2,1)S(1)} %get-tuple-element.41), channel_id=1, source_target_pairs={{0,4},{1,5},{2,6},{3,7},{4,8},{5,9},{6,10},{7,11},{8,12},{9,13},{1... | collective-permute-start | bytes 1179656 | tf_op jit(solution)/shard_map/ppermute | solution.py:342
  80.9 27.0 %collective-permute-start.25 = (bf16[368,768]{1,0:T(8,128)(2,1)S(1)}, bf16[368,768]{1,0:T(8,128)(2,1)S(1)}, u32[]{:S(2)}, u32[]{:S(2)}) collective-permute-start(bf16[368,768]{1,0:T(8,128)(2,1)S(1)} %get-tuple-element.33.refs_14_), channel_id=1, source_target_pairs={{0,2},{1,3},{2,0},{3,1},{4,6},{5,7},{6,4},{7,5},{8,10},{9,11},{10,... | collective-permute-start | bytes 1695752 | tf_op jit(solution)/shard_map/ppermute | solution.py:342
  93.6 19.5 %collective-permute-start.22 = (bf16[368,768]{1,0:T(8,128)(2,1)S(1)}, bf16[368,768]{1,0:T(8,128)(2,1)S(1)}, u32[]{:S(2)}, u32[]{:S(2)}) collective-permute-start(bf16[368,768]{1,0:T(8,128)(2,1)S(1)} %get-tuple-element.36.refs_10_), channel_id=1, source_target_pairs={{0,2},{1,3},{2,0},{3,1},{4,6},{5,7},{6,4},{7,5},{8,10},{9,11},{10,... | collective-permute-start | bytes 1695752 | tf_op jit(solution)/shard_map/ppermute | solution.py:342
  94.5 13.4 %collective-permute-start.27 = (bf16[256,768]{1,0:T(8,128)(2,1)S(1)}, bf16[256,768]{1,0:T(8,128)(2,1)S(1)}, u32[]{:S(2)}, u32[]{:S(2)}) collective-permute-start(bf16[256,768]{1,0:T(8,128)(2,1)S(1)} %get-tuple-element.42), channel_id=1, source_target_pairs={{4,0},{5,1},{6,2},{7,3},{8,4},{9,5},{10,6},{11,7},{12,8},{13,9},{1... | collective-permute-start | bytes 1179656 | tf_op jit(solution)/shard_map/ppermute | solution.py:342
  97.6 10.3 %collective-permute-start.23 = (bf16[256,768]{1,0:T(8,128)(2,1)S(1)}, bf16[256,768]{1,0:T(8,128)(2,1)S(1)}, u32[]{:S(2)}, u32[]{:S(2)}) collective-permute-start(bf16[256,768]{1,0:T(8,128)(2,1)S(1)} %get-tuple-element.39), channel_id=1, source_target_pairs={{0,4},{1,5},{2,6},{3,7},{4,8},{5,9},{6,10},{7,11},{8,12},{9,13},{1... | collective-permute-start | bytes 1179656 | tf_op jit(solution)/shard_map/ppermute | solution.py:342
  102.2 10.9 %collective-permute-start.24 = (bf16[256,768]{1,0:T(8,128)(2,1)S(1)}, bf16[256,768]{1,0:T(8,128)(2,1)S(1)}, u32[]{:S(2)}, u32[]{:S(2)}) collective-permute-start(bf16[256,768]{1,0:T(8,128)(2,1)S(1)} %get-tuple-element.40), channel_id=1, source_target_pairs={{4,0},{5,1},{6,2},{7,3},{8,4},{9,5},{10,6},{11,7},{12,8},{13,9},{1... | collective-permute-start | bytes 1179656 | tf_op jit(solution)/shard_map/ppermute | solution.py:342
  (13 other events, 159.6 us)

commit v5 on v4

--- a/solution.py
+++ b/solution.py
@@ -70,7 +70,14 @@
 
 def copy_rows(moves):
     for source, at, count, target, to in moves:
-        target[pl.ds(to, count), :] = source[pl.ds(at, count), :]
+        if not isinstance(source, tuple):
+            target[pl.ds(to, count), :] = source[pl.ds(at, count), :]
+            continue
+        x, _, _, _ = place_of()
+        width = source[0].shape[1]
+        for part, half in zip(source, (x, 1 - x)):
+            cols = pl.ds(pl.multiple_of(half * width, BLOCK), width)
+            target[pl.ds(to, count), cols] = part[pl.ds(at, count), :]
 
 
 def pack_kernel(values, queries, positions, out):
@@ -93,16 +100,14 @@
     return pl.multiple_of(c * rows, 16), pl.multiple_of((1 - c) * rows, 16)
 
 
-def join_kernel(values, positions, packed, *refs):
-    units, (joined, both, places) = refs[:-3], refs[-3:]
+def join_kernel(values, packed, *refs):
+    units, (joined, both) = refs[:-2], refs[-2:]
     rows, width = values.shape[0], both.shape[1]
     size = units[0].shape[0]
     own, mate = pair_of(values, packed, 0, width)
-    last = packed.at[:, 2 * width :]
     first_at, second_at = starts(rows)
     moves = [(unit, 0, size, joined, k * size) for k, unit in enumerate(units)]
     moves += [(own, 0, rows, both, first_at), (mate, 0, rows, both, second_at)]
-    moves += [(positions, 0, rows, places, first_at), (last, 0, rows, places, second_at)]
     copy_rows(moves)
 
 
@@ -133,45 +138,56 @@
         copy_rows([(mate, 0, rows, inner, 0), (own, block, BLOCK, inner, rows)])
 
 
-def onward_kernel(forward, kept, below, above, *outs):
-    rows = below.shape[0] // 2
+def onward_kernel(forward, halves, kept, *refs):
+    if halves:
+        rings, outs = (refs[0:2], refs[2:4]), refs[4:]
+    else:
+        rings, outs = refs[0:2], refs[2:]
+    rows = refs[0].shape[0] // 2
     shift = rows - BLOCK
     middle = kept.shape[0] // 2
-    _, _, y, _ = place_of()
+    x, _, y, _ = place_of()
 
     def start(j, frame):
         return pl.multiple_of(frame * rows + j * shift, 16)
 
-    if forward:
-        for out, source, j in ((outs[0], below, kept[middle - 8]), (outs[1], above, kept[middle + 8])):
-            copy_rows([(source, start(j, f), BLOCK, out, f * BLOCK) for f in range(2)])
     to = outs[-1]
-
-    @pl.when(y == 1)
-    def _():
-        copy_rows([(below, rows, rows, to, 0), (below, start(kept[middle - 2], 0), BLOCK, to, rows)])
-
-    @pl.when(y == 0)
-    def _():
-        copy_rows([(above, 0, rows, to, 0), (above, start(kept[middle + 2], 1), BLOCK, to, rows)])
+    for even in range(2):
+
+        @pl.when(x == 1 - even)
+        def _():
+            below, above = rings if even or not halves else rings[::-1]
+            if forward:
+                up, down = outs[:2] if even else outs[1::-1]
+                for out, source, j in ((up, below, kept[middle - 8]), (down, above, kept[middle + 8])):
+                    copy_rows([(source, start(j, f), BLOCK, out, f * BLOCK) for f in range(2)])
+
+            @pl.when(y == 1)
+            def _():
+                copy_rows([(below, rows, rows, to, 0), (below, start(kept[middle - 2], 0), BLOCK, to, rows)])
+
+            @pl.when(y == 0)
+            def _():
+                copy_rows([(above, 0, rows, to, 0), (above, start(kept[middle + 2], 1), BLOCK, to, rows)])
 
 
 def rows_kernel(plan, *refs):
     copy_rows([(refs[a], at, n, refs[b], to) for a, at, n, b, to in plan])
 
 
-def query_kernel(queries, packed, gain, positions, lanes, out, cosine, sine):
+def query_kernel(queries, packed, gain, places, lanes, out, cosine, sine):
     rows, width = queries.shape[0], out.shape[1]
     head_dim = gain.shape[1]
-    time, row, col = (positions[:, i : i + 1].astype(jnp.float32) for i in range(3))
     axis = lanes[1:2, :]
-    angle = jnp.where(axis == 0.0, time, jnp.where(axis == 1.0, row, col)) * lanes[0:1, :]
-    cosine[...] = jnp.cos(angle)
-    sine[...] = jnp.sin(angle) * lanes[2:3, :]
-    for source, at in zip(pair_of(queries, packed, 1, width), starts(rows)):
+    both_places = (places, packed.at[:, 2 * width :])
+    for source, place, at in zip(pair_of(queries, packed, 1, width), both_places, starts(rows)):
         held = source[...]
         here = pl.ds(at, rows)
-        cos_t, sin_t = cosine[here, :], sine[here, :]
+        time, row, col = (place[:, i : i + 1].astype(jnp.float32) for i in range(3))
+        angle = jnp.where(axis == 0.0, time, jnp.where(axis == 1.0, row, col)) * lanes[0:1, :]
+        cos_t, sin_t = jnp.cos(angle), jnp.sin(angle) * lanes[2:3, :]
+        cosine[here, :] = cos_t
+        sine[here, :] = sin_t
         for h in range(width // head_dim):
             cols = slice(h * head_dim, (h + 1) * head_dim)
             u = held[:, cols].astype(jnp.float32)
@@ -179,8 +195,8 @@
 
 
 def key_kernel(sources, n_pieces, kept, own, mate, gain, cosine, sine, *refs):
-    pieces, (out, weight) = refs[:n_pieces], refs[-2:]
-    x, z, y, _ = place_of()
+    pieces, (out, inner, weight) = refs[:n_pieces], refs[n_pieces:]
+    _, z, y, _ = place_of()
     rows, model = own.shape
     head_dim = gain.shape[1]
     span = sum(source[5] for source in sources if source[2] == 0 and source[3] == 0)
@@ -195,15 +211,10 @@
         for h in range(weight.shape[1] // head_dim):
             cols = slice(h * head_dim, (h + 1) * head_dim)
             out[here, cols] = norm_rotate(raw[:, cols], gain[...], cos_t, sin_t).astype(out.dtype)
-    if len(refs) > n_pieces + 2:
-        first, both, inner = refs[n_pieces : n_pieces + 3]
-        width = out.shape[1]
-        for half, at in ((first, x), (out, 1 - x)):
-            both[:, pl.ds(pl.multiple_of(at * width, BLOCK), width)] = half[...]
-        take_inner(kept, y, both, inner)
-
-
-def gather(copies, dest, used):
+    take_inner(kept, y, out, inner)
+
+
+def gather(copies, used, dest):
     copy_rows([(piece, row, count, dest, at) for piece, row, count, at in copies])
     if used < dest.shape[0]:
         dest[used:, :] = jnp.zeros((dest.shape[0] - used, dest.shape[1]), dest.dtype)
@@ -236,10 +247,10 @@
 
 
 def attend_early_kernel(depth, kept, query, *refs):
-    keys, vals = refs[:4], refs[4:8]
-    sums, weights, key_0, val_0, key_1, val_1 = refs[8:]
+    keys, vals = [refs[2 * i : 2 * i + 2] for i in range(4)], refs[8:12]
+    sums, weights, key_0, val_0, key_1, val_1 = refs[12:]
     rows = query.shape[0] // 2
-    _, z, y, _ = place_of()
+    x, z, y, _ = place_of()
     middle = kept.shape[0] // 2
     inner_j = jnp.where(y == 0, kept[middle + 2], kept[middle - 2])
     low_j, high_j = kept[middle - 4], kept[middle + 4]
@@ -263,9 +274,15 @@
 
     work = []
     for i, (frame, key_all, val_all) in enumerate(((near, key_0, val_0), (other, key_1, val_1))):
-        for pieces, dest in ((keys, key_all), (vals, val_all)):
-            copies, used = plan(pieces, frame, i == 0)
-            gather(copies, dest, used)
+        gather(*plan(vals, frame, i == 0), val_all)
+        for even in range(2):
+
+            @pl.when(x == 1 - even)
+            def _():
+                own, first, second, inner = keys
+                pieces = (own, first, second, inner) if even else (own, second, first, inner)
+                gather(*plan(pieces, frame, i == 0), key_all)
+
         runs = [(2 * rows, None, 1)] + ([(rows, None, 1)] if i == 0 else [])
         runs += [(BLOCK, inner_j, 1), (BLOCK, low_j, low_ok), (BLOCK, high_j, high_ok)]
         work.append((frame, key_all, val_all, key_mask(runs, key_all.shape[0], 2 * BLOCK - rows)))
@@ -285,17 +302,21 @@
     keep, send, key_0, val_0, key_1, val_1, result = refs[2 * per :]
     rows = query.shape[0] // 2
     depth = 1 << far
-    _, z, y, c = place_of()
+    x, z, y, c = place_of()
     middle = kept.shape[0] // 2
     crossing_j = jnp.where(y == 0, kept[middle - 2], kept[middle + 2])
     crossing_ok = jnp.where(y == 0, jnp.where(z >= 1, 1, 0), jnp.where(z + 1 < depth, 1, 0))
     near, other = y, 1 - y
     use_below = z >= depth // 2
+    use_first = jnp.logical_xor(use_below, x == 1) if far == 2 else use_below
     runs_far = []
     for level in range(1, far - 1):
         step = 1 << level
-        runs_far.append((BLOCK, kept[middle - 4 * step], jnp.where(z >= step, 1, 0)))
-        runs_far.append((BLOCK, kept[middle + 4 * step], jnp.where(z + step < depth, 1, 0)))
+        low = (kept[middle - 4 * step], jnp.where(z >= step, 1, 0))
+        high = (kept[middle + 4 * step], jnp.where(z + step < depth, 1, 0))
+        swap = jnp.logical_and(x == 1, level == 1)
+        runs_far.append((BLOCK, *(jnp.where(swap, b, a) for a, b in zip(low, high))))
+        runs_far.append((BLOCK, *(jnp.where(swap, a, b) for a, b in zip(low, high))))
     top = 2 * depth
     runs_far.append((BLOCK, jnp.where(use_below, kept[middle - top], kept[middle + top]), 1))
 
@@ -309,9 +330,9 @@
             copies = [(pieces[0], row, first, 0)]
             for k in range(2 * (far - 2)):
                 copies.append((pieces[1 + k], at_frame, BLOCK, first + k * BLOCK))
-            gather(copies, dest, used)
+            gather(copies, used, dest)
             here = pl.ds(at_frame, BLOCK)
-            dest[used - BLOCK : used, :] = jnp.where(use_below, pieces[-2][here, :], pieces[-1][here, :])
+            dest[used - BLOCK : used, :] = jnp.where(use_first, pieces[-2][here, :], pieces[-1][here, :])
         runs = [(rows, None, crossing_ok)] if i == 0 else []
         runs += [(BLOCK, crossing_j, crossing_ok)] + runs_far
         mask = key_mask(runs, key_all.shape[0], 2 * BLOCK - rows)
@@ -352,6 +373,13 @@
 
     def to_z(array, k):
         return send(array, lambda g, z, y, c: (g, z + k, y, c))
+
+    def ring(array, second):
+        def where(g, z, y, c):
+            to = z + (1 if (g + second) % 2 == 0 else -1)
+            return (g, to, y, c) if 0 <= to < depth else (g ^ 1, z, y, c)
+
+        return send(array, where)
 
     def around_z(array, k):
         return send(array, lambda g, z, y, c: (g, (z + k) % depth, y, c))
@@ -393,8 +421,12 @@
     units = [unit]
     for _ in range(1, depth):
         units.append(around_z(units[-1], 1))
-    x_0, y_0, x_1, y_1 = to_x(unit), to_y(unit), to_x(units[1]), to_y(units[1])
-    xy_0, xy_1 = to_x(y_0), to_x(y_1)
+    x_0, y_0, y_1 = to_x(unit), to_y(unit), to_y(units[1])
+    (early,) = call(
+        "early", functools.partial(rows_kernel, [(0, 0, size, 2, 0), (1, 0, size, 2, size)]),
+        [(2 * size, quarter)], here(units[1], y_0), [],
+    )
+    early, xy_1 = to_x(early), to_x(y_1)
 
     positions = jnp.pad(rope_positions.T.astype(jnp.bfloat16), ((0, 0), (0, BLOCK - 3)))
     (packed,) = call(
@@ -415,15 +447,6 @@
         ties=[hidden_mate],
     )
     value_inner = to_y(value_inner)
-    rest = depth - 2
-    joined, value_both, positions = call(
-        "join",
-        join_kernel,
-        [(rest * size, quarter), (2 * rows, half), (2 * rows, BLOCK)],
-        here(values, positions, packed, *units[2:]),
-        [],
-        ties=[xy_0, xy_1, x_1, value_inner],
-    )
     query_rot, cosine, sine = call(
         "query_rot",
         query_kernel,
@@ -433,17 +456,24 @@
         vmem=8,
         dtype=[jnp.bfloat16, jnp.float32, jnp.float32],
     )
+    rest = depth - 2
+    joined, value_both = call(
+        "join",
+        join_kernel,
+        [(rest * size, quarter), (2 * rows, half)],
+        here(values, packed, *units[2:]),
+        [],
+        ties=[early, xy_1, value_inner, query_rot],
+    )
     x_rest, y_rest = to_x(joined), to_y(joined)
 
-    def exchange(name, both, ties=()):
-        columns = both.shape[1]
-        below, above = to_z(both, 1), to_z(both, -1)
-        outs = [(2 * BLOCK, columns)] * 2 if far > 1 else []
+    def exchange(name, parts, rings, ties=()):
+        outs = [(2 * BLOCK, half)] * 2 if far > 1 else []
         onward = call(
             name,
-            functools.partial(onward_kernel, far > 1),
-            outs + [(rows + BLOCK, columns)],
-            [kept] + here(below, above),
+            functools.partial(onward_kernel, far > 1, len(parts) > 1),
+            outs + [(rows + BLOCK, half)],
+            [kept] + here(*rings),
             [],
             ties=ties,
         )
@@ -451,63 +481,64 @@
         for level in range(1, far):
             step = 1 << level
             if level == 1:
-                later += [to_z(onward[0], 1), to_z(onward[1], -1)]
+                later += [ring(onward[0], 0), ring(onward[1], 1)]
             else:
                 for sign in (-1, 1):
                     j = kept_blocks[n - 1 + sign * 4 * step] * (rows - BLOCK)
-                    blocks = [lax.dynamic_slice_in_dim(both, f * rows + j, BLOCK, 0) for f in (0, 1)]
-                    later.append(to_z(jnp.concatenate(blocks, 0), -sign * step))
-        return [both, below, above], later, onward[-1]
+                    blocks = [
+                        jnp.concatenate(
+                            [lax.dynamic_slice_in_dim(part, f * rows + j, BLOCK, 0) for f in (0, 1)], 0
+                        )
+                        for part in parts
+                    ]
+                    later.append(to_z(in_order(blocks), -sign * step))
+        return [*parts, *rings], later, onward[-1]
+
+    def in_order(parts):
+        if len(parts) == 1:
+            return parts[0]
+        return jnp.where(x == 0, jnp.concatenate(parts, 1), jnp.concatenate(parts[::-1], 1))
 
     cut = rest * size // 2
-    late_low, late_high = call(
+    turned, late_high = call(
         "turn_late",
         functools.partial(rows_kernel, [(0, 0, cut, 2, 0), (1, cut, cut, 3, 0)]),
         [(cut, quarter)] * 2,
         here(x_rest, y_rest),
         [],
-        ties=[query_rot],
-    )
-    turned = late_low
-    late_low, late_high = to_y(late_low), to_x(late_high)
+    )
+    late_low, late_high = to_y(turned), to_x(late_high)
 
     sources_0 = [(0, 0, 0, 0, 0, size), (1, 0, 0, 1, 0, size), (2, 0, 1, 0, 0, size), (3, 0, 1, 1, 0, size)]
-    sources_1 = [(0, 0, 0, 0, 0, size), (1, 0, 1, 0, 0, size)]
-    sources_1 += [(3, 0, 0, 1, 0, size), (4, 0, 1, 1, 0, size)]
+    sources_1 = [(0, 0, 0, 0, 0, size), (1, 0, 1, 0, 0, size), (1, size, 0, 1, 0, size), (3, 0, 1, 1, 0, size)]
     for k in range(rest):
         sources_0 += [(4, k * size, k + 2, 0, 0, size), (5, k * size, k + 2, 1, 0, size)]
         sources_1.append((2, k * size, k + 2, 0, 0, size))
-        for first in (k * size, k * size + span):
-            late = 5 if first < cut else 6
-            sources_1.append((late, first % cut, k + 2, 1, first - k * size, span))
-
-    def keys_of(name, sources, pieces, outs, extra, ties):
+        for first_row in (k * size, k * size + span):
+            late = 4 if first_row < cut else 5
+            sources_1.append((late, first_row % cut, k + 2, 1, first_row - k * size, span))
+
+    def keys_of(name, sources, pieces, ties):
         return call(
             name,
             functools.partial(key_kernel, sources, len(pieces)),
-            outs,
-            [kept]
-            + here(hidden, hidden_mate, key_gain[None], cosine, sine, *pieces, *extra),
-            ([pltpu.VMEM((2 * rows, quarter), jnp.bfloat16)] if extra else [])
-            + [pltpu.VMEM((model, quarter), jnp.bfloat16)],
+            [(2 * rows, quarter), (rows + BLOCK, quarter)],
+            [kept] + here(hidden, hidden_mate, key_gain[None], cosine, sine, *pieces),
+            [pltpu.VMEM((model, quarter), jnp.bfloat16)],
             ties=ties,
             vmem=12,
         )
 
     pieces = (unit, y_0, units[1], y_1, joined, y_rest)
-    (first_half,) = keys_of("key_rot_0", sources_0, pieces, [(2 * rows, quarter)], [], [turned])
-    value_parts, value_later, value_onward = exchange("value_onward", value_both, [first_half])
-    pieces = (x_0, x_1, x_rest, xy_0, xy_1, late_low, late_high)
-    key_both, key_inner = keys_of(
-        "key_rot_1",
-        sources_1,
-        pieces,
-        [(2 * rows, half), (rows + BLOCK, half)],
-        [first_half],
-        [value_onward],
-    )
-    key_inner = to_y(key_inner)
-    key_parts, key_later, key_onward = exchange("key_onward", key_both)
+    first, first_inner = keys_of("key_rot_0", sources_0, pieces, [turned])
+    value_parts, value_later, value_onward = exchange(
+        "value_onward", [value_both], [to_z(value_both, 1), to_z(value_both, -1)], [first, late_high]
+    )
+    pieces = (x_0, early, x_rest, xy_1, late_low, late_high)
+    second, second_inner = keys_of("key_rot_1", sources_1, pieces, [value_onward])
+    key_rings = [ring(part, second_ring) for second_ring in range(2) for part in (first, second)]
+    key_inner = [to_y(first_inner), to_y(second_inner)]
+    key_parts, key_later, key_onward = exchange("key_onward", [first, second], key_rings, [value_later[0]])
 
     def padded(count):
         return -(-count // BLOCK) * BLOCK
@@ -519,7 +550,7 @@
         "attend_early",
         functools.partial(attend_early_kernel, depth),
         [(2, rows, half), (2, rows, BLOCK)],
-        [kept, (VMEM, query_rot)] + here(*key_parts, key_inner, *value_parts, value_inner),
+        [kept, (VMEM, query_rot)] + here(*key_parts, *key_inner, *value_parts, value_inner),
         gathered(3 * rows + 3 * BLOCK, 2 * rows + 3 * BLOCK),
         ties=[key_onward],
         vmem=16,

time: 121 us -> 110 us (0.909)
  starting transfers between devices: 46 us -> 29.6 us
  waiting for transfers between devices: 49.1 us -> 54 us
    ppermute x29 -> x31, starting transfers between devices: 46 us -> 29.6 us  [send(): return lax.ppermute(array, BOTH, routes(groups, n, where))]
    ppermute x29 -> x31, waiting for transfers between devices: 49.1 us -> 54 us  [send(): return lax.ppermute(array, BOTH, routes(groups, n, where))]
    pallas_call x11 -> x12, Pallas kernels: 20.8 us -> 21.5 us  [call(): pl.pallas_call(run, out_shape=[jax.ShapeDtypeStruct(shape, dtype[i] if is...]
  transfers between devices with their start and end apart: 29 -> 31, of which waited for: 19 -> 21; matrix products, arithmetic and copies ran while one was open for 2% -> 2% of each run, Pallas kernels for 11% -> 15%
where the time goes in v5:
time: 110 us
  waiting for transfers between devices  54 us (49%)
  starting transfers between devices  29.6 us (27%)
  Pallas kernels  21.5 us (20%)
  local copies, waits for them, and re-layouts  2.35 us (2%)
  other arithmetic  1.83 us (2%)
    ppermute x31, waiting for transfers between devices, send(): return lax.ppermute(array, BOTH, routes(groups, n, where))  54 us
    ppermute x31, starting transfers between devices, send(): return lax.ppermute(array, BOTH, routes(groups, n, where))  29.6 us
    pallas_call x12, Pallas kernels, call(): pl.pallas_call(run, out_shape=[jax.ShapeDtypeStruct(shape, dtype[i] if is...  21.5 us
  transfers between devices with their start and end apart: 31, of which 21 were waited for; matrix products, arithmetic and copies ran while one was open for 2% of the time, Pallas kernels for 15%

profile of v5, /device:TPU:0, one launch (start us, length us, event | category | flops | bytes accessed | tf_op | source)
XLA Modules:
  0.0 109.5 jit_solution(13857526544039324971)
XLA Ops:
  1.7 1.9 %collective-permute-done = bf16[192,384]{1,0:T(8,128)(2,1)S(1)} collective-permute-done((bf16[192,384]{1,0:T(8,128)(2,1)S(1)}, bf16[192,384]{1,0:T(8,128)(2,1)S(1)}, u32[]{:S(2)}, u32[]{:S(2)}) %collective-permute-start) | collective-permute-done | bytes 147488 | tf_op jit(solution)/shard_map/ppermute | solution.py:363
  3.7 2.9 %collective-permute-start.1 = (bf16[384,384]{1,0:T(8,128)(2,1)S(1)}, bf16[384,384]{1,0:T(8,128)(2,1)S(1)}, u32[]{:S(2)}, u32[]{:S(2)}) collective-permute-start(bf16[384,384]{1,0:T(8,128)(2,1)S(1)} %maximum_select_fusion.1.refs_6_), channel_id=1, source_target_pairs={{0,16},{1,17},{2,18},{3,19},{4,20},{5,21},{6,22},{7,23},{8,24},{9,... | collective-permute-start | bytes 884744 | tf_op jit(solution)/shard_map/ppermute | solution.py:363
  6.6 1.5 %collective-permute-start.2 = (bf16[384,384]{1,0:T(8,128)(2,1)S(1)}, bf16[384,384]{1,0:T(8,128)(2,1)S(1)}, u32[]{:S(2)}, u32[]{:S(2)}) collective-permute-start(bf16[384,384]{1,0:T(8,128)(2,1)S(1)} %maximum_select_fusion.1.refs_6_), channel_id=1, source_target_pairs={{0,2},{1,3},{2,0},{3,1},{4,6},{5,7},{6,4},{7,5},{8,10},{9,11},{10,... | collective-permute-start | bytes 884744 | tf_op jit(solution)/shard_map/ppermute | solution.py:363
  8.1 1.6 %collective-permute-start.3 = (bf16[384,384]{1,0:T(8,128)(2,1)S(1)}, bf16[384,384]{1,0:T(8,128)(2,1)S(1)}, u32[]{:S(2)}, u32[]{:S(2)}) collective-permute-start(bf16[384,384]{1,0:T(8,128)(2,1)S(1)} %maximum_select_fusion.1.refs_6_), channel_id=1, source_target_pairs={{0,4},{1,5},{2,6},{3,7},{4,8},{5,9},{6,10},{7,11},{8,12},{9,13},{1... | collective-permute-start | bytes 884744 | tf_op jit(solution)/shard_map/ppermute | solution.py:363
  10.6 3.3 %collective-permute-done.1.refs_3_.refs_6_ = bf16[384,384]{1,0:T(8,128)(2,1)S(1)} collective-permute-done((bf16[384,384]{1,0:T(8,128)(2,1)S(1)}, bf16[384,384]{1,0:T(8,128)(2,1)S(1)}, u32[]{:S(2)}, u32[]{:S(2)}) %collective-permute-start.1) | collective-permute-done | bytes 294944 | tf_op jit(solution)/shard_map/ppermute | solution.py:363
  15.3 3.1 %collective-permute-done.3.refs_5_.refs_0_.refs_8_ = bf16[384,384]{1,0:T(8,128)(2,1)S(1)} collective-permute-done((bf16[384,384]{1,0:T(8,128)(2,1)S(1)}, bf16[384,384]{1,0:T(8,128)(2,1)S(1)}, u32[]{:S(2)}, u32[]{:S(2)}) %collective-permute-start.3) | collective-permute-done | bytes 294944 | tf_op jit(solution)/shard_map/ppermute | solution.py:363
  23.2 7.0 %collective-permute-done.6.refs_9_ = bf16[384,384]{1,0:T(8,128)(2,1)S(1)} collective-permute-done((bf16[384,384]{1,0:T(8,128)(2,1)S(1)}, bf16[384,384]{1,0:T(8,128)(2,1)S(1)}, u32[]{:S(2)}, u32[]{:S(2)}) %collective-permute-start.6) | collective-permute-done | bytes 294944 | tf_op jit(solution)/shard_map/ppermute | solution.py:363
  30.2 1.5 %collective-permute-start.10 = (bf16[384,384]{1,0:T(8,128)(2,1)S(1)}, bf16[384,384]{1,0:T(8,128)(2,1)S(1)}, u32[]{:S(2)}, u32[]{:S(2)}) collective-permute-start(bf16[384,384]{1,0:T(8,128)(2,1)S(1)} %collective-permute-done.6.refs_9_), channel_id=1, source_target_pairs={{0,16},{1,17},{2,18},{3,19},{4,20},{5,21},{6,22},{7,23},{8,24},{9,... | collective-permute-start | bytes 884744 | tf_op jit(solution)/shard_map/ppermute | solution.py:363
  31.7 3.8 %query_rot.1 = (bf16[480,768]{1,0:T(8,128)(2,1)S(1)}, f32[480,128]{1,0:T(8,128)S(1)}, f32[480,128]{1,0:T(8,128)S(1)}) custom-call(bf16[240,1536]{1,0:T(8,128)(2,1)S(1)} %copy-done.3, bf16[240,1664]{1,0:T(8,128)(2,1)S(1)} %collective-permute-done.4.refs_1_.refs_2_, f32[1,128]{1,0:T(1,128)S(1)} %bitcast.7, bf16[240,128]{1,0:T(8,128)(2,1)S(1)} %pad.4.refs_2_.refs_3_, ...), custom_call_target="tpu_custom_call" | custom-call | flops 1 | bytes 1 | tf_op jit(solution)/shard_map/query_rot/pallas_call | solution.py:393
  36.0 5.9 %collective-permute-done.10.refs_5_.refs_9_ = bf16[384,384]{1,0:T(8,128)(2,1)S(1)} collective-permute-done((bf16[384,384]{1,0:T(8,128)(2,1)S(1)}, bf16[384,384]{1,0:T(8,128)(2,1)S(1)}, u32[]{:S(2)}, u32[]{:S(2)}) %collective-permute-start.10) | collective-permute-done | bytes 294944 | tf_op jit(solution)/shard_map/ppermute | solution.py:363
  43.0 1.5 %collective-permute-start.13 = (bf16[768,384]{1,0:T(8,128)(2,1)S(1)}, bf16[768,384]{1,0:T(8,128)(2,1)S(1)}, u32[]{:S(2)}, u32[]{:S(2)}) collective-permute-start(bf16[768,384]{1,0:T(8,128)(2,1)S(1)} %get-tuple-element.29.refs_10_), channel_id=1, source_target_pairs={{0,16},{1,17},{2,18},{3,19},{4,20},{5,21},{6,22},{7,23},{8,24},{9,... | collective-permute-start | bytes 1769480 | tf_op jit(solution)/shard_map/ppermute | solution.py:363
  47.1 9.9 %collective-permute-done.12.refs_1_.refs_11_ = bf16[768,384]{1,0:T(8,128)(2,1)S(1)} collective-permute-done((bf16[768,384]{1,0:T(8,128)(2,1)S(1)}, bf16[768,384]{1,0:T(8,128)(2,1)S(1)}, u32[]{:S(2)}, u32[]{:S(2)}) %collective-permute-start.12) | collective-permute-done | bytes 589856 | tf_op jit(solution)/shard_map/ppermute | solution.py:363
  58.3 1.5 %collective-permute-start.14 = (bf16[384,384]{1,0:T(8,128)(2,1)S(1)}, bf16[384,384]{1,0:T(8,128)(2,1)S(1)}, u32[]{:S(2)}, u32[]{:S(2)}) collective-permute-start(bf16[384,384]{1,0:T(8,128)(2,1)S(1)} %get-tuple-element.30.refs_12_), channel_id=1, source_target_pairs={{0,2},{1,3},{2,0},{3,1},{4,6},{5,7},{6,4},{7,5},{8,10},{9,11},{10,... | collective-permute-start | bytes 884744 | tf_op jit(solution)/shard_map/ppermute | solution.py:363
  59.8 3.0 %key_rot_0.1 = (bf16[480,384]{1,0:T(8,128)(2,1)S(1)}, bf16[368,384]{1,0:T(8,128)(2,1)S(1)}) custom-call(s32[31]{0:T(128)S(1)} %slice_bitcast_fusion.refs_0_, bf16[240,3072]{1,0:T(8,128)(2,1)S(1)} %copy-done.1, bf16[240,3072]{1,0:T(8,128)(2,1)S(1)} %collective-permute-done.5.refs_3_.refs_2_, f32[1,128]{1,0:T(1,128)S(1)} %bitcast.5, ...), custom_call_target="tpu_custom_call" | custom-call | flops 1 | bytes 1 | tf_op jit(solution)/shard_map/key_rot_0/pallas_call | solution.py:393
  62.8 1.5 %collective-permute-done.17.refs_2_.refs_12_ = bf16[480,768]{1,0:T(8,128)(2,1)S(1)} collective-permute-done((bf16[480,768]{1,0:T(8,128)(2,1)S(1)}, bf16[480,768]{1,0:T(8,128)(2,1)S(1)}, u32[]{:S(2)}, u32[]{:S(2)}) %collective-permute-start.17) | collective-permute-done | bytes 737312 | tf_op jit(solution)/shard_map/ppermute | solution.py:363
  65.6 1.5 %collective-permute-start.24 = (bf16[368,768]{1,0:T(8,128)(2,1)S(1)}, bf16[368,768]{1,0:T(8,128)(2,1)S(1)}, u32[]{:S(2)}, u32[]{:S(2)}) collective-permute-start(bf16[368,768]{1,0:T(8,128)(2,1)S(1)} %get-tuple-element.34.refs_12_), channel_id=1, source_target_pairs={{0,2},{1,3},{2,0},{3,1},{4,6},{5,7},{6,4},{7,5},{8,10},{9,11},{10,... | collective-permute-start | bytes 1695752 | tf_op jit(solution)/shard_map/ppermute | solution.py:363
  69.1 3.0 %key_rot_1.1 = (bf16[480,384]{1,0:T(8,128)(2,1)S(1)}, bf16[368,384]{1,0:T(8,128)(2,1)S(1)}) custom-call(s32[31]{0:T(128)S(1)} %slice_bitcast_fusion.refs_0_, bf16[240,3072]{1,0:T(8,128)(2,1)S(1)} %copy-done.1, bf16[240,3072]{1,0:T(8,128)(2,1)S(1)} %collective-permute-done.5.refs_3_.refs_2_, f32[1,128]{1,0:T(1,128)S(1)} %bitcast.6, ...), custom_call_target="tpu_custom_call" | custom-call | flops 1 | bytes 1 | tf_op jit(solution)/shard_map/key_rot_1/pallas_call | solution.py:393
  74.2 4.1 %collective-permute-done.18.refs_1_.refs_4_ = bf16[480,384]{1,0:T(8,128)(2,1)S(1)} collective-permute-done((bf16[480,384]{1,0:T(8,128)(2,1)S(1)}, bf16[480,384]{1,0:T(8,128)(2,1)S(1)}, u32[]{:S(2)}, u32[]{:S(2)}) %collective-permute-start.18) | collective-permute-done | bytes 368672 | tf_op jit(solution)/shard_map/ppermute | solution.py:363
  80.3 2.5 %collective-permute-done.19.refs_2_.refs_5_ = bf16[480,384]{1,0:T(8,128)(2,1)S(1)} collective-permute-done((bf16[480,384]{1,0:T(8,128)(2,1)S(1)}, bf16[480,384]{1,0:T(8,128)(2,1)S(1)}, u32[]{:S(2)}, u32[]{:S(2)}) %collective-permute-start.19) | collective-permute-done | bytes 368672 | tf_op jit(solution)/shard_map/ppermute | solution.py:363
  85.0 1.6 %collective-permute-start.28 = (bf16[256,768]{1,0:T(8,128)(2,1)S(1)}, bf16[256,768]{1,0:T(8,128)(2,1)S(1)}, u32[]{:S(2)}, u32[]{:S(2)}) collective-permute-start(bf16[256,768]{1,0:T(8,128)(2,1)S(1)} %get-tuple-element.43), channel_id=1, source_target_pairs={{0,4},{1,5},{2,6},{3,7},{4,8},{5,9},{6,10},{7,11},{8,12},{9,13},{1... | collective-permute-start | bytes 1179656 | tf_op jit(solution)/shard_map/ppermute | solution.py:363
  89.0 5.0 %collective-permute-done.23.refs_9_ = bf16[368,384]{1,0:T(8,128)(2,1)S(1)} collective-permute-done((bf16[368,384]{1,0:T(8,128)(2,1)S(1)}, bf16[368,384]{1,0:T(8,128)(2,1)S(1)}, u32[]{:S(2)}, u32[]{:S(2)}) %collective-permute-start.23) | collective-permute-done | bytes 282656 | tf_op jit(solution)/shard_map/ppermute | solution.py:363
  95.0 4.7 %attend_early.1 = (f32[2,240,768]{2,1,0:T(8,128)S(1)}, f32[2,240,128]{2,1,0:T(8,128)S(1)}) custom-call(s32[31]{0:T(128)S(1)} %slice_bitcast_fusion.refs_0_, bf16[480,768]{1,0:T(8,128)(2,1)S(1)} %get-tuple-element.26.refs_7_.refs_1_, bf16[480,384]{1,0:T(8,128)(2,1)S(1)} %get-tuple-element.31.refs_3_.refs_2_, bf16[480,384]{1,0:T(8,128)(2,1)S(1)} %get-tuple-element.35.refs_3_, ...), custom_call_target="tpu_custom_call" | custom-call | flops 1 | bytes 1 | tf_op jit(solution)/shard_map/attend_early/pallas_call | solution.py:393
  102.2 4.5 %attend_late.1 = (bf16[240,768]{1,0:T(8,128)(2,1)S(1)}, bf16[240,768]{1,0:T(8,128)(2,1)S(1)}) custom-call(s32[31]{0:T(128)S(1)} %slice_bitcast_fusion.refs_0_, bf16[480,768]{1,0:T(8,128)(2,1)S(1)} %get-tuple-element.26.refs_7_.refs_1_, f32[2,240,768]{2,1,0:T(8,128)S(1)} %get-tuple-element.39.refs_2_, f32[2,240,128]{2,1,0:T(8,128)S(1)} %get-tuple-element.40.refs_3_, ...), custom_call_target="tpu_custom_call" | custom-call | flops 1 | bytes 1 | tf_op jit(solution)/shard_map/attend_late/pallas_call | solution.py:393
  106.8 1.7 %collective-permute-done.30 = bf16[240,768]{1,0:T(8,128)(2,1)S(1)} collective-permute-done((bf16[240,768]{1,0:T(8,128)(2,1)S(1)}, bf16[240,768]{1,0:T(8,128)(2,1)S(1)}, u32[]{:S(2)}, u32[]{:S(2)}) %collective-permute-start.30) | collective-permute-done | bytes 368672 | tf_op jit(solution)/shard_map/ppermute | solution.py:363
  (73 shorter events, 30.8 us)
Async XLA Ops:
  0.0 22.0 %collective-permute-start.5 = (bf16[240,3072]{1,0:T(8,128)(2,1)}, bf16[240,3072]{1,0:T(8,128)(2,1)S(1)}, u32[]{:S(2)}, u32[]{:S(2)}) collective-permute-start(bf16[240,3072]{1,0:T(8,128)(2,1)} %refs_1_.7), channel_id=1, source_target_pairs={{0,1},{1,0},{2,3},{3,2},{4,5},{5,4},{6,7},{7,6},{8,9},{9,8},{10,11... | collective-permute-start | bytes 4423688 | tf_op jit(solution)/shard_map/ppermute | solution.py:363
  3.7 10.2 %collective-permute-start.1 = (bf16[384,384]{1,0:T(8,128)(2,1)S(1)}, bf16[384,384]{1,0:T(8,128)(2,1)S(1)}, u32[]{:S(2)}, u32[]{:S(2)}) collective-permute-start(bf16[384,384]{1,0:T(8,128)(2,1)S(1)} %maximum_select_fusion.1.refs_6_), channel_id=1, source_target_pairs={{0,16},{1,17},{2,18},{3,19},{4,20},{5,21},{6,22},{7,23},{8,24},{9,... | collective-permute-start | bytes 884744 | tf_op jit(solution)/shard_map/ppermute | solution.py:363
  8.1 10.3 %collective-permute-start.3 = (bf16[384,384]{1,0:T(8,128)(2,1)S(1)}, bf16[384,384]{1,0:T(8,128)(2,1)S(1)}, u32[]{:S(2)}, u32[]{:S(2)}) collective-permute-start(bf16[384,384]{1,0:T(8,128)(2,1)S(1)} %maximum_select_fusion.1.refs_6_), channel_id=1, source_target_pairs={{0,4},{1,5},{2,6},{3,7},{4,8},{5,9},{6,10},{7,11},{8,12},{9,13},{1... | collective-permute-start | bytes 884744 | tf_op jit(solution)/shard_map/ppermute | solution.py:363
  19.8 16.2 %collective-permute-start.9 = (bf16[768,384]{1,0:T(8,128)(2,1)S(1)}, bf16[768,384]{1,0:T(8,128)(2,1)S(1)}, u32[]{:S(2)}, u32[]{:S(2)}) collective-permute-start(bf16[768,384]{1,0:T(8,128)(2,1)S(1)} %early.1), channel_id=1, source_target_pairs={{0,16},{1,17},{2,18},{3,19},{4,20},{5,21},{6,22},{7,23},{8,24},{9,... | collective-permute-start | bytes 1769480 | tf_op jit(solution)/shard_map/ppermute | solution.py:363
  20.4 9.8 %collective-permute-start.6 = (bf16[384,384]{1,0:T(8,128)(2,1)S(1)}, bf16[384,384]{1,0:T(8,128)(2,1)S(1)}, u32[]{:S(2)}, u32[]{:S(2)}) collective-permute-start(bf16[384,384]{1,0:T(8,128)(2,1)S(1)} %collective-permute-done.3.refs_5_.refs_0_.refs_8_), channel_id=1, source_target_pairs={{0,2},{1,3},{2,0},{3,1},{4,6},{5,7},{6,4},{7,5},{8,10},{9,11},{10,... | collective-permute-start | bytes 884744 | tf_op jit(solution)/shard_map/ppermute | solution.py:363
  20.9 10.8 %collective-permute-start.7 = (bf16[384,384]{1,0:T(8,128)(2,1)S(1)}, bf16[384,384]{1,0:T(8,128)(2,1)S(1)}, u32[]{:S(2)}, u32[]{:S(2)}) collective-permute-start(bf16[384,384]{1,0:T(8,128)(2,1)S(1)} %collective-permute-done.3.refs_5_.refs_0_.refs_8_), channel_id=1, source_target_pairs={{0,4},{1,5},{2,6},{3,7},{4,8},{5,9},{6,10},{7,11},{8,12},{9,13},{1... | collective-permute-start | bytes 884744 | tf_op jit(solution)/shard_map/ppermute | solution.py:363
  22.6 19.3 %collective-permute-start.11 = (bf16[368,768]{1,0:T(8,128)(2,1)S(1)}, bf16[368,768]{1,0:T(8,128)(2,1)S(1)}, u32[]{:S(2)}, u32[]{:S(2)}) collective-permute-start(bf16[368,768]{1,0:T(8,128)(2,1)S(1)} %value_inner.1), channel_id=1, source_target_pairs={{0,2},{1,3},{2,0},{3,1},{4,6},{5,7},{6,4},{7,5},{8,10},{9,11},{10,... | collective-permute-start | bytes 1695752 | tf_op jit(solution)/shard_map/ppermute | solution.py:363
  30.2 11.7 %collective-permute-start.10 = (bf16[384,384]{1,0:T(8,128)(2,1)S(1)}, bf16[384,384]{1,0:T(8,128)(2,1)S(1)}, u32[]{:S(2)}, u32[]{:S(2)}) collective-permute-start(bf16[384,384]{1,0:T(8,128)(2,1)S(1)} %collective-permute-done.6.refs_9_), channel_id=1, source_target_pairs={{0,16},{1,17},{2,18},{3,19},{4,20},{5,21},{6,22},{7,23},{8,24},{9,... | collective-permute-start | bytes 884744 | tf_op jit(solution)/shard_map/ppermute | solution.py:363
  31.7 10.2 %collective-permute-start.8 = (bf16[384,384]{1,0:T(8,128)(2,1)S(1)}, bf16[384,384]{1,0:T(8,128)(2,1)S(1)}, u32[]{:S(2)}, u32[]{:S(2)}) collective-permute-start(bf16[384,384]{1,0:T(8,128)(2,1)S(1)} %collective-permute-done.7.refs_2_), channel_id=1, source_target_pairs={{0,4},{1,5},{2,6},{3,7},{4,8},{5,9},{6,10},{7,11},{8,12},{9,13},{1... | collective-permute-start | bytes 884744 | tf_op jit(solution)/shard_map/ppermute | solution.py:363
  42.0 15.0 %collective-permute-start.12 = (bf16[768,384]{1,0:T(8,128)(2,1)S(1)}, bf16[768,384]{1,0:T(8,128)(2,1)S(1)}, u32[]{:S(2)}, u32[]{:S(2)}) collective-permute-start(bf16[768,384]{1,0:T(8,128)(2,1)S(1)} %get-tuple-element.29.refs_10_), channel_id=1, source_target_pairs={{0,2},{1,3},{2,0},{3,1},{4,6},{5,7},{6,4},{7,5},{8,10},{9,11},{10,... | collective-permute-start | bytes 1769480 | tf_op jit(solution)/shard_map/ppermute | solution.py:363
  43.0 14.3 %collective-permute-start.13 = (bf16[768,384]{1,0:T(8,128)(2,1)S(1)}, bf16[768,384]{1,0:T(8,128)(2,1)S(1)}, u32[]{:S(2)}, u32[]{:S(2)}) collective-permute-start(bf16[768,384]{1,0:T(8,128)(2,1)S(1)} %get-tuple-element.29.refs_10_), channel_id=1, source_target_pairs={{0,16},{1,17},{2,18},{3,19},{4,20},{5,21},{6,22},{7,23},{8,24},{9,... | collective-permute-start | bytes 1769480 | tf_op jit(solution)/shard_map/ppermute | solution.py:363
  44.5 18.3 %collective-permute-start.16 = (bf16[480,768]{1,0:T(8,128)(2,1)S(1)}, bf16[480,768]{1,0:T(8,128)(2,1)S(1)}, u32[]{:S(2)}, u32[]{:S(2)}) collective-permute-start(bf16[480,768]{1,0:T(8,128)(2,1)S(1)} %get-tuple-element.33.refs_10_), channel_id=1, source_target_pairs={{0,4},{1,5},{2,6},{3,7},{4,8},{5,9},{6,10},{7,11},{8,12},{9,13},{1... | collective-permute-start | bytes 2211848 | tf_op jit(solution)/shard_map/ppermute | solution.py:363
  45.8 18.5 %collective-permute-start.17 = (bf16[480,768]{1,0:T(8,128)(2,1)S(1)}, bf16[480,768]{1,0:T(8,128)(2,1)S(1)}, u32[]{:S(2)}, u32[]{:S(2)}) collective-permute-start(bf16[480,768]{1,0:T(8,128)(2,1)S(1)} %get-tuple-element.33.refs_10_), channel_id=1, source_target_pairs={{4,0},{5,1},{6,2},{7,3},{8,4},{9,5},{10,6},{11,7},{12,8},{13,9},{1... | collective-permute-start | bytes 2211848 | tf_op jit(solution)/shard_map/ppermute | solution.py:363
  58.3 10.8 %collective-permute-start.14 = (bf16[384,384]{1,0:T(8,128)(2,1)S(1)}, bf16[384,384]{1,0:T(8,128)(2,1)S(1)}, u32[]{:S(2)}, u32[]{:S(2)}) collective-permute-start(bf16[384,384]{1,0:T(8,128)(2,1)S(1)} %get-tuple-element.30.refs_12_), channel_id=1, source_target_pairs={{0,2},{1,3},{2,0},{3,1},{4,6},{5,7},{6,4},{7,5},{8,10},{9,11},{10,... | collective-permute-start | bytes 884744 | tf_op jit(solution)/shard_map/ppermute | solution.py:363
  65.6 18.0 %collective-permute-start.24 = (bf16[368,768]{1,0:T(8,128)(2,1)S(1)}, bf16[368,768]{1,0:T(8,128)(2,1)S(1)}, u32[]{:S(2)}, u32[]{:S(2)}) collective-permute-start(bf16[368,768]{1,0:T(8,128)(2,1)S(1)} %get-tuple-element.34.refs_12_), channel_id=1, source_target_pairs={{0,2},{1,3},{2,0},{3,1},{4,6},{5,7},{6,4},{7,5},{8,10},{9,11},{10,... | collective-permute-start | bytes 1695752 | tf_op jit(solution)/shard_map/ppermute | solution.py:363
  67.1 11.2 %collective-permute-start.18 = (bf16[480,384]{1,0:T(8,128)(2,1)S(1)}, bf16[480,384]{1,0:T(8,128)(2,1)S(1)}, u32[]{:S(2)}, u32[]{:S(2)}) collective-permute-start(bf16[480,384]{1,0:T(8,128)(2,1)S(1)} %get-tuple-element.31.refs_3_.refs_2_), channel_id=1, source_target_pairs={{0,4},{1,5},{2,6},{3,7},{4,8},{5,9},{6,10},{7,11},{8,12},{9,13},{1... | collective-permute-start | bytes 1105928 | tf_op jit(solution)/shard_map/ppermute | solution.py:363
  68.1 11.0 %collective-permute-start.20 = (bf16[480,384]{1,0:T(8,128)(2,1)S(1)}, bf16[480,384]{1,0:T(8,128)(2,1)S(1)}, u32[]{:S(2)}, u32[]{:S(2)}) collective-permute-start(bf16[480,384]{1,0:T(8,128)(2,1)S(1)} %get-tuple-element.31.refs_3_.refs_2_), channel_id=1, source_target_pairs={{0,16},{1,17},{2,18},{3,19},{4,0},{5,1},{6,2},{7,3},{8,4},{9,5},{1... | collective-permute-start | bytes 1105928 | tf_op jit(solution)/shard_map/ppermute | solution.py:363
  72.1 10.6 %collective-permute-start.19 = (bf16[480,384]{1,0:T(8,128)(2,1)S(1)}, bf16[480,384]{1,0:T(8,128)(2,1)S(1)}, u32[]{:S(2)}, u32[]{:S(2)}) collective-permute-start(bf16[480,384]{1,0:T(8,128)(2,1)S(1)} %get-tuple-element.35.refs_3_), channel_id=1, source_target_pairs={{0,4},{1,5},{2,6},{3,7},{4,8},{5,9},{6,10},{7,11},{8,12},{9,13},{1... | collective-permute-start | bytes 1105928 | tf_op jit(solution)/shard_map/ppermute | solution.py:363
  73.2 10.3 %collective-permute-start.21 = (bf16[480,384]{1,0:T(8,128)(2,1)S(1)}, bf16[480,384]{1,0:T(8,128)(2,1)S(1)}, u32[]{:S(2)}, u32[]{:S(2)}) collective-permute-start(bf16[480,384]{1,0:T(8,128)(2,1)S(1)} %get-tuple-element.35.refs_3_), channel_id=1, source_target_pairs={{0,16},{1,17},{2,18},{3,19},{4,0},{5,1},{6,2},{7,3},{8,4},{9,5},{1... | collective-permute-start | bytes 1105928 | tf_op jit(solution)/shard_map/ppermute | solution.py:363
  79.1 14.9 %collective-permute-start.23 = (bf16[368,384]{1,0:T(8,128)(2,1)S(1)}, bf16[368,384]{1,0:T(8,128)(2,1)S(1)}, u32[]{:S(2)}, u32[]{:S(2)}) collective-permute-start(bf16[368,384]{1,0:T(8,128)(2,1)S(1)} %get-tuple-element.37), channel_id=1, source_target_pairs={{0,2},{1,3},{2,0},{3,1},{4,6},{5,7},{6,4},{7,5},{8,10},{9,11},{10,... | collective-permute-start | bytes 847880 | tf_op jit(solution)/shard_map/ppermute | solution.py:363
  84.4 17.8 %collective-permute-start.25 = (bf16[368,768]{1,0:T(8,128)(2,1)S(1)}, bf16[368,768]{1,0:T(8,128)(2,1)S(1)}, u32[]{:S(2)}, u32[]{:S(2)}) collective-permute-start(bf16[368,768]{1,0:T(8,128)(2,1)S(1)} %get-tuple-element.38.refs_14_), channel_id=1, source_target_pairs={{0,2},{1,3},{2,0},{3,1},{4,6},{5,7},{6,4},{7,5},{8,10},{9,11},{10,... | collective-permute-start | bytes 1695752 | tf_op jit(solution)/shard_map/ppermute | solution.py:363
  85.0 14.7 %collective-permute-start.28 = (bf16[256,768]{1,0:T(8,128)(2,1)S(1)}, bf16[256,768]{1,0:T(8,128)(2,1)S(1)}, u32[]{:S(2)}, u32[]{:S(2)}) collective-permute-start(bf16[256,768]{1,0:T(8,128)(2,1)S(1)} %get-tuple-element.43), channel_id=1, source_target_pairs={{0,4},{1,5},{2,6},{3,7},{4,8},{5,9},{6,10},{7,11},{8,12},{9,13},{1... | collective-permute-start | bytes 1179656 | tf_op jit(solution)/shard_map/ppermute | solution.py:363
  86.6 13.1 %collective-permute-start.29 = (bf16[256,768]{1,0:T(8,128)(2,1)S(1)}, bf16[256,768]{1,0:T(8,128)(2,1)S(1)}, u32[]{:S(2)}, u32[]{:S(2)}) collective-permute-start(bf16[256,768]{1,0:T(8,128)(2,1)S(1)} %get-tuple-element.44), channel_id=1, source_target_pairs={{0,16},{1,17},{2,18},{3,19},{4,0},{5,1},{6,2},{7,3},{8,4},{9,5},{1... | collective-permute-start | bytes 1179656 | tf_op jit(solution)/shard_map/ppermute | solution.py:363
  87.9 13.0 %collective-permute-start.26 = (bf16[256,768]{1,0:T(8,128)(2,1)S(1)}, bf16[256,768]{1,0:T(8,128)(2,1)S(1)}, u32[]{:S(2)}, u32[]{:S(2)}) collective-permute-start(bf16[256,768]{1,0:T(8,128)(2,1)S(1)} %get-tuple-element.41), channel_id=1, source_target_pairs={{0,4},{1,5},{2,6},{3,7},{4,8},{5,9},{6,10},{7,11},{8,12},{9,13},{1... | collective-permute-start | bytes 1179656 | tf_op jit(solution)/shard_map/ppermute | solution.py:363
  (15 other events, 138.6 us)

commit v6 on v5

--- a/solution.py
+++ b/solution.py
@@ -146,7 +146,7 @@
     rows = refs[0].shape[0] // 2
     shift = rows - BLOCK
     middle = kept.shape[0] // 2
-    x, _, y, _ = place_of()
+    _, _, y, c = place_of()
 
     def start(j, frame):
         return pl.multiple_of(frame * rows + j * shift, 16)
@@ -154,9 +154,9 @@
     to = outs[-1]
     for even in range(2):
 
-        @pl.when(x == 1 - even)
+        @pl.when(c == 1 - even)
         def _():
-            below, above = rings if even or not halves else rings[::-1]
+            below, above = rings if even else rings[::-1]
             if forward:
                 up, down = outs[:2] if even else outs[1::-1]
                 for out, source, j in ((up, below, kept[middle - 8]), (down, above, kept[middle + 8])):
@@ -230,15 +230,24 @@
     return mask.astype(jnp.float32)
 
 
-def attend(query, at, keys, vals, mask):
+def attend(query, at, keys, vals, mask, ahead=0):
     head_dim = BLOCK
     scale = jnp.float32(head_dim ** (-0.5) * np.log2(np.e))
-    for h in range(query.shape[1] // head_dim):
+    heads = query.shape[1] // head_dim
+    scores = []
+    for h in range(heads):
         cols = slice(h * head_dim, (h + 1) * head_dim)
-        scores = lax.dot_general(
-            query[at, cols], keys[:, cols], (((1,), (1,)), ((), ())), preferred_element_type=jnp.float32
-        )
-        weights = jnp.exp2(scores * scale) * mask
+        for i in range(len(scores), min(h + ahead + 1, heads)):
+            there = slice(i * head_dim, (i + 1) * head_dim)
+            scores.append(
+                lax.dot_general(
+                    query[at, there],
+                    keys[:, there],
+                    (((1,), (1,)), ((), ())),
+                    preferred_element_type=jnp.float32,
+                )
+            )
+        weights = jnp.exp2(scores[h] * scale) * mask
         total = jnp.sum(weights, axis=1, keepdims=True)
         part = jnp.dot(
             weights.astype(jnp.bfloat16), vals[:, cols], preferred_element_type=jnp.float32
@@ -250,7 +259,7 @@
     keys, vals = [refs[2 * i : 2 * i + 2] for i in range(4)], refs[8:12]
     sums, weights, key_0, val_0, key_1, val_1 = refs[12:]
     rows = query.shape[0] // 2
-    x, z, y, _ = place_of()
+    _, z, y, c = place_of()
     middle = kept.shape[0] // 2
     inner_j = jnp.where(y == 0, kept[middle + 2], kept[middle - 2])
     low_j, high_j = kept[middle - 4], kept[middle + 4]
@@ -274,14 +283,13 @@
 
     work = []
     for i, (frame, key_all, val_all) in enumerate(((near, key_0, val_0), (other, key_1, val_1))):
-        gather(*plan(vals, frame, i == 0), val_all)
         for even in range(2):
 
-            @pl.when(x == 1 - even)
+            @pl.when(c == 1 - even)
             def _():
-                own, first, second, inner = keys
-                pieces = (own, first, second, inner) if even else (own, second, first, inner)
-                gather(*plan(pieces, frame, i == 0), key_all)
+                for (own, first, second, inner), dest in ((keys, key_all), (vals, val_all)):
+                    below, above = (first, second) if even else (second, first)
+                    gather(*plan((own, below, above, inner), frame, i == 0), dest)
 
         runs = [(2 * rows, None, 1)] + ([(rows, None, 1)] if i == 0 else [])
         runs += [(BLOCK, inner_j, 1), (BLOCK, low_j, low_ok), (BLOCK, high_j, high_ok)]
@@ -302,19 +310,19 @@
     keep, send, key_0, val_0, key_1, val_1, result = refs[2 * per :]
     rows = query.shape[0] // 2
     depth = 1 << far
-    x, z, y, c = place_of()
+    _, z, y, c = place_of()
     middle = kept.shape[0] // 2
     crossing_j = jnp.where(y == 0, kept[middle - 2], kept[middle + 2])
     crossing_ok = jnp.where(y == 0, jnp.where(z >= 1, 1, 0), jnp.where(z + 1 < depth, 1, 0))
     near, other = y, 1 - y
     use_below = z >= depth // 2
-    use_first = jnp.logical_xor(use_below, x == 1) if far == 2 else use_below
+    use_first = jnp.logical_xor(use_below, c == 1) if far == 2 else use_below
     runs_far = []
     for level in range(1, far - 1):
         step = 1 << level
         low = (kept[middle - 4 * step], jnp.where(z >= step, 1, 0))
         high = (kept[middle + 4 * step], jnp.where(z + step < depth, 1, 0))
-        swap = jnp.logical_and(x == 1, level == 1)
+        swap = jnp.logical_and(c == 1, level == 1)
         runs_far.append((BLOCK, *(jnp.where(swap, b, a) for a, b in zip(low, high))))
         runs_far.append((BLOCK, *(jnp.where(swap, a, b) for a, b in zip(low, high))))
     top = 2 * depth
@@ -340,8 +348,8 @@
     for frame, key_all, val_all, mask in work:
         at = pl.ds(pl.multiple_of(frame * rows, 16), rows)
         before = weights[frame]
-        for h, (cols, more, total) in enumerate(attend(query, at, key_all, val_all, mask)):
-            done = (sums[frame, :, cols] + more) / (before[:, h : h + 1] + total)
+        for h, (cols, more, total) in enumerate(attend(query, at, key_all, val_all, mask, 1)):
+            done = (sums[frame, :, cols] + more) * (1.0 / (before[:, h : h + 1] + total))
             result[frame, :, cols] = done.astype(result.dtype)
     keep[...] = result[c]
     send[...] = result[1 - c]
@@ -376,8 +384,8 @@
 
     def ring(array, second):
         def where(g, z, y, c):
-            to = z + (1 if (g + second) % 2 == 0 else -1)
-            return (g, to, y, c) if 0 <= to < depth else (g ^ 1, z, y, c)
+            to = z + (1 if (c + second) % 2 == 0 else -1)
+            return (g, to, y, c) if 0 <= to < depth else (g, z, y, 1 - c)
 
         return send(array, where)
 
@@ -467,7 +475,8 @@
     )
     x_rest, y_rest = to_x(joined), to_y(joined)
 
-    def exchange(name, parts, rings, ties=()):
+    def exchange(name, parts, ties=()):
+        rings = [ring(part, second) for second in range(2) for part in parts]
         outs = [(2 * BLOCK, half)] * 2 if far > 1 else []
         onward = call(
             name,
@@ -499,11 +508,11 @@
             return parts[0]
         return jnp.where(x == 0, jnp.concatenate(parts, 1), jnp.concatenate(parts[::-1], 1))
 
-    cut = rest * size // 2
+    cut, whole = rest * size // 2, rest * size
     turned, late_high = call(
         "turn_late",
-        functools.partial(rows_kernel, [(0, 0, cut, 2, 0), (1, cut, cut, 3, 0)]),
-        [(cut, quarter)] * 2,
+        functools.partial(rows_kernel, [(0, 0, cut, 2, 0), (1, cut, whole - cut, 3, 0)]),
+        [(cut, quarter), (whole - cut, quarter)],
         here(x_rest, y_rest),
         [],
     )
@@ -515,8 +524,8 @@
         sources_0 += [(4, k * size, k + 2, 0, 0, size), (5, k * size, k + 2, 1, 0, size)]
         sources_1.append((2, k * size, k + 2, 0, 0, size))
         for first_row in (k * size, k * size + span):
-            late = 4 if first_row < cut else 5
-            sources_1.append((late, first_row % cut, k + 2, 1, first_row - k * size, span))
+            late, at = (4, first_row) if first_row < cut else (5, first_row - cut)
+            sources_1.append((late, at, k + 2, 1, first_row - k * size, span))
 
     def keys_of(name, sources, pieces, ties):
         return call(
@@ -530,15 +539,12 @@
         )
 
     pieces = (unit, y_0, units[1], y_1, joined, y_rest)
-    first, first_inner = keys_of("key_rot_0", sources_0, pieces, [turned])
-    value_parts, value_later, value_onward = exchange(
-        "value_onward", [value_both], [to_z(value_both, 1), to_z(value_both, -1)], [first, late_high]
-    )
+    first, first_inner = keys_of("key_rot_0", sources_0, pieces, [x_rest])
+    value_parts, value_later, value_onward = exchange("value_onward", [value_both], [first, late_high])
     pieces = (x_0, early, x_rest, xy_1, late_low, late_high)
-    second, second_inner = keys_of("key_rot_1", sources_1, pieces, [value_onward])
-    key_rings = [ring(part, second_ring) for second_ring in range(2) for part in (first, second)]
+    second, second_inner = keys_of("key_rot_1", sources_1, pieces, [first, value_inner])
     key_inner = [to_y(first_inner), to_y(second_inner)]
-    key_parts, key_later, key_onward = exchange("key_onward", [first, second], key_rings, [value_later[0]])
+    key_parts, key_later, key_onward = exchange("key_onward", [first, second], [value_later[0]])
 
     def padded(count):
         return -(-count // BLOCK) * BLOCK
@@ -552,7 +558,7 @@
         [(2, rows, half), (2, rows, BLOCK)],
         [kept, (VMEM, query_rot)] + here(*key_parts, *key_inner, *value_parts, value_inner),
         gathered(3 * rows + 3 * BLOCK, 2 * rows + 3 * BLOCK),
-        ties=[key_onward],
+        ties=[key_onward, value_later[0]],
         vmem=16,
         dtype=jnp.float32,
     )

time: 110 us -> 109 us (level)
  transfers between devices with their start and end apart: 31 -> 31, of which waited for: 21 -> 16; matrix products, arithmetic and copies ran while one was open for 2% -> 2% of each run, Pallas kernels for 15% -> 16%
where the time goes in v6:
time: 109 us
  waiting for transfers between devices  53.9 us (49%)
  starting transfers between devices  29.6 us (27%)
  Pallas kernels  21.4 us (20%)
  local copies, waits for them, and re-layouts  2.35 us (2%)
  other arithmetic  1.83 us (2%)
    ppermute x31, waiting for transfers between devices, send(): return lax.ppermute(array, BOTH, routes(groups, n, where))  53.9 us
    ppermute x31, starting transfers between devices, send(): return lax.ppermute(array, BOTH, routes(groups, n, where))  29.6 us
    pallas_call x12, Pallas kernels, call(): pl.pallas_call(run, out_shape=[jax.ShapeDtypeStruct(shape, dtype[i] if is...  21.4 us
  transfers between devices with their start and end apart: 31, of which 16 were waited for; matrix products, arithmetic and copies ran while one was open for 2% of the time, Pallas kernels for 16%

profile of v6, /device:TPU:0, one launch (start us, length us, event | category | flops | bytes accessed | tf_op | source)
XLA Modules:
  0.0 109.2 jit_solution(7952379268787208394)
XLA Ops:
  1.7 1.9 %collective-permute-done = bf16[192,384]{1,0:T(8,128)(2,1)S(1)} collective-permute-done((bf16[192,384]{1,0:T(8,128)(2,1)S(1)}, bf16[192,384]{1,0:T(8,128)(2,1)S(1)}, u32[]{:S(2)}, u32[]{:S(2)}) %collective-permute-start) | collective-permute-done | bytes 147488 | tf_op jit(solution)/shard_map/ppermute | solution.py:371
  3.7 3.0 %collective-permute-start.3 = (bf16[384,384]{1,0:T(8,128)(2,1)S(1)}, bf16[384,384]{1,0:T(8,128)(2,1)S(1)}, u32[]{:S(2)}, u32[]{:S(2)}) collective-permute-start(bf16[384,384]{1,0:T(8,128)(2,1)S(1)} %maximum_select_fusion.1.refs_6_), channel_id=1, source_target_pairs={{0,4},{1,5},{2,6},{3,7},{4,8},{5,9},{6,10},{7,11},{8,12},{9,13},{1... | collective-permute-start | bytes 884744 | tf_op jit(solution)/shard_map/ppermute | solution.py:371
  10.6 5.4 %collective-permute-done.3.refs_5_.refs_0_.refs_8_ = bf16[384,384]{1,0:T(8,128)(2,1)S(1)} collective-permute-done((bf16[384,384]{1,0:T(8,128)(2,1)S(1)}, bf16[384,384]{1,0:T(8,128)(2,1)S(1)}, u32[]{:S(2)}, u32[]{:S(2)}) %collective-permute-start.3) | collective-permute-done | bytes 294944 | tf_op jit(solution)/shard_map/ppermute | solution.py:371
  22.3 1.6 %collective-permute-start.11 = (bf16[368,768]{1,0:T(8,128)(2,1)S(1)}, bf16[368,768]{1,0:T(8,128)(2,1)S(1)}, u32[]{:S(2)}, u32[]{:S(2)}) collective-permute-start(bf16[368,768]{1,0:T(8,128)(2,1)S(1)} %value_inner.1), channel_id=1, source_target_pairs={{0,2},{1,3},{2,0},{3,1},{4,6},{5,7},{6,4},{7,5},{8,10},{9,11},{10,... | collective-permute-start | bytes 1695752 | tf_op jit(solution)/shard_map/ppermute | solution.py:371
  23.9 6.6 %collective-permute-done.7.refs_2_ = bf16[384,384]{1,0:T(8,128)(2,1)S(1)} collective-permute-done((bf16[384,384]{1,0:T(8,128)(2,1)S(1)}, bf16[384,384]{1,0:T(8,128)(2,1)S(1)}, u32[]{:S(2)}, u32[]{:S(2)}) %collective-permute-start.7) | collective-permute-done | bytes 294944 | tf_op jit(solution)/shard_map/ppermute | solution.py:371
  31.6 3.8 %query_rot.1 = (bf16[480,768]{1,0:T(8,128)(2,1)S(1)}, f32[480,128]{1,0:T(8,128)S(1)}, f32[480,128]{1,0:T(8,128)S(1)}) custom-call(bf16[240,1536]{1,0:T(8,128)(2,1)S(1)} %copy-done.3, bf16[240,1664]{1,0:T(8,128)(2,1)S(1)} %collective-permute-done.4.refs_1_.refs_2_, f32[1,128]{1,0:T(1,128)S(1)} %bitcast.7, bf16[240,128]{1,0:T(8,128)(2,1)S(1)} %pad.4.refs_2_.refs_3_, ...), custom_call_target="tpu_custom_call" | custom-call | flops 1 | bytes 1 | tf_op jit(solution)/shard_map/query_rot/pallas_call | solution.py:401
  35.4 5.2 %collective-permute-done.8.refs_3_ = bf16[384,384]{1,0:T(8,128)(2,1)S(1)} collective-permute-done((bf16[384,384]{1,0:T(8,128)(2,1)S(1)}, bf16[384,384]{1,0:T(8,128)(2,1)S(1)}, u32[]{:S(2)}, u32[]{:S(2)}) %collective-permute-start.8) | collective-permute-done | bytes 294944 | tf_op jit(solution)/shard_map/ppermute | solution.py:371
  43.3 2.0 %collective-permute-start.22 = (bf16[480,768]{1,0:T(8,128)(2,1)S(1)}, bf16[480,768]{1,0:T(8,128)(2,1)S(1)}, u32[]{:S(2)}, u32[]{:S(2)}) collective-permute-start(bf16[480,768]{1,0:T(8,128)(2,1)S(1)} %get-tuple-element.36.refs_10_), channel_id=1, source_target_pairs={{0,4},{1,0},{2,6},{3,2},{4,8},{5,1},{6,10},{7,3},{8,12},{9,5},{10,... | collective-permute-start | bytes 2211848 | tf_op jit(solution)/shard_map/ppermute | solution.py:371
  45.3 11.2 %collective-permute-done.13.refs_12_.refs_0_.refs_8_ = bf16[768,384]{1,0:T(8,128)(2,1)S(1)} collective-permute-done((bf16[768,384]{1,0:T(8,128)(2,1)S(1)}, bf16[768,384]{1,0:T(8,128)(2,1)S(1)}, u32[]{:S(2)}, u32[]{:S(2)}) %collective-permute-start.13) | collective-permute-done | bytes 589856 | tf_op jit(solution)/shard_map/ppermute | solution.py:371
  58.9 3.0 %key_rot_0.1 = (bf16[480,384]{1,0:T(8,128)(2,1)S(1)}, bf16[368,384]{1,0:T(8,128)(2,1)S(1)}) custom-call(s32[31]{0:T(128)S(1)} %slice_bitcast_fusion.refs_0_, bf16[240,3072]{1,0:T(8,128)(2,1)S(1)} %copy-done.1, bf16[240,3072]{1,0:T(8,128)(2,1)S(1)} %collective-permute-done.5.refs_3_.refs_2_, f32[1,128]{1,0:T(1,128)S(1)} %bitcast.5, ...), custom_call_target="tpu_custom_call" | custom-call | flops 1 | bytes 1 | tf_op jit(solution)/shard_map/key_rot_0/pallas_call | solution.py:401
  62.0 1.7 %collective-permute-done.15.refs_11_.refs_4_ = bf16[384,384]{1,0:T(8,128)(2,1)S(1)} collective-permute-done((bf16[384,384]{1,0:T(8,128)(2,1)S(1)}, bf16[384,384]{1,0:T(8,128)(2,1)S(1)}, u32[]{:S(2)}, u32[]{:S(2)}) %collective-permute-start.15) | collective-permute-done | bytes 294944 | tf_op jit(solution)/shard_map/ppermute | solution.py:371
  65.0 2.0 %collective-permute-start.16 = (bf16[480,384]{1,0:T(8,128)(2,1)S(1)}, bf16[480,384]{1,0:T(8,128)(2,1)S(1)}, u32[]{:S(2)}, u32[]{:S(2)}) collective-permute-start(bf16[480,384]{1,0:T(8,128)(2,1)S(1)} %get-tuple-element.30.refs_12_.refs_3_.refs_2_), channel_id=1, source_target_pairs={{0,4},{1,0},{2,6},{3,2},{4,8},{5,1},{6,10},{7,3},{8,12},{9,5},{10,... | collective-permute-start | bytes 1105928 | tf_op jit(solution)/shard_map/ppermute | solution.py:371
  67.0 3.0 %key_rot_1.1 = (bf16[480,384]{1,0:T(8,128)(2,1)S(1)}, bf16[368,384]{1,0:T(8,128)(2,1)S(1)}) custom-call(s32[31]{0:T(128)S(1)} %slice_bitcast_fusion.refs_0_, bf16[240,3072]{1,0:T(8,128)(2,1)S(1)} %copy-done.1, bf16[240,3072]{1,0:T(8,128)(2,1)S(1)} %collective-permute-done.5.refs_3_.refs_2_, f32[1,128]{1,0:T(1,128)S(1)} %bitcast.6, ...), custom_call_target="tpu_custom_call" | custom-call | flops 1 | bytes 1 | tf_op jit(solution)/shard_map/key_rot_1/pallas_call | solution.py:401
  70.1 2.0 %collective-permute-start.17 = (bf16[480,384]{1,0:T(8,128)(2,1)S(1)}, bf16[480,384]{1,0:T(8,128)(2,1)S(1)}, u32[]{:S(2)}, u32[]{:S(2)}) collective-permute-start(bf16[480,384]{1,0:T(8,128)(2,1)S(1)} %get-tuple-element.33.refs_3_), channel_id=1, source_target_pairs={{0,4},{1,0},{2,6},{3,2},{4,8},{5,1},{6,10},{7,3},{8,12},{9,5},{10,... | collective-permute-start | bytes 1105928 | tf_op jit(solution)/shard_map/ppermute | solution.py:371
  72.1 4.4 %collective-permute-done.18.refs_3_.refs_6_ = bf16[480,384]{1,0:T(8,128)(2,1)S(1)} collective-permute-done((bf16[480,384]{1,0:T(8,128)(2,1)S(1)}, bf16[480,384]{1,0:T(8,128)(2,1)S(1)}, u32[]{:S(2)}, u32[]{:S(2)}) %collective-permute-start.18) | collective-permute-done | bytes 368672 | tf_op jit(solution)/shard_map/ppermute | solution.py:371
  78.5 3.5 %collective-permute-done.19.refs_4_.refs_7_ = bf16[480,384]{1,0:T(8,128)(2,1)S(1)} collective-permute-done((bf16[480,384]{1,0:T(8,128)(2,1)S(1)}, bf16[480,384]{1,0:T(8,128)(2,1)S(1)}, u32[]{:S(2)}, u32[]{:S(2)}) %collective-permute-start.19) | collective-permute-done | bytes 368672 | tf_op jit(solution)/shard_map/ppermute | solution.py:371
  82.8 1.6 %collective-permute-start.25 = (bf16[368,768]{1,0:T(8,128)(2,1)S(1)}, bf16[368,768]{1,0:T(8,128)(2,1)S(1)}, u32[]{:S(2)}, u32[]{:S(2)}) collective-permute-start(bf16[368,768]{1,0:T(8,128)(2,1)S(1)} %get-tuple-element.38.refs_14_), channel_id=1, source_target_pairs={{0,2},{1,3},{2,0},{3,1},{4,6},{5,7},{6,4},{7,5},{8,10},{9,11},{10,... | collective-permute-start | bytes 1695752 | tf_op jit(solution)/shard_map/ppermute | solution.py:371
  84.4 1.7 %collective-permute-start.28 = (bf16[256,768]{1,0:T(8,128)(2,1)S(1)}, bf16[256,768]{1,0:T(8,128)(2,1)S(1)}, u32[]{:S(2)}, u32[]{:S(2)}) collective-permute-start(bf16[256,768]{1,0:T(8,128)(2,1)S(1)} %get-tuple-element.43), channel_id=1, source_target_pairs={{0,4},{1,0},{2,6},{3,2},{4,8},{5,1},{6,10},{7,3},{8,12},{9,5},{10,... | collective-permute-start | bytes 1179656 | tf_op jit(solution)/shard_map/ppermute | solution.py:371
  86.3 1.9 %collective-permute-start.26 = (bf16[256,768]{1,0:T(8,128)(2,1)S(1)}, bf16[256,768]{1,0:T(8,128)(2,1)S(1)}, u32[]{:S(2)}, u32[]{:S(2)}) collective-permute-start(bf16[256,768]{1,0:T(8,128)(2,1)S(1)} %get-tuple-element.41), channel_id=1, source_target_pairs={{0,4},{1,0},{2,6},{3,2},{4,8},{5,1},{6,10},{7,3},{8,12},{9,5},{10,... | collective-permute-start | bytes 1179656 | tf_op jit(solution)/shard_map/ppermute | solution.py:371
  88.1 4.2 %collective-permute-done.21.refs_9_ = bf16[368,384]{1,0:T(8,128)(2,1)S(1)} collective-permute-done((bf16[368,384]{1,0:T(8,128)(2,1)S(1)}, bf16[368,384]{1,0:T(8,128)(2,1)S(1)}, u32[]{:S(2)}, u32[]{:S(2)}) %collective-permute-start.21) | collective-permute-done | bytes 282656 | tf_op jit(solution)/shard_map/ppermute | solution.py:371
  92.3 4.9 %attend_early.1 = (f32[2,240,768]{2,1,0:T(8,128)S(1)}, f32[2,240,128]{2,1,0:T(8,128)S(1)}) custom-call(s32[31]{0:T(128)S(1)} %slice_bitcast_fusion.refs_0_, bf16[480,768]{1,0:T(8,128)(2,1)S(1)} %get-tuple-element.26.refs_7_.refs_1_, bf16[480,384]{1,0:T(8,128)(2,1)S(1)} %get-tuple-element.30.refs_12_.refs_3_.refs_2_, ...), custom_call_target="tpu_custom_call" | custom-call | flops 1 | bytes 1 | tf_op jit(solution)/shard_map/attend_early/pallas_call | solution.py:401
  97.3 4.9 %collective-permute-done.26.refs_5_ = bf16[256,768]{1,0:T(8,128)(2,1)S(1)} collective-permute-done((bf16[256,768]{1,0:T(8,128)(2,1)S(1)}, bf16[256,768]{1,0:T(8,128)(2,1)S(1)}, u32[]{:S(2)}, u32[]{:S(2)}) %collective-permute-start.26) | collective-permute-done | bytes 393248 | tf_op jit(solution)/shard_map/ppermute | solution.py:371
  102.1 4.3 %attend_late.1 = (bf16[240,768]{1,0:T(8,128)(2,1)S(1)}, bf16[240,768]{1,0:T(8,128)(2,1)S(1)}) custom-call(s32[31]{0:T(128)S(1)} %slice_bitcast_fusion.refs_0_, bf16[480,768]{1,0:T(8,128)(2,1)S(1)} %get-tuple-element.26.refs_7_.refs_1_, f32[2,240,768]{2,1,0:T(8,128)S(1)} %get-tuple-element.39.refs_2_, f32[2,240,128]{2,1,0:T(8,128)S(1)} %get-tuple-element.40.refs_3_, ...), custom_call_target="tpu_custom_call" | custom-call | flops 1 | bytes 1 | tf_op jit(solution)/shard_map/attend_late/pallas_call | solution.py:401
  106.5 1.7 %collective-permute-done.30 = bf16[240,768]{1,0:T(8,128)(2,1)S(1)} collective-permute-done((bf16[240,768]{1,0:T(8,128)(2,1)S(1)}, bf16[240,768]{1,0:T(8,128)(2,1)S(1)}, u32[]{:S(2)}, u32[]{:S(2)}) %collective-permute-start.30) | collective-permute-done | bytes 368672 | tf_op jit(solution)/shard_map/ppermute | solution.py:371
  (73 shorter events, 23.3 us)
Async XLA Ops:
  0.0 21.7 %collective-permute-start.5 = (bf16[240,3072]{1,0:T(8,128)(2,1)}, bf16[240,3072]{1,0:T(8,128)(2,1)S(1)}, u32[]{:S(2)}, u32[]{:S(2)}) collective-permute-start(bf16[240,3072]{1,0:T(8,128)(2,1)} %refs_1_.7), channel_id=1, source_target_pairs={{0,1},{1,0},{2,3},{3,2},{4,5},{5,4},{6,7},{7,6},{8,9},{9,8},{10,11... | collective-permute-start | bytes 4423688 | tf_op jit(solution)/shard_map/ppermute | solution.py:371
  3.7 12.3 %collective-permute-start.3 = (bf16[384,384]{1,0:T(8,128)(2,1)S(1)}, bf16[384,384]{1,0:T(8,128)(2,1)S(1)}, u32[]{:S(2)}, u32[]{:S(2)}) collective-permute-start(bf16[384,384]{1,0:T(8,128)(2,1)S(1)} %maximum_select_fusion.1.refs_6_), channel_id=1, source_target_pairs={{0,4},{1,5},{2,6},{3,7},{4,8},{5,9},{6,10},{7,11},{8,12},{9,13},{1... | collective-permute-start | bytes 884744 | tf_op jit(solution)/shard_map/ppermute | solution.py:371
  18.0 22.6 %collective-permute-start.9 = (bf16[768,384]{1,0:T(8,128)(2,1)S(1)}, bf16[768,384]{1,0:T(8,128)(2,1)S(1)}, u32[]{:S(2)}, u32[]{:S(2)}) collective-permute-start(bf16[768,384]{1,0:T(8,128)(2,1)S(1)} %early.1), channel_id=1, source_target_pairs={{0,16},{1,17},{2,18},{3,19},{4,20},{5,21},{6,22},{7,23},{8,24},{9,... | collective-permute-start | bytes 1769480 | tf_op jit(solution)/shard_map/ppermute | solution.py:371
  19.5 10.9 %collective-permute-start.7 = (bf16[384,384]{1,0:T(8,128)(2,1)S(1)}, bf16[384,384]{1,0:T(8,128)(2,1)S(1)}, u32[]{:S(2)}, u32[]{:S(2)}) collective-permute-start(bf16[384,384]{1,0:T(8,128)(2,1)S(1)} %collective-permute-done.3.refs_5_.refs_0_.refs_8_), channel_id=1, source_target_pairs={{0,4},{1,5},{2,6},{3,7},{4,8},{5,9},{6,10},{7,11},{8,12},{9,13},{1... | collective-permute-start | bytes 884744 | tf_op jit(solution)/shard_map/ppermute | solution.py:371
  21.1 9.9 %collective-permute-start.6 = (bf16[384,384]{1,0:T(8,128)(2,1)S(1)}, bf16[384,384]{1,0:T(8,128)(2,1)S(1)}, u32[]{:S(2)}, u32[]{:S(2)}) collective-permute-start(bf16[384,384]{1,0:T(8,128)(2,1)S(1)} %collective-permute-done.3.refs_5_.refs_0_.refs_8_), channel_id=1, source_target_pairs={{0,2},{1,3},{2,0},{3,1},{4,6},{5,7},{6,4},{7,5},{8,10},{9,11},{10,... | collective-permute-start | bytes 884744 | tf_op jit(solution)/shard_map/ppermute | solution.py:371
  22.3 19.8 %collective-permute-start.11 = (bf16[368,768]{1,0:T(8,128)(2,1)S(1)}, bf16[368,768]{1,0:T(8,128)(2,1)S(1)}, u32[]{:S(2)}, u32[]{:S(2)}) collective-permute-start(bf16[368,768]{1,0:T(8,128)(2,1)S(1)} %value_inner.1), channel_id=1, source_target_pairs={{0,2},{1,3},{2,0},{3,1},{4,6},{5,7},{6,4},{7,5},{8,10},{9,11},{10,... | collective-permute-start | bytes 1695752 | tf_op jit(solution)/shard_map/ppermute | solution.py:371
  30.5 10.1 %collective-permute-start.8 = (bf16[384,384]{1,0:T(8,128)(2,1)S(1)}, bf16[384,384]{1,0:T(8,128)(2,1)S(1)}, u32[]{:S(2)}, u32[]{:S(2)}) collective-permute-start(bf16[384,384]{1,0:T(8,128)(2,1)S(1)} %collective-permute-done.7.refs_2_), channel_id=1, source_target_pairs={{0,4},{1,5},{2,6},{3,7},{4,8},{5,9},{6,10},{7,11},{8,12},{9,13},{1... | collective-permute-start | bytes 884744 | tf_op jit(solution)/shard_map/ppermute | solution.py:371
  31.0 9.6 %collective-permute-start.10 = (bf16[384,384]{1,0:T(8,128)(2,1)S(1)}, bf16[384,384]{1,0:T(8,128)(2,1)S(1)}, u32[]{:S(2)}, u32[]{:S(2)}) collective-permute-start(bf16[384,384]{1,0:T(8,128)(2,1)S(1)} %collective-permute-done.6.refs_9_), channel_id=1, source_target_pairs={{0,16},{1,17},{2,18},{3,19},{4,20},{5,21},{6,22},{7,23},{8,24},{9,... | collective-permute-start | bytes 884744 | tf_op jit(solution)/shard_map/ppermute | solution.py:371
  42.2 14.4 %collective-permute-start.13 = (bf16[768,384]{1,0:T(8,128)(2,1)S(1)}, bf16[768,384]{1,0:T(8,128)(2,1)S(1)}, u32[]{:S(2)}, u32[]{:S(2)}) collective-permute-start(bf16[768,384]{1,0:T(8,128)(2,1)S(1)} %get-tuple-element.29.refs_10_), channel_id=1, source_target_pairs={{0,16},{1,17},{2,18},{3,19},{4,20},{5,21},{6,22},{7,23},{8,24},{9,... | collective-permute-start | bytes 1769480 | tf_op jit(solution)/shard_map/ppermute | solution.py:371
  42.8 14.0 %collective-permute-start.12 = (bf16[768,384]{1,0:T(8,128)(2,1)S(1)}, bf16[768,384]{1,0:T(8,128)(2,1)S(1)}, u32[]{:S(2)}, u32[]{:S(2)}) collective-permute-start(bf16[768,384]{1,0:T(8,128)(2,1)S(1)} %get-tuple-element.29.refs_10_), channel_id=1, source_target_pairs={{0,2},{1,3},{2,0},{3,1},{4,6},{5,7},{6,4},{7,5},{8,10},{9,11},{10,... | collective-permute-start | bytes 1769480 | tf_op jit(solution)/shard_map/ppermute | solution.py:371
  43.3 18.7 %collective-permute-start.23 = (bf16[480,768]{1,0:T(8,128)(2,1)S(1)}, bf16[480,768]{1,0:T(8,128)(2,1)S(1)}, u32[]{:S(2)}, u32[]{:S(2)}) collective-permute-start(bf16[480,768]{1,0:T(8,128)(2,1)S(1)} %get-tuple-element.36.refs_10_), channel_id=1, source_target_pairs={{0,1},{1,5},{2,3},{3,7},{4,0},{5,9},{6,2},{7,11},{8,4},{9,13},{10,... | collective-permute-start | bytes 2211848 | tf_op jit(solution)/shard_map/ppermute | solution.py:371
  43.3 18.7 %collective-permute-start.22 = (bf16[480,768]{1,0:T(8,128)(2,1)S(1)}, bf16[480,768]{1,0:T(8,128)(2,1)S(1)}, u32[]{:S(2)}, u32[]{:S(2)}) collective-permute-start(bf16[480,768]{1,0:T(8,128)(2,1)S(1)} %get-tuple-element.36.refs_10_), channel_id=1, source_target_pairs={{0,4},{1,0},{2,6},{3,2},{4,8},{5,1},{6,10},{7,3},{8,12},{9,5},{10,... | collective-permute-start | bytes 2211848 | tf_op jit(solution)/shard_map/ppermute | solution.py:371
  64.4 17.7 %collective-permute-start.24 = (bf16[368,768]{1,0:T(8,128)(2,1)S(1)}, bf16[368,768]{1,0:T(8,128)(2,1)S(1)}, u32[]{:S(2)}, u32[]{:S(2)}) collective-permute-start(bf16[368,768]{1,0:T(8,128)(2,1)S(1)} %get-tuple-element.37), channel_id=1, source_target_pairs={{0,2},{1,3},{2,0},{3,1},{4,6},{5,7},{6,4},{7,5},{8,10},{9,11},{10,... | collective-permute-start | bytes 1695752 | tf_op jit(solution)/shard_map/ppermute | solution.py:371
  65.0 11.5 %collective-permute-start.18 = (bf16[480,384]{1,0:T(8,128)(2,1)S(1)}, bf16[480,384]{1,0:T(8,128)(2,1)S(1)}, u32[]{:S(2)}, u32[]{:S(2)}) collective-permute-start(bf16[480,384]{1,0:T(8,128)(2,1)S(1)} %get-tuple-element.30.refs_12_.refs_3_.refs_2_), channel_id=1, source_target_pairs={{0,1},{1,5},{2,3},{3,7},{4,0},{5,9},{6,2},{7,11},{8,4},{9,13},{10,... | collective-permute-start | bytes 1105928 | tf_op jit(solution)/shard_map/ppermute | solution.py:371
  65.0 13.0 %collective-permute-start.16 = (bf16[480,384]{1,0:T(8,128)(2,1)S(1)}, bf16[480,384]{1,0:T(8,128)(2,1)S(1)}, u32[]{:S(2)}, u32[]{:S(2)}) collective-permute-start(bf16[480,384]{1,0:T(8,128)(2,1)S(1)} %get-tuple-element.30.refs_12_.refs_3_.refs_2_), channel_id=1, source_target_pairs={{0,4},{1,0},{2,6},{3,2},{4,8},{5,1},{6,10},{7,3},{8,12},{9,5},{10,... | collective-permute-start | bytes 1105928 | tf_op jit(solution)/shard_map/ppermute | solution.py:371
  70.1 12.0 %collective-permute-start.19 = (bf16[480,384]{1,0:T(8,128)(2,1)S(1)}, bf16[480,384]{1,0:T(8,128)(2,1)S(1)}, u32[]{:S(2)}, u32[]{:S(2)}) collective-permute-start(bf16[480,384]{1,0:T(8,128)(2,1)S(1)} %get-tuple-element.33.refs_3_), channel_id=1, source_target_pairs={{0,1},{1,5},{2,3},{3,7},{4,0},{5,9},{6,2},{7,11},{8,4},{9,13},{10,... | collective-permute-start | bytes 1105928 | tf_op jit(solution)/shard_map/ppermute | solution.py:371
  70.1 12.0 %collective-permute-start.17 = (bf16[480,384]{1,0:T(8,128)(2,1)S(1)}, bf16[480,384]{1,0:T(8,128)(2,1)S(1)}, u32[]{:S(2)}, u32[]{:S(2)}) collective-permute-start(bf16[480,384]{1,0:T(8,128)(2,1)S(1)} %get-tuple-element.33.refs_3_), channel_id=1, source_target_pairs={{0,4},{1,0},{2,6},{3,2},{4,8},{5,1},{6,10},{7,3},{8,12},{9,5},{10,... | collective-permute-start | bytes 1105928 | tf_op jit(solution)/shard_map/ppermute | solution.py:371
  76.5 9.8 %collective-permute-start.20 = (bf16[368,384]{1,0:T(8,128)(2,1)S(1)}, bf16[368,384]{1,0:T(8,128)(2,1)S(1)}, u32[]{:S(2)}, u32[]{:S(2)}) collective-permute-start(bf16[368,384]{1,0:T(8,128)(2,1)S(1)} %get-tuple-element.34), channel_id=1, source_target_pairs={{0,2},{1,3},{2,0},{3,1},{4,6},{5,7},{6,4},{7,5},{8,10},{9,11},{10,... | collective-permute-start | bytes 847880 | tf_op jit(solution)/shard_map/ppermute | solution.py:371
  78.0 14.3 %collective-permute-start.21 = (bf16[368,384]{1,0:T(8,128)(2,1)S(1)}, bf16[368,384]{1,0:T(8,128)(2,1)S(1)}, u32[]{:S(2)}, u32[]{:S(2)}) collective-permute-start(bf16[368,384]{1,0:T(8,128)(2,1)S(1)} %get-tuple-element.35), channel_id=1, source_target_pairs={{0,2},{1,3},{2,0},{3,1},{4,6},{5,7},{6,4},{7,5},{8,10},{9,11},{10,... | collective-permute-start | bytes 847880 | tf_op jit(solution)/shard_map/ppermute | solution.py:371
  82.8 19.3 %collective-permute-start.25 = (bf16[368,768]{1,0:T(8,128)(2,1)S(1)}, bf16[368,768]{1,0:T(8,128)(2,1)S(1)}, u32[]{:S(2)}, u32[]{:S(2)}) collective-permute-start(bf16[368,768]{1,0:T(8,128)(2,1)S(1)} %get-tuple-element.38.refs_14_), channel_id=1, source_target_pairs={{0,2},{1,3},{2,0},{3,1},{4,6},{5,7},{6,4},{7,5},{8,10},{9,11},{10,... | collective-permute-start | bytes 1695752 | tf_op jit(solution)/shard_map/ppermute | solution.py:371
  84.4 12.9 %collective-permute-start.28 = (bf16[256,768]{1,0:T(8,128)(2,1)S(1)}, bf16[256,768]{1,0:T(8,128)(2,1)S(1)}, u32[]{:S(2)}, u32[]{:S(2)}) collective-permute-start(bf16[256,768]{1,0:T(8,128)(2,1)S(1)} %get-tuple-element.43), channel_id=1, source_target_pairs={{0,4},{1,0},{2,6},{3,2},{4,8},{5,1},{6,10},{7,3},{8,12},{9,5},{10,... | collective-permute-start | bytes 1179656 | tf_op jit(solution)/shard_map/ppermute | solution.py:371
  86.1 11.2 %collective-permute-start.29 = (bf16[256,768]{1,0:T(8,128)(2,1)S(1)}, bf16[256,768]{1,0:T(8,128)(2,1)S(1)}, u32[]{:S(2)}, u32[]{:S(2)}) collective-permute-start(bf16[256,768]{1,0:T(8,128)(2,1)S(1)} %get-tuple-element.44), channel_id=1, source_target_pairs={{0,1},{1,5},{2,3},{3,7},{4,0},{5,9},{6,2},{7,11},{8,4},{9,13},{10,... | collective-permute-start | bytes 1179656 | tf_op jit(solution)/shard_map/ppermute | solution.py:371
  86.3 15.9 %collective-permute-start.26 = (bf16[256,768]{1,0:T(8,128)(2,1)S(1)}, bf16[256,768]{1,0:T(8,128)(2,1)S(1)}, u32[]{:S(2)}, u32[]{:S(2)}) collective-permute-start(bf16[256,768]{1,0:T(8,128)(2,1)S(1)} %get-tuple-element.41), channel_id=1, source_target_pairs={{0,4},{1,0},{2,6},{3,2},{4,8},{5,1},{6,10},{7,3},{8,12},{9,5},{10,... | collective-permute-start | bytes 1179656 | tf_op jit(solution)/shard_map/ppermute | solution.py:371
  92.3 9.8 %collective-permute-start.27 = (bf16[256,768]{1,0:T(8,128)(2,1)S(1)}, bf16[256,768]{1,0:T(8,128)(2,1)S(1)}, u32[]{:S(2)}, u32[]{:S(2)}) collective-permute-start(bf16[256,768]{1,0:T(8,128)(2,1)S(1)} %get-tuple-element.42), channel_id=1, source_target_pairs={{0,1},{1,5},{2,3},{3,7},{4,0},{5,9},{6,2},{7,11},{8,4},{9,13},{10,... | collective-permute-start | bytes 1179656 | tf_op jit(solution)/shard_map/ppermute | solution.py:371
  (15 other events, 133.3 us)

commit v7 on v6

--- a/solution.py
+++ b/solution.py
@@ -248,6 +248,15 @@
                 )
             )
         weights = jnp.exp2(scores[h] * scale) * mask
+        if ahead:
+            ones = jnp.ones((vals.shape[0], head_dim), vals.dtype)
+            both = jnp.dot(
+                weights.astype(jnp.bfloat16),
+                jnp.concatenate([vals[:, cols], ones], 1),
+                preferred_element_type=jnp.float32,
+            )
+            yield cols, both[:, :head_dim], both[:, head_dim : head_dim + 1]
+            continue
         total = jnp.sum(weights, axis=1, keepdims=True)
         part = jnp.dot(
             weights.astype(jnp.bfloat16), vals[:, cols], preferred_element_type=jnp.float32

time: 109 us -> 107 us (0.982)
  Pallas kernels: 21.4 us -> 19.4 us
    pallas_call x12, Pallas kernels: 21.4 us -> 19.4 us  [call(): pl.pallas_call(run, out_shape=[jax.ShapeDtypeStruct(shape, dtype[i] if is...]
where the time goes in v7:
time: 107 us
  waiting for transfers between devices  53.9 us (50%)
  starting transfers between devices  29.6 us (28%)
  Pallas kernels  19.4 us (18%)
  local copies, waits for them, and re-layouts  2.35 us (2%)
  other arithmetic  1.83 us (2%)
    ppermute x31, waiting for transfers between devices, send(): return lax.ppermute(array, BOTH, routes(groups, n, where))  53.9 us
    ppermute x31, starting transfers between devices, send(): return lax.ppermute(array, BOTH, routes(groups, n, where))  29.6 us
    pallas_call x12, Pallas kernels, call(): pl.pallas_call(run, out_shape=[jax.ShapeDtypeStruct(shape, dtype[i] if is...  19.4 us
  transfers between devices with their start and end apart: 31, of which 16 were waited for; matrix products, arithmetic and copies ran while one was open for 2% of the time, Pallas kernels for 16%

profile of v7, /device:TPU:0, one launch (start us, length us, event | category | flops | bytes accessed | tf_op | source)
XLA Modules:
  0.0 107.3 jit_solution(14151202969359784161)
XLA Ops:
  1.7 1.9 %collective-permute-done = bf16[192,384]{1,0:T(8,128)(2,1)S(1)} collective-permute-done((bf16[192,384]{1,0:T(8,128)(2,1)S(1)}, bf16[192,384]{1,0:T(8,128)(2,1)S(1)}, u32[]{:S(2)}, u32[]{:S(2)}) %collective-permute-start) | collective-permute-done | bytes 147488 | tf_op jit(solution)/shard_map/ppermute | solution.py:380
  3.7 3.0 %collective-permute-start.3 = (bf16[384,384]{1,0:T(8,128)(2,1)S(1)}, bf16[384,384]{1,0:T(8,128)(2,1)S(1)}, u32[]{:S(2)}, u32[]{:S(2)}) collective-permute-start(bf16[384,384]{1,0:T(8,128)(2,1)S(1)} %maximum_select_fusion.1.refs_6_), channel_id=1, source_target_pairs={{0,4},{1,5},{2,6},{3,7},{4,8},{5,9},{6,10},{7,11},{8,12},{9,13},{1... | collective-permute-start | bytes 884744 | tf_op jit(solution)/shard_map/ppermute | solution.py:380
  10.6 5.4 %collective-permute-done.3.refs_5_.refs_0_.refs_8_ = bf16[384,384]{1,0:T(8,128)(2,1)S(1)} collective-permute-done((bf16[384,384]{1,0:T(8,128)(2,1)S(1)}, bf16[384,384]{1,0:T(8,128)(2,1)S(1)}, u32[]{:S(2)}, u32[]{:S(2)}) %collective-permute-start.3) | collective-permute-done | bytes 294944 | tf_op jit(solution)/shard_map/ppermute | solution.py:380
  22.3 1.6 %collective-permute-start.11 = (bf16[368,768]{1,0:T(8,128)(2,1)S(1)}, bf16[368,768]{1,0:T(8,128)(2,1)S(1)}, u32[]{:S(2)}, u32[]{:S(2)}) collective-permute-start(bf16[368,768]{1,0:T(8,128)(2,1)S(1)} %value_inner.1), channel_id=1, source_target_pairs={{0,2},{1,3},{2,0},{3,1},{4,6},{5,7},{6,4},{7,5},{8,10},{9,11},{10,... | collective-permute-start | bytes 1695752 | tf_op jit(solution)/shard_map/ppermute | solution.py:380
  23.9 6.6 %collective-permute-done.7.refs_2_ = bf16[384,384]{1,0:T(8,128)(2,1)S(1)} collective-permute-done((bf16[384,384]{1,0:T(8,128)(2,1)S(1)}, bf16[384,384]{1,0:T(8,128)(2,1)S(1)}, u32[]{:S(2)}, u32[]{:S(2)}) %collective-permute-start.7) | collective-permute-done | bytes 294944 | tf_op jit(solution)/shard_map/ppermute | solution.py:380
  31.6 3.8 %query_rot.1 = (bf16[480,768]{1,0:T(8,128)(2,1)S(1)}, f32[480,128]{1,0:T(8,128)S(1)}, f32[480,128]{1,0:T(8,128)S(1)}) custom-call(bf16[240,1536]{1,0:T(8,128)(2,1)S(1)} %copy-done.3, bf16[240,1664]{1,0:T(8,128)(2,1)S(1)} %collective-permute-done.4.refs_1_.refs_2_, f32[1,128]{1,0:T(1,128)S(1)} %bitcast.7, bf16[240,128]{1,0:T(8,128)(2,1)S(1)} %pad.4.refs_2_.refs_3_, ...), custom_call_target="tpu_custom_call" | custom-call | flops 1 | bytes 1 | tf_op jit(solution)/shard_map/query_rot/pallas_call | solution.py:410
  35.4 5.2 %collective-permute-done.8.refs_3_ = bf16[384,384]{1,0:T(8,128)(2,1)S(1)} collective-permute-done((bf16[384,384]{1,0:T(8,128)(2,1)S(1)}, bf16[384,384]{1,0:T(8,128)(2,1)S(1)}, u32[]{:S(2)}, u32[]{:S(2)}) %collective-permute-start.8) | collective-permute-done | bytes 294944 | tf_op jit(solution)/shard_map/ppermute | solution.py:380
  43.3 2.0 %collective-permute-start.22 = (bf16[480,768]{1,0:T(8,128)(2,1)S(1)}, bf16[480,768]{1,0:T(8,128)(2,1)S(1)}, u32[]{:S(2)}, u32[]{:S(2)}) collective-permute-start(bf16[480,768]{1,0:T(8,128)(2,1)S(1)} %get-tuple-element.36.refs_10_), channel_id=1, source_target_pairs={{0,4},{1,0},{2,6},{3,2},{4,8},{5,1},{6,10},{7,3},{8,12},{9,5},{10,... | collective-permute-start | bytes 2211848 | tf_op jit(solution)/shard_map/ppermute | solution.py:380
  45.3 11.2 %collective-permute-done.13.refs_12_.refs_0_.refs_8_ = bf16[768,384]{1,0:T(8,128)(2,1)S(1)} collective-permute-done((bf16[768,384]{1,0:T(8,128)(2,1)S(1)}, bf16[768,384]{1,0:T(8,128)(2,1)S(1)}, u32[]{:S(2)}, u32[]{:S(2)}) %collective-permute-start.13) | collective-permute-done | bytes 589856 | tf_op jit(solution)/shard_map/ppermute | solution.py:380
  58.9 3.0 %key_rot_0.1 = (bf16[480,384]{1,0:T(8,128)(2,1)S(1)}, bf16[368,384]{1,0:T(8,128)(2,1)S(1)}) custom-call(s32[31]{0:T(128)S(1)} %slice_bitcast_fusion.refs_0_, bf16[240,3072]{1,0:T(8,128)(2,1)S(1)} %copy-done.1, bf16[240,3072]{1,0:T(8,128)(2,1)S(1)} %collective-permute-done.5.refs_3_.refs_2_, f32[1,128]{1,0:T(1,128)S(1)} %bitcast.5, ...), custom_call_target="tpu_custom_call" | custom-call | flops 1 | bytes 1 | tf_op jit(solution)/shard_map/key_rot_0/pallas_call | solution.py:410
  62.0 1.7 %collective-permute-done.15.refs_11_.refs_4_ = bf16[384,384]{1,0:T(8,128)(2,1)S(1)} collective-permute-done((bf16[384,384]{1,0:T(8,128)(2,1)S(1)}, bf16[384,384]{1,0:T(8,128)(2,1)S(1)}, u32[]{:S(2)}, u32[]{:S(2)}) %collective-permute-start.15) | collective-permute-done | bytes 294944 | tf_op jit(solution)/shard_map/ppermute | solution.py:380
  65.0 2.0 %collective-permute-start.16 = (bf16[480,384]{1,0:T(8,128)(2,1)S(1)}, bf16[480,384]{1,0:T(8,128)(2,1)S(1)}, u32[]{:S(2)}, u32[]{:S(2)}) collective-permute-start(bf16[480,384]{1,0:T(8,128)(2,1)S(1)} %get-tuple-element.30.refs_12_.refs_3_.refs_2_), channel_id=1, source_target_pairs={{0,4},{1,0},{2,6},{3,2},{4,8},{5,1},{6,10},{7,3},{8,12},{9,5},{10,... | collective-permute-start | bytes 1105928 | tf_op jit(solution)/shard_map/ppermute | solution.py:380
  67.0 3.0 %key_rot_1.1 = (bf16[480,384]{1,0:T(8,128)(2,1)S(1)}, bf16[368,384]{1,0:T(8,128)(2,1)S(1)}) custom-call(s32[31]{0:T(128)S(1)} %slice_bitcast_fusion.refs_0_, bf16[240,3072]{1,0:T(8,128)(2,1)S(1)} %copy-done.1, bf16[240,3072]{1,0:T(8,128)(2,1)S(1)} %collective-permute-done.5.refs_3_.refs_2_, f32[1,128]{1,0:T(1,128)S(1)} %bitcast.6, ...), custom_call_target="tpu_custom_call" | custom-call | flops 1 | bytes 1 | tf_op jit(solution)/shard_map/key_rot_1/pallas_call | solution.py:410
  70.1 2.0 %collective-permute-start.17 = (bf16[480,384]{1,0:T(8,128)(2,1)S(1)}, bf16[480,384]{1,0:T(8,128)(2,1)S(1)}, u32[]{:S(2)}, u32[]{:S(2)}) collective-permute-start(bf16[480,384]{1,0:T(8,128)(2,1)S(1)} %get-tuple-element.33.refs_3_), channel_id=1, source_target_pairs={{0,4},{1,0},{2,6},{3,2},{4,8},{5,1},{6,10},{7,3},{8,12},{9,5},{10,... | collective-permute-start | bytes 1105928 | tf_op jit(solution)/shard_map/ppermute | solution.py:380
  72.1 4.4 %collective-permute-done.18.refs_3_.refs_6_ = bf16[480,384]{1,0:T(8,128)(2,1)S(1)} collective-permute-done((bf16[480,384]{1,0:T(8,128)(2,1)S(1)}, bf16[480,384]{1,0:T(8,128)(2,1)S(1)}, u32[]{:S(2)}, u32[]{:S(2)}) %collective-permute-start.18) | collective-permute-done | bytes 368672 | tf_op jit(solution)/shard_map/ppermute | solution.py:380
  78.5 3.5 %collective-permute-done.19.refs_4_.refs_7_ = bf16[480,384]{1,0:T(8,128)(2,1)S(1)} collective-permute-done((bf16[480,384]{1,0:T(8,128)(2,1)S(1)}, bf16[480,384]{1,0:T(8,128)(2,1)S(1)}, u32[]{:S(2)}, u32[]{:S(2)}) %collective-permute-start.19) | collective-permute-done | bytes 368672 | tf_op jit(solution)/shard_map/ppermute | solution.py:380
  82.8 1.6 %collective-permute-start.25 = (bf16[368,768]{1,0:T(8,128)(2,1)S(1)}, bf16[368,768]{1,0:T(8,128)(2,1)S(1)}, u32[]{:S(2)}, u32[]{:S(2)}) collective-permute-start(bf16[368,768]{1,0:T(8,128)(2,1)S(1)} %get-tuple-element.38.refs_14_), channel_id=1, source_target_pairs={{0,2},{1,3},{2,0},{3,1},{4,6},{5,7},{6,4},{7,5},{8,10},{9,11},{10,... | collective-permute-start | bytes 1695752 | tf_op jit(solution)/shard_map/ppermute | solution.py:380
  84.4 1.7 %collective-permute-start.28 = (bf16[256,768]{1,0:T(8,128)(2,1)S(1)}, bf16[256,768]{1,0:T(8,128)(2,1)S(1)}, u32[]{:S(2)}, u32[]{:S(2)}) collective-permute-start(bf16[256,768]{1,0:T(8,128)(2,1)S(1)} %get-tuple-element.43), channel_id=1, source_target_pairs={{0,4},{1,0},{2,6},{3,2},{4,8},{5,1},{6,10},{7,3},{8,12},{9,5},{10,... | collective-permute-start | bytes 1179656 | tf_op jit(solution)/shard_map/ppermute | solution.py:380
  86.3 1.9 %collective-permute-start.26 = (bf16[256,768]{1,0:T(8,128)(2,1)S(1)}, bf16[256,768]{1,0:T(8,128)(2,1)S(1)}, u32[]{:S(2)}, u32[]{:S(2)}) collective-permute-start(bf16[256,768]{1,0:T(8,128)(2,1)S(1)} %get-tuple-element.41), channel_id=1, source_target_pairs={{0,4},{1,0},{2,6},{3,2},{4,8},{5,1},{6,10},{7,3},{8,12},{9,5},{10,... | collective-permute-start | bytes 1179656 | tf_op jit(solution)/shard_map/ppermute | solution.py:380
  88.1 4.2 %collective-permute-done.21.refs_9_ = bf16[368,384]{1,0:T(8,128)(2,1)S(1)} collective-permute-done((bf16[368,384]{1,0:T(8,128)(2,1)S(1)}, bf16[368,384]{1,0:T(8,128)(2,1)S(1)}, u32[]{:S(2)}, u32[]{:S(2)}) %collective-permute-start.21) | collective-permute-done | bytes 282656 | tf_op jit(solution)/shard_map/ppermute | solution.py:380
  92.3 4.9 %attend_early.1 = (f32[2,240,768]{2,1,0:T(8,128)S(1)}, f32[2,240,128]{2,1,0:T(8,128)S(1)}) custom-call(s32[31]{0:T(128)S(1)} %slice_bitcast_fusion.refs_0_, bf16[480,768]{1,0:T(8,128)(2,1)S(1)} %get-tuple-element.26.refs_7_.refs_1_, bf16[480,384]{1,0:T(8,128)(2,1)S(1)} %get-tuple-element.30.refs_12_.refs_3_.refs_2_, ...), custom_call_target="tpu_custom_call" | custom-call | flops 1 | bytes 1 | tf_op jit(solution)/shard_map/attend_early/pallas_call | solution.py:410
  97.3 4.8 %collective-permute-done.26.refs_5_ = bf16[256,768]{1,0:T(8,128)(2,1)S(1)} collective-permute-done((bf16[256,768]{1,0:T(8,128)(2,1)S(1)}, bf16[256,768]{1,0:T(8,128)(2,1)S(1)}, u32[]{:S(2)}, u32[]{:S(2)}) %collective-permute-start.26) | collective-permute-done | bytes 393248 | tf_op jit(solution)/shard_map/ppermute | solution.py:380
  102.1 2.3 %attend_late.1 = (bf16[240,768]{1,0:T(8,128)(2,1)S(1)}, bf16[240,768]{1,0:T(8,128)(2,1)S(1)}) custom-call(s32[31]{0:T(128)S(1)} %slice_bitcast_fusion.refs_0_, bf16[480,768]{1,0:T(8,128)(2,1)S(1)} %get-tuple-element.26.refs_7_.refs_1_, f32[2,240,768]{2,1,0:T(8,128)S(1)} %get-tuple-element.39.refs_2_, f32[2,240,128]{2,1,0:T(8,128)S(1)} %get-tuple-element.40.refs_3_, ...), custom_call_target="tpu_custom_call" | custom-call | flops 1 | bytes 1 | tf_op jit(solution)/shard_map/attend_late/pallas_call | solution.py:410
  104.5 1.7 %collective-permute-done.30 = bf16[240,768]{1,0:T(8,128)(2,1)S(1)} collective-permute-done((bf16[240,768]{1,0:T(8,128)(2,1)S(1)}, bf16[240,768]{1,0:T(8,128)(2,1)S(1)}, u32[]{:S(2)}, u32[]{:S(2)}) %collective-permute-start.30) | collective-permute-done | bytes 368672 | tf_op jit(solution)/shard_map/ppermute | solution.py:380
  (73 shorter events, 23.3 us)
Async XLA Ops:
  0.0 21.7 %collective-permute-start.5 = (bf16[240,3072]{1,0:T(8,128)(2,1)}, bf16[240,3072]{1,0:T(8,128)(2,1)S(1)}, u32[]{:S(2)}, u32[]{:S(2)}) collective-permute-start(bf16[240,3072]{1,0:T(8,128)(2,1)} %refs_1_.7), channel_id=1, source_target_pairs={{0,1},{1,0},{2,3},{3,2},{4,5},{5,4},{6,7},{7,6},{8,9},{9,8},{10,11... | collective-permute-start | bytes 4423688 | tf_op jit(solution)/shard_map/ppermute | solution.py:380
  3.7 12.3 %collective-permute-start.3 = (bf16[384,384]{1,0:T(8,128)(2,1)S(1)}, bf16[384,384]{1,0:T(8,128)(2,1)S(1)}, u32[]{:S(2)}, u32[]{:S(2)}) collective-permute-start(bf16[384,384]{1,0:T(8,128)(2,1)S(1)} %maximum_select_fusion.1.refs_6_), channel_id=1, source_target_pairs={{0,4},{1,5},{2,6},{3,7},{4,8},{5,9},{6,10},{7,11},{8,12},{9,13},{1... | collective-permute-start | bytes 884744 | tf_op jit(solution)/shard_map/ppermute | solution.py:380
  18.0 22.6 %collective-permute-start.9 = (bf16[768,384]{1,0:T(8,128)(2,1)S(1)}, bf16[768,384]{1,0:T(8,128)(2,1)S(1)}, u32[]{:S(2)}, u32[]{:S(2)}) collective-permute-start(bf16[768,384]{1,0:T(8,128)(2,1)S(1)} %early.1), channel_id=1, source_target_pairs={{0,16},{1,17},{2,18},{3,19},{4,20},{5,21},{6,22},{7,23},{8,24},{9,... | collective-permute-start | bytes 1769480 | tf_op jit(solution)/shard_map/ppermute | solution.py:380
  19.5 10.9 %collective-permute-start.7 = (bf16[384,384]{1,0:T(8,128)(2,1)S(1)}, bf16[384,384]{1,0:T(8,128)(2,1)S(1)}, u32[]{:S(2)}, u32[]{:S(2)}) collective-permute-start(bf16[384,384]{1,0:T(8,128)(2,1)S(1)} %collective-permute-done.3.refs_5_.refs_0_.refs_8_), channel_id=1, source_target_pairs={{0,4},{1,5},{2,6},{3,7},{4,8},{5,9},{6,10},{7,11},{8,12},{9,13},{1... | collective-permute-start | bytes 884744 | tf_op jit(solution)/shard_map/ppermute | solution.py:380
  21.1 9.9 %collective-permute-start.6 = (bf16[384,384]{1,0:T(8,128)(2,1)S(1)}, bf16[384,384]{1,0:T(8,128)(2,1)S(1)}, u32[]{:S(2)}, u32[]{:S(2)}) collective-permute-start(bf16[384,384]{1,0:T(8,128)(2,1)S(1)} %collective-permute-done.3.refs_5_.refs_0_.refs_8_), channel_id=1, source_target_pairs={{0,2},{1,3},{2,0},{3,1},{4,6},{5,7},{6,4},{7,5},{8,10},{9,11},{10,... | collective-permute-start | bytes 884744 | tf_op jit(solution)/shard_map/ppermute | solution.py:380
  22.3 19.8 %collective-permute-start.11 = (bf16[368,768]{1,0:T(8,128)(2,1)S(1)}, bf16[368,768]{1,0:T(8,128)(2,1)S(1)}, u32[]{:S(2)}, u32[]{:S(2)}) collective-permute-start(bf16[368,768]{1,0:T(8,128)(2,1)S(1)} %value_inner.1), channel_id=1, source_target_pairs={{0,2},{1,3},{2,0},{3,1},{4,6},{5,7},{6,4},{7,5},{8,10},{9,11},{10,... | collective-permute-start | bytes 1695752 | tf_op jit(solution)/shard_map/ppermute | solution.py:380
  30.5 10.1 %collective-permute-start.8 = (bf16[384,384]{1,0:T(8,128)(2,1)S(1)}, bf16[384,384]{1,0:T(8,128)(2,1)S(1)}, u32[]{:S(2)}, u32[]{:S(2)}) collective-permute-start(bf16[384,384]{1,0:T(8,128)(2,1)S(1)} %collective-permute-done.7.refs_2_), channel_id=1, source_target_pairs={{0,4},{1,5},{2,6},{3,7},{4,8},{5,9},{6,10},{7,11},{8,12},{9,13},{1... | collective-permute-start | bytes 884744 | tf_op jit(solution)/shard_map/ppermute | solution.py:380
  31.0 9.6 %collective-permute-start.10 = (bf16[384,384]{1,0:T(8,128)(2,1)S(1)}, bf16[384,384]{1,0:T(8,128)(2,1)S(1)}, u32[]{:S(2)}, u32[]{:S(2)}) collective-permute-start(bf16[384,384]{1,0:T(8,128)(2,1)S(1)} %collective-permute-done.6.refs_9_), channel_id=1, source_target_pairs={{0,16},{1,17},{2,18},{3,19},{4,20},{5,21},{6,22},{7,23},{8,24},{9,... | collective-permute-start | bytes 884744 | tf_op jit(solution)/shard_map/ppermute | solution.py:380
  42.2 14.4 %collective-permute-start.13 = (bf16[768,384]{1,0:T(8,128)(2,1)S(1)}, bf16[768,384]{1,0:T(8,128)(2,1)S(1)}, u32[]{:S(2)}, u32[]{:S(2)}) collective-permute-start(bf16[768,384]{1,0:T(8,128)(2,1)S(1)} %get-tuple-element.29.refs_10_), channel_id=1, source_target_pairs={{0,16},{1,17},{2,18},{3,19},{4,20},{5,21},{6,22},{7,23},{8,24},{9,... | collective-permute-start | bytes 1769480 | tf_op jit(solution)/shard_map/ppermute | solution.py:380
  42.8 14.0 %collective-permute-start.12 = (bf16[768,384]{1,0:T(8,128)(2,1)S(1)}, bf16[768,384]{1,0:T(8,128)(2,1)S(1)}, u32[]{:S(2)}, u32[]{:S(2)}) collective-permute-start(bf16[768,384]{1,0:T(8,128)(2,1)S(1)} %get-tuple-element.29.refs_10_), channel_id=1, source_target_pairs={{0,2},{1,3},{2,0},{3,1},{4,6},{5,7},{6,4},{7,5},{8,10},{9,11},{10,... | collective-permute-start | bytes 1769480 | tf_op jit(solution)/shard_map/ppermute | solution.py:380
  43.3 18.7 %collective-permute-start.23 = (bf16[480,768]{1,0:T(8,128)(2,1)S(1)}, bf16[480,768]{1,0:T(8,128)(2,1)S(1)}, u32[]{:S(2)}, u32[]{:S(2)}) collective-permute-start(bf16[480,768]{1,0:T(8,128)(2,1)S(1)} %get-tuple-element.36.refs_10_), channel_id=1, source_target_pairs={{0,1},{1,5},{2,3},{3,7},{4,0},{5,9},{6,2},{7,11},{8,4},{9,13},{10,... | collective-permute-start | bytes 2211848 | tf_op jit(solution)/shard_map/ppermute | solution.py:380
  43.3 18.7 %collective-permute-start.22 = (bf16[480,768]{1,0:T(8,128)(2,1)S(1)}, bf16[480,768]{1,0:T(8,128)(2,1)S(1)}, u32[]{:S(2)}, u32[]{:S(2)}) collective-permute-start(bf16[480,768]{1,0:T(8,128)(2,1)S(1)} %get-tuple-element.36.refs_10_), channel_id=1, source_target_pairs={{0,4},{1,0},{2,6},{3,2},{4,8},{5,1},{6,10},{7,3},{8,12},{9,5},{10,... | collective-permute-start | bytes 2211848 | tf_op jit(solution)/shard_map/ppermute | solution.py:380
  64.4 17.7 %collective-permute-start.24 = (bf16[368,768]{1,0:T(8,128)(2,1)S(1)}, bf16[368,768]{1,0:T(8,128)(2,1)S(1)}, u32[]{:S(2)}, u32[]{:S(2)}) collective-permute-start(bf16[368,768]{1,0:T(8,128)(2,1)S(1)} %get-tuple-element.37), channel_id=1, source_target_pairs={{0,2},{1,3},{2,0},{3,1},{4,6},{5,7},{6,4},{7,5},{8,10},{9,11},{10,... | collective-permute-start | bytes 1695752 | tf_op jit(solution)/shard_map/ppermute | solution.py:380
  65.0 11.5 %collective-permute-start.18 = (bf16[480,384]{1,0:T(8,128)(2,1)S(1)}, bf16[480,384]{1,0:T(8,128)(2,1)S(1)}, u32[]{:S(2)}, u32[]{:S(2)}) collective-permute-start(bf16[480,384]{1,0:T(8,128)(2,1)S(1)} %get-tuple-element.30.refs_12_.refs_3_.refs_2_), channel_id=1, source_target_pairs={{0,1},{1,5},{2,3},{3,7},{4,0},{5,9},{6,2},{7,11},{8,4},{9,13},{10,... | collective-permute-start | bytes 1105928 | tf_op jit(solution)/shard_map/ppermute | solution.py:380
  65.0 13.0 %collective-permute-start.16 = (bf16[480,384]{1,0:T(8,128)(2,1)S(1)}, bf16[480,384]{1,0:T(8,128)(2,1)S(1)}, u32[]{:S(2)}, u32[]{:S(2)}) collective-permute-start(bf16[480,384]{1,0:T(8,128)(2,1)S(1)} %get-tuple-element.30.refs_12_.refs_3_.refs_2_), channel_id=1, source_target_pairs={{0,4},{1,0},{2,6},{3,2},{4,8},{5,1},{6,10},{7,3},{8,12},{9,5},{10,... | collective-permute-start | bytes 1105928 | tf_op jit(solution)/shard_map/ppermute | solution.py:380
  70.1 12.0 %collective-permute-start.19 = (bf16[480,384]{1,0:T(8,128)(2,1)S(1)}, bf16[480,384]{1,0:T(8,128)(2,1)S(1)}, u32[]{:S(2)}, u32[]{:S(2)}) collective-permute-start(bf16[480,384]{1,0:T(8,128)(2,1)S(1)} %get-tuple-element.33.refs_3_), channel_id=1, source_target_pairs={{0,1},{1,5},{2,3},{3,7},{4,0},{5,9},{6,2},{7,11},{8,4},{9,13},{10,... | collective-permute-start | bytes 1105928 | tf_op jit(solution)/shard_map/ppermute | solution.py:380
  70.1 12.0 %collective-permute-start.17 = (bf16[480,384]{1,0:T(8,128)(2,1)S(1)}, bf16[480,384]{1,0:T(8,128)(2,1)S(1)}, u32[]{:S(2)}, u32[]{:S(2)}) collective-permute-start(bf16[480,384]{1,0:T(8,128)(2,1)S(1)} %get-tuple-element.33.refs_3_), channel_id=1, source_target_pairs={{0,4},{1,0},{2,6},{3,2},{4,8},{5,1},{6,10},{7,3},{8,12},{9,5},{10,... | collective-permute-start | bytes 1105928 | tf_op jit(solution)/shard_map/ppermute | solution.py:380
  76.5 9.8 %collective-permute-start.20 = (bf16[368,384]{1,0:T(8,128)(2,1)S(1)}, bf16[368,384]{1,0:T(8,128)(2,1)S(1)}, u32[]{:S(2)}, u32[]{:S(2)}) collective-permute-start(bf16[368,384]{1,0:T(8,128)(2,1)S(1)} %get-tuple-element.34), channel_id=1, source_target_pairs={{0,2},{1,3},{2,0},{3,1},{4,6},{5,7},{6,4},{7,5},{8,10},{9,11},{10,... | collective-permute-start | bytes 847880 | tf_op jit(solution)/shard_map/ppermute | solution.py:380
  78.0 14.3 %collective-permute-start.21 = (bf16[368,384]{1,0:T(8,128)(2,1)S(1)}, bf16[368,384]{1,0:T(8,128)(2,1)S(1)}, u32[]{:S(2)}, u32[]{:S(2)}) collective-permute-start(bf16[368,384]{1,0:T(8,128)(2,1)S(1)} %get-tuple-element.35), channel_id=1, source_target_pairs={{0,2},{1,3},{2,0},{3,1},{4,6},{5,7},{6,4},{7,5},{8,10},{9,11},{10,... | collective-permute-start | bytes 847880 | tf_op jit(solution)/shard_map/ppermute | solution.py:380
  82.8 19.3 %collective-permute-start.25 = (bf16[368,768]{1,0:T(8,128)(2,1)S(1)}, bf16[368,768]{1,0:T(8,128)(2,1)S(1)}, u32[]{:S(2)}, u32[]{:S(2)}) collective-permute-start(bf16[368,768]{1,0:T(8,128)(2,1)S(1)} %get-tuple-element.38.refs_14_), channel_id=1, source_target_pairs={{0,2},{1,3},{2,0},{3,1},{4,6},{5,7},{6,4},{7,5},{8,10},{9,11},{10,... | collective-permute-start | bytes 1695752 | tf_op jit(solution)/shard_map/ppermute | solution.py:380
  84.4 12.9 %collective-permute-start.28 = (bf16[256,768]{1,0:T(8,128)(2,1)S(1)}, bf16[256,768]{1,0:T(8,128)(2,1)S(1)}, u32[]{:S(2)}, u32[]{:S(2)}) collective-permute-start(bf16[256,768]{1,0:T(8,128)(2,1)S(1)} %get-tuple-element.43), channel_id=1, source_target_pairs={{0,4},{1,0},{2,6},{3,2},{4,8},{5,1},{6,10},{7,3},{8,12},{9,5},{10,... | collective-permute-start | bytes 1179656 | tf_op jit(solution)/shard_map/ppermute | solution.py:380
  86.1 11.2 %collective-permute-start.29 = (bf16[256,768]{1,0:T(8,128)(2,1)S(1)}, bf16[256,768]{1,0:T(8,128)(2,1)S(1)}, u32[]{:S(2)}, u32[]{:S(2)}) collective-permute-start(bf16[256,768]{1,0:T(8,128)(2,1)S(1)} %get-tuple-element.44), channel_id=1, source_target_pairs={{0,1},{1,5},{2,3},{3,7},{4,0},{5,9},{6,2},{7,11},{8,4},{9,13},{10,... | collective-permute-start | bytes 1179656 | tf_op jit(solution)/shard_map/ppermute | solution.py:380
  86.3 15.9 %collective-permute-start.26 = (bf16[256,768]{1,0:T(8,128)(2,1)S(1)}, bf16[256,768]{1,0:T(8,128)(2,1)S(1)}, u32[]{:S(2)}, u32[]{:S(2)}) collective-permute-start(bf16[256,768]{1,0:T(8,128)(2,1)S(1)} %get-tuple-element.41), channel_id=1, source_target_pairs={{0,4},{1,0},{2,6},{3,2},{4,8},{5,1},{6,10},{7,3},{8,12},{9,5},{10,... | collective-permute-start | bytes 1179656 | tf_op jit(solution)/shard_map/ppermute | solution.py:380
  92.3 9.8 %collective-permute-start.27 = (bf16[256,768]{1,0:T(8,128)(2,1)S(1)}, bf16[256,768]{1,0:T(8,128)(2,1)S(1)}, u32[]{:S(2)}, u32[]{:S(2)}) collective-permute-start(bf16[256,768]{1,0:T(8,128)(2,1)S(1)} %get-tuple-element.42), channel_id=1, source_target_pairs={{0,1},{1,5},{2,3},{3,7},{4,0},{5,9},{6,2},{7,11},{8,4},{9,13},{10,... | collective-permute-start | bytes 1179656 | tf_op jit(solution)/shard_map/ppermute | solution.py:380
  (15 other events, 133.3 us)
